TPU v7x, 32 devices: a whole 2x2x4 slice. The times are simulated.
32 devices in a mesh: th: 4 (over x, core), tw: 8 (over z, y).
Axes of the slice: x: 2, y: 2, z: 4, core: 2. Of those that a mesh axis runs over, the one named last changes fastest.
Arguments:
- image: bfloat16 [256, 768, 384], P('th', 'tw'), may hold values from -6 to 6
- image_heights: int32 [3], replicated, may hold values from 1 to 192, as said below
- rate_log: float32 [2, 384, 32], replicated, may hold values from -1.5 to 1
- freq: float32 [2, 384, 32], replicated, may hold values from 0 to 3
- coef_re: float32 [2, 384, 32], replicated, may hold values from -0.18 to 0.18
- coef_im: float32 [2, 384, 32], replicated, may hold values from -0.18 to 0.18
- log_step: float32 [2, 384], replicated, may hold values from -3 to -0.5
- skip: float32 [384], replicated, may hold values from -3 to 3
- ln_gain: float32 [384], replicated, may hold values from 0.5 to 1.5
- ln_bias: float32 [384], replicated, may hold values from -1.8 to 1.8
- w_in: bfloat16 [384, 1536], replicated, may hold values from -0.3125 to 0.3125
- b_in: float32 [1536], replicated, may hold values from -1.8 to 1.8
- w_out: bfloat16 [1536, 384], replicated, may hold values from -0.15625 to 0.15625
- b_out: float32 [384], replicated, may hold values from -1.8 to 1.8
- layer_scale: float32 [384], replicated, may hold values from 0.5 to 2
- out_grad: bfloat16 [256, 768, 384], P('th', 'tw'), may hold values from -6 to 6
Outputs:
- output: bfloat16 [256, 768, 384], P('th', 'tw')
- image_grad: bfloat16 [256, 768, 384], P('th', 'tw')
- grad_rate_log: float32 [2, 384, 32], replicated
- grad_freq: float32 [2, 384, 32], replicated
- grad_coef_re: float32 [2, 384, 32], replicated
- grad_coef_im: float32 [2, 384, 32], replicated
- grad_log_step: float32 [2, 384], replicated
- grad_skip: float32 [384], replicated
- grad_ln_gain: float32 [384], replicated
- grad_ln_bias: float32 [384], replicated
- grad_w_in: float32 [384, 1536], replicated
- grad_b_in: float32 [1536], replicated
- grad_w_out: float32 [1536, 384], replicated
- grad_b_out: float32 [384], replicated
- grad_layer_scale: float32 [384], replicated
Inputs may be any that keep to these rules, and one draw needn't show every extreme that they name: `image_heights`: 3 images stacked top to bottom, each as wide as the grid; the first and the last together have 64 rows, each at least one, and the middle one has exactly 192 rows.
All inputs are finite; a program needn't handle non-finite values.
Results may differ from a plain program's by a relative error of at most 0.005.
The roundings to bfloat16 on the way count: a program that leaves them out, or rounds other values in their place, can miss the bound.
Values may be sent and summed in bfloat16 or wider, within the bound.
No kernel may reach another device: no remote copies, remote signals or barrier semaphores. Data moves between devices by JAX's collectives and lax.ppermute only.
A program may use at most 384 MiB of HBM per device.

v0:
```python
import jax
import jax.numpy as jnp
from jax import lax
from jax.sharding import PartitionSpec as P

KSIZE = 15


def extended_2(block, sides, width):
    for axis, dim in sides:
        count = lax.axis_size(axis)
        forward = [(i, i + 1) for i in range(count - 1)]
        backward = [(target, source) for source, target in forward]
        low = lax.ppermute(
            lax.slice_in_dim(block, block.shape[dim] - width, None, axis=dim), axis, forward
        )
        high = lax.ppermute(lax.slice_in_dim(block, 0, width, axis=dim), axis, backward)
        block = jnp.concatenate([low, block, high], axis=dim)
    return block


def kernel_taps(rate_log, freq, coef_re, coef_im, log_step):
    step = jnp.exp(log_step)[:, None, :, None]
    offsets = jnp.arange(KSIZE, dtype=jnp.float32)[None, :, None, None]
    decay = jnp.exp(-jnp.exp(rate_log)[:, None] * step * offsets)
    phase = freq[:, None] * step * offsets
    terms = decay * (coef_re[:, None] * jnp.cos(phase) - coef_im[:, None] * jnp.sin(phase))
    return 2.0 * jnp.sum(terms, axis=-1)


def normalize(mixed, gain, bias):
    mean = jnp.mean(mixed, axis=-1, keepdims=True)
    centred = mixed - mean
    var = jnp.mean(centred * centred, axis=-1, keepdims=True)
    return centred * lax.rsqrt(var + 1e-06) * gain + bias


def row_mask(ident, offset, height, reach):
    return (ident[reach : reach + height] == ident[offset : offset + height]).astype(jnp.float32)[
        :, None, None
    ]


def rows_filter(extended, ident, row_taps, height, reach):
    total = row_taps[0][None, None, :] * row_mask(ident, 0, height, reach) * extended[0:height]
    for tap in range(1, KSIZE):
        total = (
            total
            + row_taps[tap][None, None, :]
            * row_mask(ident, tap, height, reach)
            * extended[tap : tap + height]
        )
    return total


def rows_filter_back(extended, ident, row_taps, height, reach):
    total = jnp.zeros(extended[0:height].shape, jnp.float32)
    for tap in range(KSIZE):
        offset = 2 * reach - tap
        total = (
            total
            + row_taps[tap][None, None, :]
            * row_mask(ident, offset, height, reach)
            * extended[offset : offset + height]
        )
    return total


def cols_filter(extended, col_taps, width):
    total = col_taps[0][None, None, :] * extended[:, 0:width]
    for tap in range(1, KSIZE):
        total = total + col_taps[tap][None, None, :] * extended[:, tap : tap + width]
    return total


def cols_filter_back(extended, col_taps, width, reach):
    total = jnp.zeros(extended[:, 0:width].shape, jnp.float32)
    for tap in range(KSIZE):
        offset = 2 * reach - tap
        total = total + col_taps[tap][None, None, :] * extended[:, offset : offset + width]
    return total


def per_device(
    image,
    image_heights,
    rate_log,
    freq,
    coef_re,
    coef_im,
    log_step,
    skip,
    ln_gain,
    ln_bias,
    w_in,
    b_in,
    w_out,
    b_out,
    layer_scale,
    out_grad,
):
    height, width, chans = image.shape
    reach = KSIZE // 2
    pixels = height * width
    taps, taps_pull = jax.vjp(kernel_taps, rate_log, freq, coef_re, coef_im, log_step)
    bounds = jnp.cumsum(image_heights)
    rows = lax.axis_index("th") * height - reach + jnp.arange(height + 2 * reach, dtype=jnp.int32)
    ident = jnp.sum((rows[:, None] >= bounds[None, :]).astype(jnp.int32), axis=1)
    pixel_ext = extended_2(image, (("th", 0), ("tw", 1)), reach)
    pixel_rows = pixel_ext[:, reach : reach + width]
    partial_ext = rows_filter(pixel_ext, ident, taps[0], height, reach)
    mixed = cols_filter(partial_ext, taps[1], width) + skip * image
    normed_f, norm_pull = jax.vjp(normalize, mixed, ln_gain, ln_bias)
    normed = normed_f.astype(jnp.bfloat16).reshape(pixels, chans)
    pre = jnp.dot(normed, w_in, preferred_element_type=jnp.float32) + b_in
    act_f, gelu_pull = jax.vjp(lambda v: jax.nn.gelu(v, approximate=False), pre)
    act = act_f.astype(jnp.bfloat16)
    branch = jnp.dot(act, w_out, preferred_element_type=jnp.float32) + b_out
    flat_image = image.reshape(pixels, chans)
    output = (flat_image + layer_scale * branch).astype(jnp.bfloat16).reshape(height, width, chans)
    grad_out = out_grad.reshape(pixels, chans).astype(jnp.float32)
    d_scale = jnp.sum(grad_out * branch, axis=0)
    d_branch = (layer_scale * grad_out).astype(jnp.bfloat16)
    d_bout = jnp.sum(d_branch.astype(jnp.float32), axis=0)
    d_wout = lax.dot_general(
        act, d_branch, (((0,), (0,)), ((), ())), preferred_element_type=jnp.float32
    )
    d_act = lax.dot_general(
        d_branch, w_out, (((1,), (1,)), ((), ())), preferred_element_type=jnp.float32
    )
    d_pre = gelu_pull(d_act)[0].astype(jnp.bfloat16)
    d_bin = jnp.sum(d_pre.astype(jnp.float32), axis=0)
    d_win = lax.dot_general(
        normed, d_pre, (((0,), (0,)), ((), ())), preferred_element_type=jnp.float32
    )
    d_normed = lax.dot_general(
        d_pre, w_in, (((1,), (1,)), ((), ())), preferred_element_type=jnp.float32
    )
    d_mixed_f, d_gain, d_bias = norm_pull(d_normed.reshape(height, width, chans))
    d_mixed = d_mixed_f.astype(jnp.bfloat16)
    d_skip = jnp.sum(d_mixed.astype(jnp.float32) * image, axis=(0, 1))
    grad_ext = extended_2(d_mixed, (("th", 0), ("tw", 1)), reach)
    d_partial_ext = cols_filter_back(grad_ext, taps[1], width, reach)
    d_partial = d_partial_ext[reach : reach + height]
    col_grads = []
    row_grads = []
    for tap in range(KSIZE):
        col_grads.append(jnp.sum(d_mixed * partial_ext[:, tap : tap + width], axis=(0, 1)))
        row_grads.append(
            jnp.sum(
                d_partial * row_mask(ident, tap, height, reach) * pixel_rows[tap : tap + height],
                axis=(0, 1),
            )
        )
    d_taps = jnp.stack([jnp.stack(row_grads), jnp.stack(col_grads)])
    image_grad = (
        out_grad.astype(jnp.float32)
        + skip * d_mixed
        + rows_filter_back(d_partial_ext, ident, taps[0], height, reach)
    )
    image_grad = image_grad.astype(jnp.bfloat16)
    d_win, d_wout, d_bin, d_bout, d_scale, d_gain, d_bias, d_skip, d_taps = lax.psum(
        (d_win, d_wout, d_bin, d_bout, d_scale, d_gain, d_bias, d_skip, d_taps), ("th", "tw")
    )
    g_rate, g_freq, g_re, g_im, g_step = taps_pull(d_taps)
    return (
        output,
        image_grad,
        g_rate,
        g_freq,
        g_re,
        g_im,
        g_step,
        d_skip,
        d_gain,
        d_bias,
        d_win,
        d_bin,
        d_wout,
        d_bout,
        d_scale,
    )


def solution(mesh):
    in_specs = (
        P("th", "tw", None),
        P(),
        P(),
        P(),
        P(),
        P(),
        P(),
        P(),
        P(),
        P(),
        P(),
        P(),
        P(),
        P(),
        P(),
        P("th", "tw", None),
    )
    out_specs = (
        P("th", "tw", None),
        P("th", "tw", None),
        P(),
        P(),
        P(),
        P(),
        P(),
        P(),
        P(),
        P(),
        P(),
        P(),
        P(),
        P(),
        P(),
    )
    return jax.shard_map(
        per_device, mesh=mesh, in_specs=in_specs, out_specs=out_specs, check_vma=False
    )
```

profile of v0, /device:TPU:0, one launch (start us, length us, event | category | flops | bytes accessed | tf_op | source)
XLA Modules:
  0.0 673.0 jit_solution(13202793137528216365)
XLA Ops:
  7.2 1.4 fusion.54
  8.6 2.4 collective-permute-start
  11.0 1.3 collective-permute-start.1
  13.0 1.0 negate_multiply_fusion.2
  14.6 6.8 %multiply_reduce_fusion.22 = f32[2,15,384]{2,1,0:T(8,128)S(1)} fusion(f32[2,384,32]{1,2,0:T(8,128)} %param.21, f32[2,384,32]{1,2,0:T(8,128)S(1)} %get-tuple-element.123, f32[2,384,32]{1,2,0:T(8,128)} %param.20, f32[2,384,32]{1,2,0:T(8,128)S(1)} %get-tuple-element.122), kind=kLoop, calls=%fused_computation.124 | loop fusion | flops 2568960 | bytes 439296 | tf_op jit(solution)/shard_map/jvp()/reduce_sum | solution.py:28
  21.8 0.8 reduce-window.8
  23.0 0.8 broadcast_multiply_fusion.11
  24.6 0.8 broadcast_multiply_fusion.5
  27.0 0.8 broadcast_multiply_fusion.17
  27.7 1.1 constant_dynamic-update-slice_fusion.4
  28.8 7.2 %constant_dynamic-update-slice_fusion.3 = (bf16[71,96,384]{2,1,0:T(8,128)(2,1)}, bf16[78,96,384]{2,1,0:T(8,128)(2,1)}, bf16[71,96,384]{2,1,0:T(8,128)(2,1)S(1)}) fusion(bf16[71,96,384]{2,1,0:T(8,128)(2,1)} %get-tuple-element.114, bf16[64,96,384]{2,1,0:T(8,128)(2,1)} %param.16, bf16[78,96,384]{2,1,0:T(8,128)(2,1)} %get-tuple-element.115), kind=kLoop, calls=%fused_computation.177 | loop fusion | bytes 18874368 | tf_op jit(solution)/shard_map/concatenate | solution.py:18
  36.0 0.9 constant_dynamic-update-slice_fusion.5
  37.0 2.2 fusion.52
  39.2 4.5 collective-permute-start.2
  43.7 1.5 collective-permute-start.3
  45.3 0.8 broadcast_multiply_fusion.14
  46.0 4.0 convert_reduce_fusion.1
  50.0 13.8 %collective-permute-done.2 = bf16[78,7,384]{2,1,0:T(8,128)(2,1)S(1)} collective-permute-done((bf16[78,7,384]{2,1,0:T(8,128)(2,1)S(1)}, bf16[78,7,384]{2,1,0:T(8,128)(2,1)S(1)}, u32[]{:S(2)}, u32[]{:S(2)}) %collective-permute-start.2) | collective-permute-done | bytes 419360 | tf_op jit(solution)/shard_map/ppermute | solution.py:14
  63.9 5.1 pad_maximum_fusion
  68.9 36.9 %multiply_add_fusion.1 = f32[64,110,384]{2,1,0:T(8,128)} fusion(bf16[78,110,384]{2,1,0:T(8,128)(2,1)} %pad_maximum_fusion, f32[64,384]{1,0:T(8,128)S(1)} %get-tuple-element.151, f32[64,384]{1,0:T(8,128)S(1)} %get-tuple-element.149, f32[64,384]{1,0:T(8,128)S(1)} %get-tuple-element.147, f32[64,384]{1,0:T(8,128)S(1)} %get-tuple-element.145, ...), kind=kLoop, calls=%fused_computation.37 | loop fusion | flops 118947840 | bytes 93292032 | tf_op jit(solution)/shard_map/add | solution.py:48
  106.0 60.6 %fusion.50 = (f32[64,96]{1,0:T(8,128)S(1)}, f32[64,96,384]{2,1,0:T(8,128)}) fusion(bf16[64,96,384]{2,1,0:T(8,128)(2,1)} %param.16, f32[384]{0:T(512)S(1)} %copy-done.65, f32[64,110,384]{2,1,0:T(8,128)} %multiply_add_fusion.1, f32[384]{0:T(512)S(1)} %get-tuple-element.55, f32[384]{0:T(512)S(1)} %get-tuple-element.56, f32[384]{0:T(512)S(1)} %get-tuple-element.57, ...), kind=kLoop, calls=%fused_computation.229 | loop fusion | flops 77850624 | bytes 155762688 | tf_op jit(solution)/shard_map/jvp()/reduce_sum | solution.py:32
  166.6 5.5 multiply_reduce_fusion.17
  173.0 2.0 add_convert_fusion.2
  175.1 93.4 %multiply_convert_fusion = (bf16[6144,1536]{1,0:T(8,128)(2,1)}, f32[6144,1536]{1,0:T(8,128)}, f32[6144,1536]{1,0:T(8,128)}) fusion(f32[1536]{0:T(1024)S(1)} %copy-done.100, bf16[6144,384]{1,0:T(8,128)(2,1)S(1)} %bitcast.39, bf16[384,1536]{1,0:T(8,128)(2,1)S(1)} %copy-done), kind=kOutput, calls=%fused_computation.21 | convolution fusion | flops 7870611456 | bytes 100276224 | tf_op jit(solution)/shard_map/dot_general | solution.py:115
  268.5 19.0 %fusion.41 = (f32[384]{0:T(512)}, bf16[6144,384]{1,0:T(8,128)(2,1)}, bf16[6144,384]{1,0:T(8,128)(2,1)}) fusion(bf16[64,96,384]{2,1,0:T(8,128)(2,1)} %param.31, f32[384]{0:T(512)S(1)} %copy-done.97, bf16[64,96,384]{2,1,0:T(8,128)(2,1)S(1)} %copy-done.7, f32[384]{0:T(512)S(1)} %copy-done.101, bf16[6144,1536]{1,0:T(8,128)(2,1)} %get-tuple-element.94, ...), kind=kOutput, calls=%fused_computation.90 | convolution fusion | flops 7271349760 | bytes 38932992 | tf_op jit(solution)/shard_map/dot_general | solution.py:118
  287.6 36.1 %convert_reduce_fusion = (f32[1536]{0:T(1024)}, bf16[6144,1536]{1,0:T(8,128)(2,1)}) fusion(f32[6144,1536]{1,0:T(8,128)} %get-tuple-element.95, bf16[6144,384]{1,0:T(8,128)(2,1)} %get-tuple-element.106, bf16[1536,384]{1,0:T(8,128)(2,1)S(1)} %copy-done.99, f32[6144,1536]{1,0:T(8,128)} %get-tuple-element.180, f32[1536]{0:T(1024)S(1)} %copy-done.100), kind=kOutput, calls=%fused_computation.19 | convolution fusion | flops 7408187904 | bytes 100282368 | tf_op jit(solution)/shard_map/dot_general | solution.py:128
  323.7 14.6 %fusion.55 = (f32[384]{0:T(512)}, f32[6144,384]{1,0:T(8,128)S(1)}) fusion(bf16[6144,1536]{1,0:T(8,128)(2,1)} %get-tuple-element.184, bf16[384,1536]{1,0:T(8,128)(2,1)S(1)} %copy-done), kind=kOutput, calls=%fused_computation.234 | convolution fusion | flops 7250116096 | bytes 29492736 | tf_op jit(solution)/shard_map/dot_general | solution.py:136
  338.3 2.8 multiply_reduce_fusion.16
  341.9 5.6 multiply_reduce_fusion
  347.5 63.6 %fusion.23 = (f32[384]{0:T(512)S(1)}, f32[384]{0:T(512)S(1)}, f32[384]{0:T(512)S(1)}, f32[384]{0:T(512)S(1)}, f32[384]{0:T(512)S(1)}, /*index=5*/f32[384]{0:T(51...) fusion(f32[64,110,384]{2,1,0:T(8,128)} %multiply_add_fusion.1, ...), kind=kLoop, calls=%fused_computation.55 | loop fusion | flops 92006784 | bytes 165273600 | tf_op jit(solution)/shard_map/reduce_sum | solution.py:148
  411.2 3.5 collective-permute-start.4
  414.8 1.3 collective-permute-start.5
  416.1 13.8 %fusion.56 = f32[384,1536]{1,0:T(8,128)} fusion(bf16[6144,384]{1,0:T(8,128)(2,1)} %bitcast.40, bf16[6144,1536]{1,0:T(8,128)(2,1)} %get-tuple-element.184), kind=kOutput, calls=%fused_computation.235 | convolution fusion | flops 7247757312 | bytes 25952256 | tf_op jit(solution)/shard_map/dot_general | solution.py:133
  429.9 0.9 pad_maximum_fusion.2
  431.0 1.3 collective-permute-start.6
  432.3 5.7 collective-permute-start.7
  438.1 16.2 %fusion.57 = f32[1536,384]{1,0:T(8,128)} fusion(bf16[6144,1536]{1,0:T(8,128)(2,1)} %get-tuple-element.94, bf16[6144,384]{1,0:T(8,128)(2,1)} %get-tuple-element.106), kind=kOutput, calls=%fused_computation.236 | convolution fusion | flops 7247757312 | bytes 25952256 | tf_op jit(solution)/shard_map/dot_general | solution.py:125
  454.5 3.0 collective-permute-done.7
  457.5 9.7 %pad_maximum_fusion.1 = (bf16[78,103,384]{2,1,0:T(8,128)(2,1)S(1)}, bf16[78,103,384]{2,1,0:T(8,128)(2,1)}) fusion(bf16[78,7,384]{2,1,0:T(8,128)(2,1)S(1)} %collective-permute-done.6, bf16[7,96,384]{2,1,0:T(8,128)(2,1)} %copy-done.11, bf16[64,96,384]{2,1,0:T(8,128)(2,1)} %copy-done.5, bf16[7,96,384]{2,1,0:T(8,128)(2,1)} %copy-done.10, ...), kind=kLoop, calls=%fused_computation.117 | loop fusion | flops 49360896 | bytes 18929664 | tf_op jit(solution)/shard_map/concatenate | solution.py:18
  467.3 40.2 %multiply_add_fusion = f32[78,96,384]{2,1,0:T(8,128)S(1)} fusion(bf16[78,103,384]{2,1,0:T(8,128)(2,1)} %get-tuple-element.101, bf16[78,103,384]{2,1,0:T(8,128)(2,1)S(1)} %get-tuple-element.100, f32[384]{0:T(512)S(1)} %copy-done.45, f32[384]{0:T(512)} %copy-done.46, f32[384]{0:T(512)} %copy-done.47, f32[384]{0:T(512)} %copy-done.48, f32[384]{0:T(512)} %copy-done.49, ...), kind=kLoop, calls=%fused_computation.36 | loop fusion | flops 132268032 | bytes 97786368 | tf_op jit(solution)/shard_map/add | solution.py:80
  507.7 17.5 %multiply_reduce_fusion.1 = (f32[384]{0:T(512)S(1)}, f32[384]{0:T(512)S(1)}, f32[384]{0:T(512)S(1)}, f32[384]{0:T(512)S(1)}, f32[384]{0:T(512)S(1)}, /*index=5*/f32[384]{0:T(512)S(1)}) fusion(bf16[71,96,384]{2,1,0:T(8,128)(2,1)} %copy-done.4, f32[64]{0:T(128)S(1)} %copy-done.94, f32[78,96,384]{2,1,0:T(8,128)S(1)} %multiply_add_fusion, f32[64]{0:T(128)S(1)} %copy-done.76, ...), kind=kLoop, calls=%fused_computation.95 | loop fusion | flops 56620800 | bytes 37759488 | tf_op jit(solution)/shard_map/reduce_sum | solution.py:150
  525.3 14.9 %multiply_reduce_fusion.9 = (f32[384]{0:T(512)S(1)}, f32[384]{0:T(512)S(1)}, f32[384]{0:T(512)S(1)}, f32[384]{0:T(512)S(1)}, f32[384]{0:T(512)S(1)}, /*index=5*/f32[384]{0:T(512)S(1)}) fusion(bf16[71,96,384]{2,1,0:T(8,128)(2,1)} %get-tuple-element.107, f32[64]{0:T(128)S(1)} %copy-done.72, f32[78,96,384]{2,1,0:T(8,128)S(1)} %multiply_add_fusion, ...), kind=kLoop, calls=%fused_computation.103 | loop fusion | flops 56620800 | bytes 37759488 | tf_op jit(solution)/shard_map/reduce_sum | solution.py:150
  540.6 6.5 multiply_reduce_fusion.7
  547.4 43.9 %all-reduce = (f32[2,15,384]{2,1,0:T(8,128)S(1)}, f32[384]{0:T(512)}, f32[384]{0:T(512)}, f32[384]{0:T(512)}, f32[1536]{0:T(1024)}, /*index=5*/f32[384]{0:T(512)}, f32[384]{0:T(512)}) all-reduce(f32[2,15,384]{2,1,0:T(8,128)S(1)} %pad_maximum_fusion.3, f32[384]{0:T(512)S(1)} %get-tuple-element.47, ...), channel_id=1, replica_groups=mesh['th'=4,'tw'=8] {'th','tw'}, use_global_device_ids=true, to_apply=%region_37.38 | all-reduce | flops 14976 | bytes 119808 | tf_op jit(solution)/shard_map/psum | solution.py:162
  591.4 8.0 %multiply_reduce_fusion.18 = (f32[2,384,32]{1,2,0:T(8,128)}, f32[2,384,32]{1,2,0:T(8,128)}, f32[2,384,32]{1,2,0:T(8,128)S(1)}, f32[2,384,32]{1,2,0:T(8,128)S(1)}) fusion(f32[2,15,384]{2,1,0:T(8,128)S(1)} %broadcast_multiply_fusion.30, f32[2,384,32]{1,2,0:T(8,128)S(1)} %copy-done.37, f32[2,384,32]{1,2,0:T(8,128)S(1)} %copy-done.35, f32[2,384,32]{1,2,0:T(8,128)} %param.21, ...), kind=kLoop, calls=%fused_computation.120 | loop fusion | flops 8380416 | bytes 832512 | tf_op jit(solution)/shard_map/transpose(jvp())/reduce_sum | solution.py:27
  600.8 58.4 %fusion.8 = bf16[64,96,384]{2,1,0:T(8,128)(2,1)} fusion(bf16[64,96,384]{2,1,0:T(8,128)(2,1)} %copy-done.5, f32[78,96,384]{2,1,0:T(8,128)} %copy-done.1, bf16[64,96,384]{2,1,0:T(8,128)(2,1)} %param.31, f32[64,384]{1,0:T(8,128)S(1)} %copy-done.24, f32[64,384]{1,0:T(8,128)S(1)} %copy-done.22, f32[64,384]{1,0:T(8,128)S(1)} %copy-done.20, ...), kind=kLoop, calls=%fused_computation.40 | loop fusion | flops 82575360 | bytes 157092864 | tf_op jit(solution)/shard_map/convert_element_type | solution.py:161
  659.2 3.2 copy.41
  662.5 3.2 copy.42
  (281 shorter events, 8.0 us)
Async XLA Ops:
  7.2 167.9 %copy-start = (bf16[384,1536]{1,0:T(8,128)(2,1)S(1)}, bf16[384,1536]{1,0:T(8,128)(2,1)}, u32[]{:S(2)}) copy-start(bf16[384,1536]{1,0:T(8,128)(2,1)} %param.26) | copy-start | bytes 3538948
  7.2 652.0 %all-reduce.4.cloned.1.call-start = ((), (), s32[]{:S(2)}) async-start(), calls=%async_computation | async-start | bytes 9437184 | tf_op jit(solution)/shard_map/psum | solution.py:162
  8.6 19.1 %collective-permute-start = (bf16[7,96,384]{2,1,0:T(8,128)(2,1)S(1)}, bf16[7,96,384]{2,1,0:T(8,128)(2,1)S(1)}, u32[]{:S(2)}, u32[]{:S(2)}) collective-permute-start(bf16[7,96,384]{2,1,0:T(8,128)(2,1)S(1)} %get-tuple-element.113), channel_id=1, source_target_pairs={{0,8},{8,16},{16,24},{1,9},{9,17},{17,25},{2,10},{10,18},{18,26},{... | collective-permute-start | bytes 1548296 | tf_op jit(solution)/shard_map/ppermute | solution.py:14
  11.0 25.0 %collective-permute-start.1 = (bf16[7,96,384]{2,1,0:T(8,128)(2,1)S(1)}, bf16[7,96,384]{2,1,0:T(8,128)(2,1)S(1)}, u32[]{:S(2)}, u32[]{:S(2)}) collective-permute-start(bf16[7,96,384]{2,1,0:T(8,128)(2,1)S(1)} %get-tuple-element.112), channel_id=1, source_target_pairs={{8,0},{16,8},{24,16},{9,1},{17,9},{25,17},{10,2},{18,10},{26,18},{... | collective-permute-start | bytes 1548296 | tf_op jit(solution)/shard_map/ppermute | solution.py:17
  21.6 84.2 %copy-start.42 = (f32[384]{0:T(512)}, f32[384]{0:T(512)S(1)}, u32[]{:S(2)}) copy-start(f32[384]{0:T(512)S(1)} %get-tuple-element.54) | copy-start | bytes 4612
  21.6 84.2 %copy-start.44 = (f32[384]{0:T(512)}, f32[384]{0:T(512)S(1)}, u32[]{:S(2)}) copy-start(f32[384]{0:T(512)S(1)} %get-tuple-element.55) | copy-start | bytes 4612
  21.6 84.2 %copy-start.46 = (f32[384]{0:T(512)}, f32[384]{0:T(512)S(1)}, u32[]{:S(2)}) copy-start(f32[384]{0:T(512)S(1)} %get-tuple-element.56) | copy-start | bytes 4612
  21.6 84.2 %copy-start.47 = (f32[384]{0:T(512)}, f32[384]{0:T(512)S(1)}, u32[]{:S(2)}) copy-start(f32[384]{0:T(512)S(1)} %get-tuple-element.57) | copy-start | bytes 4612
  21.6 84.2 %copy-start.48 = (f32[384]{0:T(512)}, f32[384]{0:T(512)S(1)}, u32[]{:S(2)}) copy-start(f32[384]{0:T(512)S(1)} %get-tuple-element.58) | copy-start | bytes 4612
  21.6 84.2 %copy-start.49 = (f32[384]{0:T(512)}, f32[384]{0:T(512)S(1)}, u32[]{:S(2)}) copy-start(f32[384]{0:T(512)S(1)} %get-tuple-element.59) | copy-start | bytes 4612
  21.6 84.2 %copy-start.50 = (f32[384]{0:T(512)}, f32[384]{0:T(512)S(1)}, u32[]{:S(2)}) copy-start(f32[384]{0:T(512)S(1)} %get-tuple-element.60) | copy-start | bytes 4612
  21.7 84.2 %copy-start.51 = (f32[384]{0:T(512)}, f32[384]{0:T(512)S(1)}, u32[]{:S(2)}) copy-start(f32[384]{0:T(512)S(1)} %get-tuple-element.61) | copy-start | bytes 4612
  21.7 84.2 %copy-start.52 = (f32[384]{0:T(512)}, f32[384]{0:T(512)S(1)}, u32[]{:S(2)}) copy-start(f32[384]{0:T(512)S(1)} %get-tuple-element.62) | copy-start | bytes 4612
  21.7 84.2 %copy-start.53 = (f32[384]{0:T(512)}, f32[384]{0:T(512)S(1)}, u32[]{:S(2)}) copy-start(f32[384]{0:T(512)S(1)} %get-tuple-element.63) | copy-start | bytes 4612
  21.7 84.2 %copy-start.54 = (f32[384]{0:T(512)}, f32[384]{0:T(512)S(1)}, u32[]{:S(2)}) copy-start(f32[384]{0:T(512)S(1)} %get-tuple-element.64) | copy-start | bytes 4612
  21.7 84.2 %copy-start.55 = (f32[384]{0:T(512)}, f32[384]{0:T(512)S(1)}, u32[]{:S(2)}) copy-start(f32[384]{0:T(512)S(1)} %get-tuple-element.65) | copy-start | bytes 4612
  21.7 84.2 %copy-start.56 = (f32[384]{0:T(512)}, f32[384]{0:T(512)S(1)}, u32[]{:S(2)}) copy-start(f32[384]{0:T(512)S(1)} %get-tuple-element.66) | copy-start | bytes 4612
  21.7 84.2 %copy-start.57 = (f32[384]{0:T(512)}, f32[384]{0:T(512)S(1)}, u32[]{:S(2)}) copy-start(f32[384]{0:T(512)S(1)} %get-tuple-element.67) | copy-start | bytes 4612
  21.7 84.2 %copy-start.58 = (f32[384]{0:T(512)}, f32[384]{0:T(512)S(1)}, u32[]{:S(2)}) copy-start(f32[384]{0:T(512)S(1)} %get-tuple-element.68) | copy-start | bytes 4612
  39.2 24.7 %collective-permute-start.2 = (bf16[78,7,384]{2,1,0:T(8,128)(2,1)S(1)}, bf16[78,7,384]{2,1,0:T(8,128)(2,1)S(1)}, u32[]{:S(2)}, u32[]{:S(2)}) collective-permute-start(bf16[78,7,384]{2,1,0:T(8,128)(2,1)S(1)} %get-tuple-element.104), channel_id=1, source_target_pairs={{0,1},{1,2},{2,3},{3,4},{4,5},{5,6},{6,7},{8,9},{9,10},{10,11},{11... | collective-permute-start | bytes 1257992 | tf_op jit(solution)/shard_map/ppermute | solution.py:14
  43.7 20.1 %collective-permute-start.3 = (bf16[78,7,384]{2,1,0:T(8,128)(2,1)S(1)}, bf16[78,7,384]{2,1,0:T(8,128)(2,1)S(1)}, u32[]{:S(2)}, u32[]{:S(2)}) collective-permute-start(bf16[78,7,384]{2,1,0:T(8,128)(2,1)S(1)} %get-tuple-element.105), channel_id=1, source_target_pairs={{1,0},{2,1},{3,2},{4,3},{5,4},{6,5},{7,6},{9,8},{10,9},{11,10},{12... | collective-permute-start | bytes 1257992 | tf_op jit(solution)/shard_map/ppermute | solution.py:17
  173.0 95.5 %copy-start.14 = (f32[64,96]{1,0:T(8,128)}, f32[64,96]{1,0:T(8,128)S(1)}, u32[]{:S(2)}) copy-start(f32[64,96]{1,0:T(8,128)S(1)} %fusion.48) | copy-start | bytes 73732
  175.0 93.5 %copy-start.9 = (bf16[64,96,384]{2,1,0:T(8,128)(2,1)}, bf16[64,96,384]{2,1,0:T(8,128)(2,1)S(1)}, u32[]{:S(2)}) copy-start(bf16[64,96,384]{2,1,0:T(8,128)(2,1)S(1)} %add_convert_fusion.2) | copy-start | bytes 14155780
  175.1 93.4 %copy-start.7 = (bf16[64,96,384]{2,1,0:T(8,128)(2,1)S(1)}, bf16[64,96,384]{2,1,0:T(8,128)(2,1)}, u32[]{:S(2)}) copy-start(bf16[64,96,384]{2,1,0:T(8,128)(2,1)} %param.16) | copy-start | bytes 14155780
  175.1 93.4 %copy-start.97 = (f32[384]{0:T(512)S(1)}, f32[384]{0:T(512)}, u32[]{:S(2)}) copy-start(f32[384]{0:T(512)} %param.30) | copy-start | bytes 4612
  175.1 93.4 %copy-start.99 = (bf16[1536,384]{1,0:T(8,128)(2,1)S(1)}, bf16[1536,384]{1,0:T(8,128)(2,1)}, u32[]{:S(2)}) copy-start(bf16[1536,384]{1,0:T(8,128)(2,1)} %param.28) | copy-start | bytes 3538948
  175.1 93.4 %copy-start.101 = (f32[384]{0:T(512)S(1)}, f32[384]{0:T(512)}, u32[]{:S(2)}) copy-start(f32[384]{0:T(512)} %param.29) | copy-start | bytes 4612
  411.2 18.7 %collective-permute-start.4 = (bf16[7,96,384]{2,1,0:T(8,128)(2,1)S(1)}, bf16[7,96,384]{2,1,0:T(8,128)(2,1)S(1)}, u32[]{:S(2)}, u32[]{:S(2)}) collective-permute-start(bf16[7,96,384]{2,1,0:T(8,128)(2,1)S(1)} %get-tuple-element.110), channel_id=1, source_target_pairs={{0,8},{8,16},{16,24},{1,9},{9,17},{17,25},{2,10},{10,18},{18,26},{... | collective-permute-start | bytes 1548296 | tf_op jit(solution)/shard_map/ppermute | solution.py:14
  414.8 15.2 %collective-permute-start.5 = (bf16[7,96,384]{2,1,0:T(8,128)(2,1)S(1)}, bf16[7,96,384]{2,1,0:T(8,128)(2,1)S(1)}, u32[]{:S(2)}, u32[]{:S(2)}) collective-permute-start(bf16[7,96,384]{2,1,0:T(8,128)(2,1)S(1)} %get-tuple-element.111), channel_id=1, source_target_pairs={{8,0},{16,8},{24,16},{9,1},{17,9},{25,17},{10,2},{18,10},{26,18},{... | collective-permute-start | bytes 1548296 | tf_op jit(solution)/shard_map/ppermute | solution.py:17
  431.0 23.5 %collective-permute-start.6 = (bf16[78,7,384]{2,1,0:T(8,128)(2,1)S(1)}, bf16[78,7,384]{2,1,0:T(8,128)(2,1)S(1)}, u32[]{:S(2)}, u32[]{:S(2)}) collective-permute-start(bf16[78,7,384]{2,1,0:T(8,128)(2,1)S(1)} %get-tuple-element.102), channel_id=1, source_target_pairs={{1,0},{2,1},{3,2},{4,3},{5,4},{6,5},{7,6},{9,8},{10,9},{11,10},{12... | collective-permute-start | bytes 1257992 | tf_op jit(solution)/shard_map/ppermute | solution.py:17
  432.3 25.2 %collective-permute-start.7 = (bf16[78,7,384]{2,1,0:T(8,128)(2,1)S(1)}, bf16[78,7,384]{2,1,0:T(8,128)(2,1)}, u32[]{:S(2)}, u32[]{:S(2)}) collective-permute-start(bf16[78,7,384]{2,1,0:T(8,128)(2,1)S(1)} %get-tuple-element.103), channel_id=1, source_target_pairs={{0,1},{1,2},{2,3},{3,4},{4,5},{5,6},{6,7},{8,9},{9,10},{10,11},{11... | collective-permute-start | bytes 1257992 | tf_op jit(solution)/shard_map/ppermute | solution.py:14
  540.4 59.7 %copy-start.61 = (f32[2,384]{1,0:T(2,128)S(1)}, f32[2,384]{1,0:T(2,128)}, u32[]{:S(2)}) copy-start(f32[2,384]{1,0:T(2,128)} %param.22) | copy-start | bytes 9220
  540.4 60.3 %copy-start.18 = (f32[64,384]{1,0:T(8,128)S(1)}, f32[64,384]{1,0:T(8,128)}, u32[]{:S(2)}) copy-start(f32[64,384]{1,0:T(8,128)} %get-tuple-element.144) | copy-start | bytes 294916
  540.5 60.2 %copy-start.19 = (f32[64,384]{1,0:T(8,128)S(1)}, f32[64,384]{1,0:T(8,128)}, u32[]{:S(2)}) copy-start(f32[64,384]{1,0:T(8,128)} %get-tuple-element.159) | copy-start | bytes 294916
  540.5 60.2 %copy-start.20 = (f32[64,384]{1,0:T(8,128)S(1)}, f32[64,384]{1,0:T(8,128)}, u32[]{:S(2)}) copy-start(f32[64,384]{1,0:T(8,128)} %get-tuple-element.146) | copy-start | bytes 294916
  540.5 60.2 %copy-start.21 = (f32[64,384]{1,0:T(8,128)S(1)}, f32[64,384]{1,0:T(8,128)}, u32[]{:S(2)}) copy-start(f32[64,384]{1,0:T(8,128)} %get-tuple-element.157) | copy-start | bytes 294916
  540.5 60.2 %copy-start.22 = (f32[64,384]{1,0:T(8,128)S(1)}, f32[64,384]{1,0:T(8,128)}, u32[]{:S(2)}) copy-start(f32[64,384]{1,0:T(8,128)} %get-tuple-element.148) | copy-start | bytes 294916
  540.5 60.2 %copy-start.23 = (f32[64,384]{1,0:T(8,128)S(1)}, f32[64,384]{1,0:T(8,128)}, u32[]{:S(2)}) copy-start(f32[64,384]{1,0:T(8,128)} %get-tuple-element.155) | copy-start | bytes 294916
  540.5 60.2 %copy-start.24 = (f32[64,384]{1,0:T(8,128)S(1)}, f32[64,384]{1,0:T(8,128)}, u32[]{:S(2)}) copy-start(f32[64,384]{1,0:T(8,128)} %get-tuple-element.150) | copy-start | bytes 294916
  540.5 60.2 %copy-start.25 = (f32[64,384]{1,0:T(8,128)S(1)}, f32[64,384]{1,0:T(8,128)}, u32[]{:S(2)}) copy-start(f32[64,384]{1,0:T(8,128)} %get-tuple-element.153) | copy-start | bytes 294916
  540.5 60.2 %copy-start.26 = (f32[64,384]{1,0:T(8,128)S(1)}, f32[64,384]{1,0:T(8,128)}, u32[]{:S(2)}) copy-start(f32[64,384]{1,0:T(8,128)} %get-tuple-element.138) | copy-start | bytes 294916
  540.5 60.2 %copy-start.27 = (f32[64,384]{1,0:T(8,128)S(1)}, f32[64,384]{1,0:T(8,128)}, u32[]{:S(2)}) copy-start(f32[64,384]{1,0:T(8,128)} %get-tuple-element.165) | copy-start | bytes 294916
  540.5 60.2 %copy-start.28 = (f32[64,384]{1,0:T(8,128)S(1)}, f32[64,384]{1,0:T(8,128)}, u32[]{:S(2)}) copy-start(f32[64,384]{1,0:T(8,128)} %get-tuple-element.140) | copy-start | bytes 294916
  540.6 60.2 %copy-start.29 = (f32[64,384]{1,0:T(8,128)S(1)}, f32[64,384]{1,0:T(8,128)}, u32[]{:S(2)}) copy-start(f32[64,384]{1,0:T(8,128)} %get-tuple-element.163) | copy-start | bytes 294916
  540.6 60.2 %copy-start.30 = (f32[64,384]{1,0:T(8,128)S(1)}, f32[64,384]{1,0:T(8,128)}, u32[]{:S(2)}) copy-start(f32[64,384]{1,0:T(8,128)} %get-tuple-element.142) | copy-start | bytes 294916
  540.6 60.2 %copy-start.31 = (f32[64,384]{1,0:T(8,128)S(1)}, f32[64,384]{1,0:T(8,128)}, u32[]{:S(2)}) copy-start(f32[64,384]{1,0:T(8,128)} %get-tuple-element.161) | copy-start | bytes 294916
  540.6 60.2 %copy-start.60 = (f32[384]{0:T(512)S(1)}, f32[384]{0:T(512)}, u32[]{:S(2)}) copy-start(f32[384]{0:T(512)} %copy-done.59) | copy-start | bytes 4612
  540.6 60.2 %copy-start.66 = (f32[384]{0:T(512)S(1)}, f32[384]{0:T(512)}, u32[]{:S(2)}) copy-start(f32[384]{0:T(512)} %param.23) | copy-start | bytes 4612
  (69 other events, 1317.0 us)
Sparse Core Ops, SparseCore 0:
  454.6 149.1 all-reduce.3
where the time goes:
time: 677 us; the launch traced here: 673 us
  other arithmetic  358 us (53%)
  matrix products  193 us (29%)
  blocking collectives  43.9 us (6%)
  local copies, waits for them, and re-layouts  23.2 us (3%)
  starting transfers between devices  21.6 us (3%)
  waiting for transfers between devices  16.9 us (2%)
  between operations  16.4 us (2%)
    dot_general x1, matrix products, per_device(): pre = jnp.dot(normed, w_in, preferred_element_type=jnp.float32) + b_in  93.4 us
    reduce_sum x1, other arithmetic, per_device(): jnp.sum(d_mixed * partial_ext[:, tap:tap + width], axis=(0, 1))  63.6 us
    reduce_sum x1, other arithmetic, normalize(): mean = jnp.mean(mixed, axis=-1, keepdims=True)  60.6 us
    convert_element_type x1, other arithmetic, per_device(): image_grad = image_grad.astype(jnp.bfloat16)  58.4 us
    psum x1, blocking collectives, per_device(): lax.psum((d_win, d_wout, d_bin, d_bout, d_scale, d_gain, d_bias, d_skip,...  43.9 us
    add x1, other arithmetic, cols_filter_back(): total + col_taps[tap][None, None, :] * extended[:, offset:offset + width]  40.2 us
    reduce_sum x3, other arithmetic, per_device(): jnp.sum(d_partial * row_mask(ident, tap, height, reach) * pixel_rows[tap:...  38.9 us
    add x1, other arithmetic, rows_filter(): total + row_taps[tap][None, None, :] * row_mask(ident, tap, height, reach...  36.9 us
  transfers between devices with their start and end apart: 9, of which 2 were waited for; matrix products, arithmetic and copies ran while one was open for 32% of the time, Pallas kernels for 0%

commit v1 on v0

v1 whole, which is shorter than its diff:
```python
import functools

import jax
import jax.numpy as jnp
from jax import lax
from jax.experimental import pallas as pl
from jax.experimental.pallas import tpu as pltpu
from jax.sharding import PartitionSpec as P

KSIZE = 15
REACH = KSIZE // 2
EDGE = 8
LANES = 128
MIB = 2**20


def shift(block, axis, step):
    count = lax.axis_size(axis)
    pairs = [(i, i + step) for i in range(count) if 0 <= i + step < count]
    return lax.ppermute(block, axis, pairs)


def swap(block, axis, bit):
    count = lax.axis_size(axis)
    return lax.ppermute(block, axis, [(i, i ^ bit) for i in range(count)])


def halo(block):
    above = shift(block[-REACH:], "th", 1)
    below = shift(block[:REACH], "th", -1)
    tall_right = jnp.concatenate([above[:, -EDGE:], block[:, -EDGE:], below[:, -EDGE:]], axis=0)
    tall_left = jnp.concatenate([above[:, :EDGE], block[:, :EDGE], below[:, :EDGE]], axis=0)
    left = shift(tall_right, "tw", 1)
    right = shift(tall_left, "tw", -1)
    return above, below, left, right


def powers(rate, freq, log_step):
    step = jnp.exp(log_step)
    decay = jnp.exp(-jnp.exp(rate) * step)
    phase = freq * step
    return decay * jnp.cos(phase), decay * jnp.sin(phase), step


def taps_kernel(zr_ref, zi_ref, cr_ref, ci_ref, taps_ref):
    for d in range(2):
        zr, zi = zr_ref[d], zi_ref[d]
        cr, ci = cr_ref[d], ci_ref[d]
        ur, ui = jnp.ones_like(zr), jnp.zeros_like(zr)
        for m in range(KSIZE):
            taps_ref[d, m] = 2.0 * jnp.sum(cr * ur - ci * ui, axis=0)
            ur, ui = ur * zr - ui * zi, ur * zi + ui * zr
        taps_ref[d, KSIZE] = jnp.zeros_like(taps_ref[d, KSIZE])


def taps_grad_kernel(
    zr_ref, zi_ref, cr_ref, ci_ref, rate_ref, freq_ref, step_ref, g_ref,
    d_rate_ref, d_freq_ref, d_cr_ref, d_ci_ref, d_step_ref,
):
    for d in range(2):
        zr, zi = zr_ref[d], zi_ref[d]
        cr, ci = cr_ref[d], ci_ref[d]
        ur, ui = jnp.ones_like(zr), jnp.zeros_like(zr)
        su, sv = jnp.zeros_like(zr), jnp.zeros_like(zr)
        mu, mv = jnp.zeros_like(zr), jnp.zeros_like(zr)
        for m in range(KSIZE):
            g = 2.0 * g_ref[d, m][None, :]
            gu, gv = g * ur, g * ui
            su, sv = su + gu, sv + gv
            if m:
                mu, mv = mu + float(m) * gu, mv + float(m) * gv
            ur, ui = ur * zr - ui * zi, ur * zi + ui * zr
        step = step_ref[d][None, :]
        freq = freq_ref[d]
        d_freq = -step * (cr * mv + ci * mu)
        d_rate = -jnp.exp(rate_ref[d]) * step * (cr * mu - ci * mv)
        d_cr_ref[d] = su
        d_ci_ref[d] = -sv
        d_freq_ref[d] = d_freq
        d_rate_ref[d] = d_rate
        d_step_ref[d] = jnp.sum(d_rate + freq * d_freq, axis=0)


def load_tile(ext, centre, above, below, left, right, height, width):
    wide = ext.shape[1]
    at = 0 if left is None else EDGE
    full = height + 2 * REACH
    ext[full] = jnp.zeros(ext.shape[1:], jnp.float32)
    for i in range(REACH):
        ext[i, at : at + width] = above[i].astype(jnp.float32)
        ext[REACH + height + i, at : at + width] = below[i].astype(jnp.float32)

    def row(r, _):
        ext[r + REACH, at : at + width] = centre[r].astype(jnp.float32)
        return 0

    lax.fori_loop(0, height, row, 0)
    if left is not None:

        def sides(r, _):
            ext[r, 0:EDGE] = left[r].astype(jnp.float32)
            ext[r, EDGE + width : wide] = right[r].astype(jnp.float32)
            return 0

        lax.fori_loop(0, full, sides, 0)


def conv_kernel(
    source_ref, taps_ref, skip_ref, centre, above, below, left, right, mixed_ref, partial_ref, ext
):
    height, width = centre.shape[0], centre.shape[1]
    load_tile(ext, centre, above, below, left, right, height, width)
    rows = [taps_ref[0, i][None, :] for i in range(KSIZE)]
    cols = [taps_ref[1, j][None, :] for j in range(KSIZE)]
    skip = skip_ref[0][None, :]

    def row(r, _):
        total = rows[0] * ext[source_ref[r * KSIZE]]
        for i in range(1, KSIZE):
            total = total + rows[i] * ext[source_ref[r * KSIZE + i]]
        partial_ref[r] = total
        return 0

    lax.fori_loop(0, height, row, 0)

    def col(r, _):
        total = skip * ext[r + REACH, EDGE : EDGE + width]
        for j in range(KSIZE):
            total = total + cols[j] * partial_ref[r, 1 + j : 1 + j + width]
        mixed_ref[r] = total
        return 0

    lax.fori_loop(0, height, col, 0)


def conv_back_kernel(
    source_ref, taps_ref, skip_ref, partial_ref, grad_ref,
    centre, above, below, left, right, image, image_above, image_below,
    image_grad_ref, sums_ref, ext, image_ext, d_partial, col_sums, row_sums, skip_sums,
):
    height, width = centre.shape[0], centre.shape[1]
    full = height + 2 * REACH
    load_tile(ext, centre, above, below, left, right, height, width)
    load_tile(image_ext, image, image_above, image_below, None, None, height, width)
    rows = [taps_ref[0, i][None, :] for i in range(KSIZE)]
    cols = [taps_ref[1, j][None, :] for j in range(KSIZE)]
    skip = skip_ref[0][None, :]
    for sums in (col_sums, row_sums):
        sums[...] = jnp.zeros(sums.shape, jnp.float32)
    skip_sums[...] = jnp.zeros(skip_sums.shape, jnp.float32)
    d_partial[full] = jnp.zeros(d_partial.shape[1:], jnp.float32)

    def fold(v):
        return jnp.sum(v.reshape(width // 8, 8, v.shape[-1]), axis=0)

    def back_col(e, _):
        total = cols[0] * ext[e, KSIZE : KSIZE + width]
        for j in range(1, KSIZE):
            total = total + cols[j] * ext[e, KSIZE - j : KSIZE - j + width]
        d_partial[e] = total
        return 0

    lax.fori_loop(0, full, back_col, 0)

    def col_grad(r, _):
        d = ext[r + REACH, EDGE : EDGE + width]
        for j in range(KSIZE):
            col_sums[j] += fold(d * partial_ref[r, 1 + j : 1 + j + width])
        skip_sums[...] += fold(d * image_ext[r + REACH])
        return 0

    lax.fori_loop(0, height, col_grad, 0)

    def row_grad(r, _):
        d = d_partial[r + REACH]
        for i in range(KSIZE):
            row_sums[i] += fold(d * image_ext[source_ref[r * KSIZE + i]])
        return 0

    lax.fori_loop(0, height, row_grad, 0)

    def back_row(r, _):
        total = grad_ref[r].astype(jnp.float32) + skip * ext[r + REACH, EDGE : EDGE + width]
        for i in range(KSIZE):
            total = total + rows[i] * d_partial[source_ref[r * KSIZE + KSIZE - 1 - i]]
        image_grad_ref[r] = total.astype(jnp.bfloat16)
        return 0

    lax.fori_loop(0, height, back_row, 0)
    sums_ref[0:KSIZE] = jnp.sum(row_sums[...], axis=1)
    sums_ref[KSIZE : 2 * KSIZE] = jnp.sum(col_sums[...], axis=1)
    sums_ref[2 * KSIZE : 2 * KSIZE + 1] = jnp.sum(skip_sums[...], axis=0, keepdims=True)
    sums_ref[2 * KSIZE + 1 :] = jnp.zeros(
        (sums_ref.shape[0] - 2 * KSIZE - 1, sums_ref.shape[1]), jnp.float32
    )


def dot(a, b, dims=((1,), (0,))):
    return lax.dot_general(a, b, (dims, ((), ())), preferred_element_type=jnp.float32)


def feed_kernel(
    mixed_ref, image_ref, grad_ref, w_in_ref, w_out_t_ref, w_in_t_ref, w_out_ref,
    b_in_ref, vectors_ref,
    output_ref, d_mixed_ref, weights_ref, b_sums_ref, sums_ref,
    act_ref, d_pre_ref, total_ref,
):
    step = pl.program_id(0)
    chans, hidden = w_in_ref.shape
    piece = 512

    @pl.when(step == 0)
    def _():
        total_ref[...] = jnp.zeros(total_ref.shape, jnp.float32)
        b_sums_ref[...] = jnp.zeros(b_sums_ref.shape, jnp.float32)
        sums_ref[...] = jnp.zeros(sums_ref.shape, jnp.float32)

    gain, bias = vectors_ref[0:1], vectors_ref[1:2]
    b_out, scale = vectors_ref[2:3], vectors_ref[3:4]
    mixed = mixed_ref[...]
    mean = jnp.mean(mixed, axis=-1, keepdims=True)
    centred = mixed - mean
    var = jnp.mean(centred * centred, axis=-1, keepdims=True)
    inverse = lax.rsqrt(var + 1e-06)
    xhat = centred * inverse
    normed = (xhat * gain + bias).astype(jnp.bfloat16)
    grad = grad_ref[...].astype(jnp.float32)
    d_branch = (scale * grad).astype(jnp.bfloat16)
    normed_t = normed.T
    d_branch_t = d_branch.T
    ones = jnp.ones((8, normed.shape[0]), jnp.bfloat16)
    for k in range(0, hidden, piece):
        cut = slice(k, k + piece)
        pre = dot(normed, w_in_ref[:, cut]) + b_in_ref[:, cut]
        d_act = dot(d_branch, w_out_t_ref[:, cut])
        half = 0.5 + 0.5 * lax.erf(pre * 0.7071067811865476)
        bell = jnp.exp(pre * pre * -0.5) * 0.3989422804014327
        act = (pre * half).astype(jnp.bfloat16)
        d_pre = (d_act * (half + pre * bell)).astype(jnp.bfloat16)
        act_ref[:, cut] = act
        d_pre_ref[:, cut] = d_pre
        total_ref[0:chans, cut] += dot(normed_t, d_pre)
        total_ref[chans : 2 * chans, cut] += dot(d_branch_t, act)
        b_sums_ref[:, cut] += dot(ones, d_pre)
    branch = dot(act_ref[...], w_out_ref[...]) + b_out
    output_ref[...] = (image_ref[...].astype(jnp.float32) + scale * branch).astype(jnp.bfloat16)
    d_normed = dot(d_pre_ref[...], w_in_t_ref[...])

    def fold(v):
        return jnp.sum(v.reshape(v.shape[0] // 8, 8, v.shape[1]), axis=0)

    g = d_normed * gain
    g_mean = jnp.mean(g, axis=-1, keepdims=True)
    g_xhat = jnp.mean(g * xhat, axis=-1, keepdims=True)
    d_mixed_ref[...] = ((g - g_mean - xhat * g_xhat) * inverse).astype(jnp.bfloat16)
    sums_ref[0] += fold(d_normed * xhat)
    sums_ref[1] += fold(d_normed)
    sums_ref[2] += fold(d_branch.astype(jnp.float32))
    sums_ref[3] += fold(grad * branch)

    @pl.when(step == pl.num_programs(0) - 1)
    def _():
        weights_ref[...] = total_ref[...].astype(jnp.bfloat16)


def whole(shape):
    return pl.BlockSpec(shape, lambda *_: (0,) * len(shape))


def sum_over_mesh(part, steps):
    for axis, bit in steps:
        part = part + swap(part, axis, bit)
    return part


def mesh_steps():
    steps = []
    for axis in ("th", "tw"):
        bit = 1
        while bit < lax.axis_size(axis):
            steps.append((axis, bit))
            bit *= 2
    return steps


def scatter_gather(block, steps):
    places = []
    for axis, bit in steps:
        side = lax.rem(lax.axis_index(axis) // bit, 2)
        size = block.shape[0] // 2
        keep = lax.dynamic_slice_in_dim(block, side * size, size, 0)
        give = lax.dynamic_slice_in_dim(block, (1 - side) * size, size, 0)
        take = swap(give, axis, bit)
        block = (keep.astype(jnp.float32) + take.astype(jnp.float32)).astype(jnp.bfloat16)
        places.append((axis, bit, side))
    for axis, bit, side in reversed(places):
        other = swap(block, axis, bit)
        block = jnp.where(
            side == 0,
            jnp.concatenate([block, other], axis=0),
            jnp.concatenate([other, block], axis=0),
        )
    return block


def per_device(
    image, image_heights, rate_log, freq, coef_re, coef_im, log_step, skip, ln_gain, ln_bias,
    w_in, b_in, w_out, b_out, layer_scale, out_grad,
):
    height, width, chans = image.shape
    hidden = w_in.shape[1]
    pixels = height * width
    full = height + 2 * REACH
    wide = width + 2 * EDGE
    blocks = chans // LANES
    f32, bf16 = jnp.float32, jnp.bfloat16

    above, below, left, right = halo(image)

    first, second = image_heights[0], image_heights[0] + image_heights[1]
    start = lax.axis_index("th") * height

    def ident(r):
        return (r >= first).astype(jnp.int32) + (r >= second).astype(jnp.int32)

    row = jnp.arange(height, dtype=jnp.int32)[:, None]
    tap = jnp.arange(KSIZE, dtype=jnp.int32)[None, :]
    source = jnp.where(
        ident(start + row) == ident(start + row + tap - REACH), row + tap, full
    ).reshape(-1)

    rate_t, freq_t, cr_t, ci_t = (v.transpose(0, 2, 1) for v in (rate_log, freq, coef_re, coef_im))
    zr, zi, step = powers(rate_t, freq_t, log_step[:, None, :])
    step = step[:, 0]
    taps = pl.pallas_call(
        taps_kernel, out_shape=jax.ShapeDtypeStruct((2, KSIZE + 1, chans), f32)
    )(zr, zi, cr_t, ci_t)

    lane_block = lambda *lead: pl.BlockSpec((*lead, LANES), lambda c: (0,) * len(lead) + (c,))
    smem = pl.BlockSpec(memory_space=pltpu.SMEM)
    skip_row = skip[None, :]
    mixed, partial = pl.pallas_call(
        conv_kernel,
        grid=(blocks,),
        in_specs=[
            smem, lane_block(2, KSIZE + 1), lane_block(1), lane_block(height, width),
            lane_block(REACH, width), lane_block(REACH, width),
            lane_block(full, EDGE), lane_block(full, EDGE),
        ],
        out_specs=[lane_block(height, width), lane_block(height, wide)],
        out_shape=[
            jax.ShapeDtypeStruct((height, width, chans), f32),
            jax.ShapeDtypeStruct((height, wide, chans), f32),
        ],
        scratch_shapes=[pltpu.VMEM((full + 1, wide, LANES), f32)],
        compiler_params=pltpu.CompilerParams(vmem_limit_bytes=48 * MIB),
        cost_estimate=pl.CostEstimate(
            flops=60 * pixels * chans, bytes_accessed=12 * pixels * chans, transcendentals=0
        ),
        name="filter_forward",
    )(source, taps, skip_row, image, above, below, left, right)

    tile = 768
    pixel_block = pl.BlockSpec((tile, chans), lambda i: (i, 0))
    vectors = jnp.stack([ln_gain, ln_bias, b_out, layer_scale])
    output, d_mixed, weights, b_sums, sums = pl.pallas_call(
        feed_kernel,
        grid=(pixels // tile,),
        in_specs=[
            pixel_block, pixel_block, pixel_block,
            whole((chans, hidden)), whole((chans, hidden)), whole((hidden, chans)), whole((hidden, chans)),
            whole((1, hidden)), whole((4, chans)),
        ],
        out_specs=[
            pixel_block, pixel_block, whole((2 * chans, hidden)), whole((8, hidden)), whole((4, 8, chans)),
        ],
        out_shape=[
            jax.ShapeDtypeStruct((pixels, chans), bf16),
            jax.ShapeDtypeStruct((pixels, chans), bf16),
            jax.ShapeDtypeStruct((2 * chans, hidden), bf16),
            jax.ShapeDtypeStruct((8, hidden), f32),
            jax.ShapeDtypeStruct((4, 8, chans), f32),
        ],
        scratch_shapes=[
            pltpu.VMEM((tile, hidden), bf16),
            pltpu.VMEM((tile, hidden), bf16),
            pltpu.VMEM((2 * chans, hidden), f32),
        ],
        compiler_params=pltpu.CompilerParams(vmem_limit_bytes=60 * MIB),
        cost_estimate=pl.CostEstimate(
            flops=12 * pixels * chans * hidden, bytes_accessed=14 * pixels * chans, transcendentals=0
        ),
        name="feed_forward",
    )(
        mixed.reshape(pixels, chans), image.reshape(pixels, chans), out_grad.reshape(pixels, chans),
        w_in, w_out.T, w_in.T, w_out, b_in[None, :], vectors,
    )
    output = output.reshape(height, width, chans)
    d_mixed = d_mixed.reshape(height, width, chans)

    g_above, g_below, g_left, g_right = halo(d_mixed)
    n_sums = 2 * KSIZE + 2
    image_grad, tap_sums = pl.pallas_call(
        conv_back_kernel,
        grid=(blocks,),
        in_specs=[
            smem, lane_block(2, KSIZE + 1), lane_block(1), lane_block(height, wide), lane_block(height, width),
            lane_block(height, width), lane_block(REACH, width), lane_block(REACH, width),
            lane_block(full, EDGE), lane_block(full, EDGE),
            lane_block(height, width), lane_block(REACH, width), lane_block(REACH, width),
        ],
        out_specs=[lane_block(height, width), lane_block(n_sums)],
        out_shape=[
            jax.ShapeDtypeStruct((height, width, chans), bf16),
            jax.ShapeDtypeStruct((n_sums, chans), f32),
        ],
        scratch_shapes=[
            pltpu.VMEM((full + 1, wide, LANES), f32),
            pltpu.VMEM((full + 1, width, LANES), f32),
            pltpu.VMEM((full + 1, width, LANES), f32),
            pltpu.VMEM((KSIZE, 8, LANES), f32),
            pltpu.VMEM((KSIZE, 8, LANES), f32),
            pltpu.VMEM((8, LANES), f32),
        ],
        compiler_params=pltpu.CompilerParams(vmem_limit_bytes=60 * MIB),
        cost_estimate=pl.CostEstimate(
            flops=120 * pixels * chans, bytes_accessed=16 * pixels * chans, transcendentals=0
        ),
        name="filter_backward",
    )(
        source, taps, skip_row, partial, out_grad, d_mixed, g_above, g_below, g_left, g_right,
        image, above, below,
    )

    steps = mesh_steps()
    small = jnp.concatenate(
        [tap_sums, jnp.sum(sums, axis=1), b_sums[0].reshape(hidden // chans, chans)], axis=0
    )
    small = sum_over_mesh(small, steps)
    weights = scatter_gather(weights, steps).astype(f32)
    d_taps = small[: 2 * KSIZE].reshape(2, KSIZE, chans)
    d_skip = small[2 * KSIZE]
    d_gain, d_bias, d_bout, d_scale = (small[n_sums + i] for i in range(4))
    d_bin = small[n_sums + 4 :].reshape(hidden)

    mode_shape = jax.ShapeDtypeStruct(zr.shape, f32)
    g_rate, g_freq, g_re, g_im, g_step = pl.pallas_call(
        taps_grad_kernel,
        out_shape=[mode_shape] * 4 + [jax.ShapeDtypeStruct((2, chans), f32)],
    )(zr, zi, cr_t, ci_t, rate_t, freq_t, step, d_taps)
    g_rate, g_freq, g_re, g_im = (v.transpose(0, 2, 1) for v in (g_rate, g_freq, g_re, g_im))
    return (
        output, image_grad, g_rate, g_freq, g_re, g_im, g_step, d_skip, d_gain, d_bias,
        weights[:chans], d_bin, weights[chans:].T, d_bout, d_scale,
    )


def solution(mesh):
    tiled = P("th", "tw", None)
    return jax.shard_map(
        per_device,
        mesh=mesh,
        in_specs=(tiled,) + (P(),) * 14 + (tiled,),
        out_specs=(tiled, tiled) + (P(),) * 13,
        check_vma=False,
    )
```

time: 677 us -> 335 us (0.49)
  other arithmetic: 358 us -> 11.4 us
  matrix products: 193 us -> 0 us
  Pallas kernels: 0 us -> 178 us
  waiting for transfers between devices: 16.9 us -> 64.4 us
  blocking collectives: 43.9 us -> 0 us
  starting transfers between devices: 21.6 us -> 57 us
  between operations: 16.4 us -> 2.54 us
    reduce_sum x13 -> x1, other arithmetic: 197 us -> 0.03 us  [per_device(): jnp.sum(sums, axis=1)]
    dot_general x6 -> x0, matrix products: 193 us -> none  [the longest x1 93.4 us: per_device(): pre = jnp.dot(normed, w_in, preferred_element_type=jnp.float32) + b_in]
    pallas_call x0 -> x5, Pallas kernels: none -> 178 us  [the longest x1 76.7 us: per_device(): pl.pallas_call(feed_kernel, grid=(pixels // tile,), in_specs=[pixel_block...]
    add x3 -> x6, other arithmetic: 77.1 us -> 1.5 us  [the longest x5 0.85 us: sum_over_mesh(): part = part + swap(part, axis, bit)]
    convert_element_type x4 -> x6, other arithmetic: 60.6 us -> 2.51 us  [the longest x5 1.82 us: scatter_gather(): (keep.astype(jnp.float32) + take.astype(jnp.float32)).astype(jnp.bfloat16)]
    ppermute x8 -> x23, waiting for transfers between devices: 16.9 us -> 64.4 us  [the longest x15 56.2 us: swap(): return lax.ppermute(block, axis, [(i, i ^ bit) for i in range(count)])]
    psum x1 -> x0, blocking collectives: 43.9 us -> none  [per_device(): lax.psum((d_win, d_wout, d_bin, d_bout, d_scale, d_gain, d_bias, d_skip,...]
    ppermute x8 -> x23, starting transfers between devices: 21.6 us -> 57 us  [the longest x15 36.2 us: swap(): return lax.ppermute(block, axis, [(i, i ^ bit) for i in range(count)])]
  transfers between devices with their start and end apart: 9 -> 23, of which waited for: 2 -> 14; matrix products, arithmetic and copies ran while one was open for 32% -> 6% of each run, Pallas kernels for 0% -> 20%
where the time goes in v1:
time: 335 us; the launch traced here: 334 us
  Pallas kernels  178 us (53%)
  waiting for transfers between devices  64.4 us (19%)
  starting transfers between devices  57 us (17%)
  local copies, waits for them, and re-layouts  20.8 us (6%)
  other arithmetic  11.4 us (3%)
    pallas_call x1, Pallas kernels, per_device(): pl.pallas_call(feed_kernel, grid=(pixels // tile,), in_specs=[pixel_block...  76.7 us
    pallas_call x1, Pallas kernels, per_device(): pl.pallas_call(conv_back_kernel, grid=(blocks,), in_specs=[smem, lane_blo...  62.3 us
    ppermute x15, waiting for transfers between devices, swap(): return lax.ppermute(block, axis, [(i, i ^ bit) for i in range(count)])  56.2 us
    ppermute x15, starting transfers between devices, swap(): return lax.ppermute(block, axis, [(i, i ^ bit) for i in range(count)])  36.2 us
    pallas_call x1, Pallas kernels, per_device(): pl.pallas_call(conv_kernel, grid=(blocks,), in_specs=[smem, lane_block(2,...  34.3 us
    ppermute x8, starting transfers between devices, shift(): return lax.ppermute(block, axis, pairs)  20.8 us
    ppermute x8, waiting for transfers between devices, shift(): return lax.ppermute(block, axis, pairs)  8.24 us
  transfers between devices with their start and end apart: 23, of which 14 were waited for; matrix products, arithmetic and copies ran while one was open for 6% of the time, Pallas kernels for 20%

profile of v1, /device:TPU:0, one launch (start us, length us, event | category | flops | bytes accessed | tf_op | source)
XLA Modules:
  0.0 334.2 jit_solution(4284145891237865139)
XLA Ops:
  0.6 2.3 fusion.8
  2.9 1.4 collective-permute-start.1
  4.3 3.1 collective-permute-start
  7.4 1.3 fusion.13
  10.7 1.2 fusion.7
  12.8 4.9 %collective-permute-start.2 = (bf16[78,8,384]{2,1,0:T(8,128)(2,1)}, bf16[78,8,384]{2,1,0:T(8,128)(2,1)S(1)}, u32[]{:S(2)}, u32[]{:S(2)}) collective-permute-start(bf16[78,8,384]{2,1,0:T(8,128)(2,1)} %pad_maximum_fusion), channel_id=1, source_target_pairs={{0,1},{1,2},{2,3},{3,4},{4,5},{5,6},{6,7},{8,9},{9,10},{10,11},{11... | collective-permute-start | bytes 1437704 | tf_op jit(solution)/shard_map/ppermute | solution.py:20
  18.6 1.3 collective-permute-start.3
  20.9 2.4 copy.34
  23.3 1.4 copy.35
  26.5 2.3 shard_map.271.taps_ref
  29.4 8.2 %collective-permute-done.2.left = bf16[78,8,384]{2,1,0:T(8,128)(2,1)S(1)} collective-permute-done((bf16[78,8,384]{2,1,0:T(8,128)(2,1)}, bf16[78,8,384]{2,1,0:T(8,128)(2,1)S(1)}, u32[]{:S(2)}, u32[]{:S(2)}) %collective-permute-start.2) | collective-permute-done | bytes 479264 | tf_op jit(solution)/shard_map/ppermute | solution.py:20
  38.4 34.3 %filter_forward.1 = (f32[64,96,384]{2,1,0:T(8,128)}, f32[64,112,384]{2,1,0:T(8,128)}) custom-call(s32[960]{0:T(1024)S(1)} %reshape.102.source_ref, f32[2,16,384]{2,1,0:T(8,128)S(1)} %copy-done.2, f32[1,384]{1,0:T(1,128)S(1)} %broadcast_in_dim.14.skip_ref, bf16[64,96,384]{2,1,0:T(8,128)(2,1)} %image.1, ...), custom_call_target="tpu_custom_call" | custom-call | flops 141557760 | bytes 28311552 | tf_op jit(solution)/shard_map/filter_forward/pallas_call | solution.py:342
  72.7 76.7 %feed_forward.1 = (bf16[6144,384]{1,0:T(8,128)(2,1)}, bf16[6144,384]{1,0:T(8,128)(2,1)}, bf16[768,1536]{1,0:T(8,128)(2,1)}, f32[8,1536]{1,0:T(8,128)}, f32[4,8,384]{2,1,0:T(8,128)}) custom-call(f32[6144,384]{1,0:T(8,128)} %bitcast.39, bf16[6144,384]{1,0:T(8,128)(2,1)} %bitcast.25, bf16[6144,384]{1,0:T(8,128)(2,1)} %bitcast.28, bf16[384,1536]{1,0:T(8,128)(2,1)} %w_in_ref.1, ...), custom_call_target="tpu_custom_call" | custom-call | flops 43486543872 | bytes 33030144 | tf_op jit(solution)/shard_map/feed_forward/pallas_call | solution.py:366
  149.4 1.5 constant_dynamic-slice_fusion.4
  150.9 2.1 collective-permute-start.13
  153.0 2.6 collective-permute-done.13
  155.6 1.5 add_convert_fusion
  157.5 15.5 %collective-permute-done.14 = bf16[192,1536]{1,0:T(8,128)(2,1)S(1)} collective-permute-done((bf16[192,1536]{1,0:T(8,128)(2,1)S(1)}, bf16[192,1536]{1,0:T(8,128)(2,1)S(1)}, u32[]{:S(2)}, u32[]{:S(2)}) %collective-permute-start.14) | collective-permute-done | bytes 589856 | tf_op jit(solution)/shard_map/ppermute | solution.py:25
  173.1 2.1 collective-permute-start.15
  175.2 6.7 %collective-permute-done.15 = bf16[96,1536]{1,0:T(8,128)(2,1)S(1)} collective-permute-done((bf16[96,1536]{1,0:T(8,128)(2,1)S(1)}, bf16[96,1536]{1,0:T(8,128)(2,1)S(1)}, u32[]{:S(2)}, u32[]{:S(2)}) %collective-permute-start.15) | collective-permute-done | bytes 294944 | tf_op jit(solution)/shard_map/ppermute | solution.py:25
  182.1 2.8 collective-permute-start.16
  184.9 3.1 collective-permute-done.16
  188.1 3.2 collective-permute-start.17
  191.3 2.4 collective-permute-done.17
  193.7 3.4 %collective-permute-start.18 = (bf16[24,1536]{1,0:T(8,128)(2,1)S(1)}, bf16[24,1536]{1,0:T(8,128)(2,1)S(1)}, u32[]{:S(2)}, u32[]{:S(2)}) collective-permute-start(bf16[24,1536]{1,0:T(8,128)(2,1)S(1)} %add_convert_fusion.4), channel_id=1, source_target_pairs={{0,4},{1,5},{2,6},{3,7},{4,0},{5,1},{6,2},{7,3},{8,12},{9,13},{10,... | collective-permute-start | bytes 221192 | tf_op jit(solution)/shard_map/ppermute | solution.py:25
  197.1 2.6 collective-permute-done.18
  199.8 3.7 %collective-permute-start.19 = (bf16[48,1536]{1,0:T(8,128)(2,1)S(1)}, bf16[48,1536]{1,0:T(8,128)(2,1)S(1)}, u32[]{:S(2)}, u32[]{:S(2)}) collective-permute-start(bf16[48,1536]{1,0:T(8,128)(2,1)S(1)} %maximum_select_fusion.4), channel_id=1, source_target_pairs={{0,2},{1,3},{2,0},{3,1},{4,6},{5,7},{6,4},{7,5},{8,10},{9,11},{10,... | collective-permute-start | bytes 442376 | tf_op jit(solution)/shard_map/ppermute | solution.py:25
  203.5 3.1 collective-permute-done.19
  206.9 1.3 fusion.6
  208.2 1.3 collective-permute-start.5
  209.5 3.1 collective-permute-start.4
  212.6 1.2 fusion.5
  215.5 4.5 %collective-permute-start.6 = (bf16[78,8,384]{2,1,0:T(8,128)(2,1)}, bf16[78,8,384]{2,1,0:T(8,128)(2,1)}, u32[]{:S(2)}, u32[]{:S(2)}) collective-permute-start(bf16[78,8,384]{2,1,0:T(8,128)(2,1)} %pad_maximum_fusion.2), channel_id=1, source_target_pairs={{0,1},{1,2},{2,3},{3,4},{4,5},{5,6},{6,7},{8,9},{9,10},{10,11},{11... | collective-permute-start | bytes 1437704 | tf_op jit(solution)/shard_map/ppermute | solution.py:20
  220.9 1.3 collective-permute-start.7
  222.2 8.1 %collective-permute-done.21 = bf16[192,1536]{1,0:T(8,128)(2,1)S(1)} collective-permute-done((bf16[192,1536]{1,0:T(8,128)(2,1)S(1)}, bf16[192,1536]{1,0:T(8,128)(2,1)S(1)}, u32[]{:S(2)}, u32[]{:S(2)}) %collective-permute-start.21) | collective-permute-done | bytes 589856 | tf_op jit(solution)/shard_map/ppermute | solution.py:25
  230.7 1.1 collective-permute-start.22
  232.8 62.3 %filter_backward.1 = (bf16[64,96,384]{2,1,0:T(8,128)(2,1)}, f32[32,384]{1,0:T(8,128)}) custom-call(s32[960]{0:T(1024)} %copy-done.3, f32[2,16,384]{2,1,0:T(8,128)} %shard_map.271.taps_ref, f32[1,384]{1,0:T(1,128)} %copy-done.4, f32[64,112,384]{2,1,0:T(8,128)} %get-tuple-element.31.partial_ref, bf16[64,96,384]{2,1,0:T(8,128)(2,1)} %grad_ref.1, ...), custom_call_target="tpu_custom_call" | custom-call | flops 283115520 | bytes 37748736 | tf_op jit(solution)/shard_map/filter_backward/pallas_call | solution.py:403
  295.8 8.7 %collective-permute-start.8 = (f32[40,384]{1,0:T(8,128)S(1)}, f32[40,384]{1,0:T(8,128)S(1)}, u32[]{:S(2)}, u32[]{:S(2)}) collective-permute-start(f32[40,384]{1,0:T(8,128)S(1)} %pad_maximum_fusion.4), channel_id=1, source_target_pairs={{0,8},{8,0},{16,24},{24,16},{1,9},{9,1},{17,25},{25,17},{2,10},{10... | collective-permute-start | bytes 184328 | tf_op jit(solution)/shard_map/ppermute | solution.py:25
  306.8 3.8 %collective-permute-done.9 = f32[40,384]{1,0:T(8,128)S(1)} collective-permute-done((f32[40,384]{1,0:T(8,128)S(1)}, f32[40,384]{1,0:T(8,128)S(1)}, u32[]{:S(2)}, u32[]{:S(2)}) %collective-permute-start.9) | collective-permute-done | bytes 61472 | tf_op jit(solution)/shard_map/ppermute | solution.py:25
  310.6 2.3 collective-permute-start.10
  312.9 2.2 collective-permute-done.10
  315.1 3.0 collective-permute-start.11
  318.0 2.2 collective-permute-done.11
  320.2 2.3 collective-permute-start.12
  322.5 2.9 collective-permute-done.12
  326.7 2.5 shard_map.272
  330.5 1.7 slice_bitcast_fusion
  332.3 1.9 copy.36
  (101 shorter events, 16.8 us)
Async XLA Ops:
  2.9 17.8 %copy-start.14 = (f32[2,384]{1,0:T(2,128)S(1)}, f32[2,384]{1,0:T(2,128)}, u32[]{:S(2)}) copy-start(f32[2,384]{1,0:T(2,128)} %param.22) | copy-start | bytes 9220
  2.9 17.9 %copy-start.15 = (f32[384]{0:T(512)S(1)}, f32[384]{0:T(512)}, u32[]{:S(2)}) copy-start(f32[384]{0:T(512)} %param.23) | copy-start | bytes 4612
  2.9 9.0 %collective-permute-start.1 = (bf16[7,96,384]{2,1,0:T(8,128)(2,1)}, bf16[7,96,384]{2,1,0:T(8,128)(2,1)S(1)}, u32[]{:S(2)}, u32[]{:S(2)}) collective-permute-start(bf16[7,96,384]{2,1,0:T(8,128)(2,1)} %get-tuple-element.86), channel_id=1, source_target_pairs={{8,0},{16,8},{24,16},{9,1},{17,9},{25,17},{10,2},{18,10},{26,18},{... | collective-permute-start | bytes 1548296 | tf_op jit(solution)/shard_map/ppermute | solution.py:20
  4.3 7.6 %collective-permute-start = (bf16[7,96,384]{2,1,0:T(8,128)(2,1)}, bf16[7,96,384]{2,1,0:T(8,128)(2,1)S(1)}, u32[]{:S(2)}, u32[]{:S(2)}) collective-permute-start(bf16[7,96,384]{2,1,0:T(8,128)(2,1)} %get-tuple-element.87), channel_id=1, source_target_pairs={{0,8},{8,16},{16,24},{1,9},{9,17},{17,25},{2,10},{10,18},{18,26},{... | collective-permute-start | bytes 1548296 | tf_op jit(solution)/shard_map/ppermute | solution.py:20
  11.9 11.4 %copy-start.6 = (bf16[384,1536]{1,0:T(8,128)(2,1)S(1)}, bf16[384,1536]{1,0:T(8,128)(2,1)}, u32[]{:S(2)}) copy-start(bf16[384,1536]{1,0:T(8,128)(2,1)} %w_in_ref.1) | copy-start | bytes 3538948
  11.9 25.7 %copy-start = (bf16[7,96,384]{2,1,0:T(8,128)(2,1)}, bf16[7,96,384]{2,1,0:T(8,128)(2,1)S(1)}, u32[]{:S(2)}) copy-start(bf16[7,96,384]{2,1,0:T(8,128)(2,1)S(1)} %collective-permute-done.1.below.image_below) | copy-start | bytes 1548292
  11.9 25.7 %copy-start.1 = (bf16[7,96,384]{2,1,0:T(8,128)(2,1)}, bf16[7,96,384]{2,1,0:T(8,128)(2,1)S(1)}, u32[]{:S(2)}) copy-start(bf16[7,96,384]{2,1,0:T(8,128)(2,1)S(1)} %collective-permute-done.above.image_above) | copy-start | bytes 1548292
  12.8 24.8 %collective-permute-start.2 = (bf16[78,8,384]{2,1,0:T(8,128)(2,1)}, bf16[78,8,384]{2,1,0:T(8,128)(2,1)S(1)}, u32[]{:S(2)}, u32[]{:S(2)}) collective-permute-start(bf16[78,8,384]{2,1,0:T(8,128)(2,1)} %pad_maximum_fusion), channel_id=1, source_target_pairs={{0,1},{1,2},{2,3},{3,4},{4,5},{5,6},{6,7},{8,9},{9,10},{10,11},{11... | collective-permute-start | bytes 1437704 | tf_op jit(solution)/shard_map/ppermute | solution.py:20
  18.6 19.0 %collective-permute-start.3 = (bf16[78,8,384]{2,1,0:T(8,128)(2,1)}, bf16[78,8,384]{2,1,0:T(8,128)(2,1)S(1)}, u32[]{:S(2)}, u32[]{:S(2)}) collective-permute-start(bf16[78,8,384]{2,1,0:T(8,128)(2,1)} %pad_maximum_fusion.1), channel_id=1, source_target_pairs={{1,0},{2,1},{3,2},{4,3},{5,4},{6,5},{7,6},{9,8},{10,9},{11,10},{12... | collective-permute-start | bytes 1437704 | tf_op jit(solution)/shard_map/ppermute | solution.py:20
  20.7 16.9 %copy-start.3 = (s32[960]{0:T(1024)}, s32[960]{0:T(1024)S(1)}, u32[]{:S(2)}) copy-start(s32[960]{0:T(1024)S(1)} %reshape.102.source_ref) | copy-start | bytes 11524
  20.8 4.6 %copy-start.12 = (f32[2,384]{1,0:T(2,128)}, f32[2,384]{1,0:T(2,128)S(1)}, u32[]{:S(2)}) copy-start(f32[2,384]{1,0:T(2,128)S(1)} %exp.11.step_ref) | copy-start | bytes 9220
  20.8 16.8 %copy-start.4 = (f32[1,384]{1,0:T(1,128)}, f32[1,384]{1,0:T(1,128)S(1)}, u32[]{:S(2)}) copy-start(f32[1,384]{1,0:T(1,128)S(1)} %broadcast_in_dim.14.skip_ref) | copy-start | bytes 4612
  20.8 3.9 %copy-start.13 = (f32[1536]{0:T(1024)S(1)}, f32[1536]{0:T(1024)}, u32[]{:S(2)}) copy-start(f32[1536]{0:T(1024)} %param.27) | copy-start | bytes 18436
  20.8 4.5 %copy-start.16 = (f32[384]{0:T(512)S(1)}, f32[384]{0:T(512)}, u32[]{:S(2)}) copy-start(f32[384]{0:T(512)} %param.30) | copy-start | bytes 4612
  20.8 4.5 %copy-start.17 = (f32[384]{0:T(512)S(1)}, f32[384]{0:T(512)}, u32[]{:S(2)}) copy-start(f32[384]{0:T(512)} %param.29) | copy-start | bytes 4612
  20.8 4.5 %copy-start.18 = (f32[384]{0:T(512)S(1)}, f32[384]{0:T(512)}, u32[]{:S(2)}) copy-start(f32[384]{0:T(512)} %param.25) | copy-start | bytes 4612
  20.9 4.5 %copy-start.19 = (f32[384]{0:T(512)S(1)}, f32[384]{0:T(512)}, u32[]{:S(2)}) copy-start(f32[384]{0:T(512)} %param.24) | copy-start | bytes 4612
  20.9 4.5 %copy-start.9 = (f32[2,384,32]{1,2,0:T(8,128)S(1)}, f32[2,384,32]{1,2,0:T(8,128)}, u32[]{:S(2)}) copy-start(f32[2,384,32]{1,2,0:T(8,128)} %param.19) | copy-start | bytes 294916
  20.9 4.5 %copy-start.10 = (f32[2,384,32]{1,2,0:T(8,128)S(1)}, f32[2,384,32]{1,2,0:T(8,128)}, u32[]{:S(2)}) copy-start(f32[2,384,32]{1,2,0:T(8,128)} %param.18) | copy-start | bytes 294916
  37.6 0.8 copy-start.2
  149.4 6.2 %copy-start.5 = (bf16[768,1536]{1,0:T(8,128)(2,1)S(1)}, bf16[768,1536]{1,0:T(8,128)(2,1)}, u32[]{:S(2)}) copy-start(bf16[768,1536]{1,0:T(8,128)(2,1)} %get-tuple-element.42) | copy-start | bytes 7077892
  150.9 4.7 %collective-permute-start.13 = (bf16[384,1536]{1,0:T(8,128)(2,1)S(1)}, bf16[384,1536]{1,0:T(8,128)(2,1)}, u32[]{:S(2)}, u32[]{:S(2)}) collective-permute-start(bf16[384,1536]{1,0:T(8,128)(2,1)S(1)} %constant_dynamic-slice_fusion.4), channel_id=1, source_target_pairs={{0,8},{8,0},{16,24},{24,16},{1,9},{9,1},{17,25},{25,17},{2,10},{10... | collective-permute-start | bytes 3538952 | tf_op jit(solution)/shard_map/ppermute | solution.py:25
  157.2 15.7 %collective-permute-start.14 = (bf16[192,1536]{1,0:T(8,128)(2,1)S(1)}, bf16[192,1536]{1,0:T(8,128)(2,1)S(1)}, u32[]{:S(2)}, u32[]{:S(2)}) collective-permute-start(bf16[192,1536]{1,0:T(8,128)(2,1)S(1)} %constant_dynamic-slice_fusion.3), channel_id=1, source_target_pairs={{0,16},{8,24},{16,0},{24,8},{1,17},{9,25},{17,1},{25,9},{2,18},{10... | collective-permute-start | bytes 1769480 | tf_op jit(solution)/shard_map/ppermute | solution.py:25
  173.1 8.9 %collective-permute-start.15 = (bf16[96,1536]{1,0:T(8,128)(2,1)S(1)}, bf16[96,1536]{1,0:T(8,128)(2,1)S(1)}, u32[]{:S(2)}, u32[]{:S(2)}) collective-permute-start(bf16[96,1536]{1,0:T(8,128)(2,1)S(1)} %constant_dynamic-slice_fusion.2), channel_id=1, source_target_pairs={{0,1},{1,0},{2,3},{3,2},{4,5},{5,4},{6,7},{7,6},{8,9},{9,8},{10,11... | collective-permute-start | bytes 884744 | tf_op jit(solution)/shard_map/ppermute | solution.py:25
  182.1 5.9 %collective-permute-start.16 = (bf16[48,1536]{1,0:T(8,128)(2,1)S(1)}, bf16[48,1536]{1,0:T(8,128)(2,1)S(1)}, u32[]{:S(2)}, u32[]{:S(2)}) collective-permute-start(bf16[48,1536]{1,0:T(8,128)(2,1)S(1)} %constant_dynamic-slice_fusion.1), channel_id=1, source_target_pairs={{0,2},{1,3},{2,0},{3,1},{4,6},{5,7},{6,4},{7,5},{8,10},{9,11},{10,... | collective-permute-start | bytes 442376 | tf_op jit(solution)/shard_map/ppermute | solution.py:25
  188.1 5.6 %collective-permute-start.17 = (bf16[24,1536]{1,0:T(8,128)(2,1)S(1)}, bf16[24,1536]{1,0:T(8,128)(2,1)S(1)}, u32[]{:S(2)}, u32[]{:S(2)}) collective-permute-start(bf16[24,1536]{1,0:T(8,128)(2,1)S(1)} %constant_dynamic-slice_fusion), channel_id=1, source_target_pairs={{0,4},{1,5},{2,6},{3,7},{4,0},{5,1},{6,2},{7,3},{8,12},{9,13},{10,... | collective-permute-start | bytes 221192 | tf_op jit(solution)/shard_map/ppermute | solution.py:25
  193.7 6.0 %collective-permute-start.18 = (bf16[24,1536]{1,0:T(8,128)(2,1)S(1)}, bf16[24,1536]{1,0:T(8,128)(2,1)S(1)}, u32[]{:S(2)}, u32[]{:S(2)}) collective-permute-start(bf16[24,1536]{1,0:T(8,128)(2,1)S(1)} %add_convert_fusion.4), channel_id=1, source_target_pairs={{0,4},{1,5},{2,6},{3,7},{4,0},{5,1},{6,2},{7,3},{8,12},{9,13},{10,... | collective-permute-start | bytes 221192 | tf_op jit(solution)/shard_map/ppermute | solution.py:25
  199.8 6.8 %collective-permute-start.19 = (bf16[48,1536]{1,0:T(8,128)(2,1)S(1)}, bf16[48,1536]{1,0:T(8,128)(2,1)S(1)}, u32[]{:S(2)}, u32[]{:S(2)}) collective-permute-start(bf16[48,1536]{1,0:T(8,128)(2,1)S(1)} %maximum_select_fusion.4), channel_id=1, source_target_pairs={{0,2},{1,3},{2,0},{3,1},{4,6},{5,7},{6,4},{7,5},{8,10},{9,11},{10,... | collective-permute-start | bytes 442376 | tf_op jit(solution)/shard_map/ppermute | solution.py:25
  206.7 7.1 %collective-permute-start.20 = (bf16[96,1536]{1,0:T(8,128)(2,1)S(1)}, bf16[96,1536]{1,0:T(8,128)(2,1)S(1)}, u32[]{:S(2)}, u32[]{:S(2)}) collective-permute-start(bf16[96,1536]{1,0:T(8,128)(2,1)S(1)} %maximum_select_fusion.3), channel_id=1, source_target_pairs={{0,1},{1,0},{2,3},{3,2},{4,5},{5,4},{6,7},{7,6},{8,9},{9,8},{10,11... | collective-permute-start | bytes 884744 | tf_op jit(solution)/shard_map/ppermute | solution.py:25
  208.2 6.3 %collective-permute-start.5 = (bf16[7,96,384]{2,1,0:T(8,128)(2,1)S(1)}, bf16[7,96,384]{2,1,0:T(8,128)(2,1)S(1)}, u32[]{:S(2)}, u32[]{:S(2)}) collective-permute-start(bf16[7,96,384]{2,1,0:T(8,128)(2,1)S(1)} %bitcast.32), channel_id=1, source_target_pairs={{8,0},{16,8},{24,16},{9,1},{17,9},{25,17},{10,2},{18,10},{26,18},{... | collective-permute-start | bytes 1548296 | tf_op jit(solution)/shard_map/ppermute | solution.py:20
  209.5 5.0 %collective-permute-start.4 = (bf16[7,96,384]{2,1,0:T(8,128)(2,1)S(1)}, bf16[7,96,384]{2,1,0:T(8,128)(2,1)S(1)}, u32[]{:S(2)}, u32[]{:S(2)}) collective-permute-start(bf16[7,96,384]{2,1,0:T(8,128)(2,1)S(1)} %bitcast.31), channel_id=1, source_target_pairs={{0,8},{8,16},{16,24},{1,9},{9,17},{17,25},{2,10},{10,18},{18,26},{... | collective-permute-start | bytes 1548296 | tf_op jit(solution)/shard_map/ppermute | solution.py:20
  213.9 18.8 %copy-start.11 = (f32[4,8,384]{2,1,0:T(8,128)S(1)}, f32[4,8,384]{2,1,0:T(8,128)}, u32[]{:S(2)}) copy-start(f32[4,8,384]{2,1,0:T(8,128)} %get-tuple-element.35) | copy-start | bytes 147460
  213.9 16.4 %collective-permute-start.21 = (bf16[192,1536]{1,0:T(8,128)(2,1)S(1)}, bf16[192,1536]{1,0:T(8,128)(2,1)S(1)}, u32[]{:S(2)}, u32[]{:S(2)}) collective-permute-start(bf16[192,1536]{1,0:T(8,128)(2,1)S(1)} %maximum_select_fusion.2), channel_id=1, source_target_pairs={{0,16},{8,24},{16,0},{24,8},{1,17},{9,25},{17,1},{25,9},{2,18},{10... | collective-permute-start | bytes 1769480 | tf_op jit(solution)/shard_map/ppermute | solution.py:25
  214.5 18.2 %copy-start.7 = (bf16[7,96,384]{2,1,0:T(8,128)(2,1)}, bf16[7,96,384]{2,1,0:T(8,128)(2,1)S(1)}, u32[]{:S(2)}) copy-start(bf16[7,96,384]{2,1,0:T(8,128)(2,1)S(1)} %collective-permute-done.5.below) | copy-start | bytes 1548292
  214.5 18.2 %copy-start.8 = (bf16[7,96,384]{2,1,0:T(8,128)(2,1)}, bf16[7,96,384]{2,1,0:T(8,128)(2,1)S(1)}, u32[]{:S(2)}) copy-start(bf16[7,96,384]{2,1,0:T(8,128)(2,1)S(1)} %collective-permute-done.4.above) | copy-start | bytes 1548292
  215.5 17.2 %collective-permute-start.6 = (bf16[78,8,384]{2,1,0:T(8,128)(2,1)}, bf16[78,8,384]{2,1,0:T(8,128)(2,1)}, u32[]{:S(2)}, u32[]{:S(2)}) collective-permute-start(bf16[78,8,384]{2,1,0:T(8,128)(2,1)} %pad_maximum_fusion.2), channel_id=1, source_target_pairs={{0,1},{1,2},{2,3},{3,4},{4,5},{5,6},{6,7},{8,9},{9,10},{10,11},{11... | collective-permute-start | bytes 1437704 | tf_op jit(solution)/shard_map/ppermute | solution.py:20
  220.9 11.8 %collective-permute-start.7 = (bf16[78,8,384]{2,1,0:T(8,128)(2,1)}, bf16[78,8,384]{2,1,0:T(8,128)(2,1)}, u32[]{:S(2)}, u32[]{:S(2)}) collective-permute-start(bf16[78,8,384]{2,1,0:T(8,128)(2,1)} %pad_maximum_fusion.3), channel_id=1, source_target_pairs={{1,0},{2,1},{3,2},{4,3},{5,4},{6,5},{7,6},{9,8},{10,9},{11,10},{12... | collective-permute-start | bytes 1437704 | tf_op jit(solution)/shard_map/ppermute | solution.py:20
  230.7 99.1 %collective-permute-start.22 = (bf16[384,1536]{1,0:T(8,128)(2,1)S(1)}, bf16[384,1536]{1,0:T(8,128)(2,1)S(1)}, u32[]{:S(2)}, u32[]{:S(2)}) collective-permute-start(bf16[384,1536]{1,0:T(8,128)(2,1)S(1)} %maximum_select_fusion.1), channel_id=1, source_target_pairs={{0,8},{8,0},{16,24},{24,16},{1,9},{9,1},{17,25},{25,17},{2,10},{10... | collective-permute-start | bytes 3538952 | tf_op jit(solution)/shard_map/ppermute | solution.py:25
  295.8 9.6 %collective-permute-start.8 = (f32[40,384]{1,0:T(8,128)S(1)}, f32[40,384]{1,0:T(8,128)S(1)}, u32[]{:S(2)}, u32[]{:S(2)}) collective-permute-start(f32[40,384]{1,0:T(8,128)S(1)} %pad_maximum_fusion.4), channel_id=1, source_target_pairs={{0,8},{8,0},{16,24},{24,16},{1,9},{9,1},{17,25},{25,17},{2,10},{10... | collective-permute-start | bytes 184328 | tf_op jit(solution)/shard_map/ppermute | solution.py:25
  306.3 4.3 %collective-permute-start.9 = (f32[40,384]{1,0:T(8,128)S(1)}, f32[40,384]{1,0:T(8,128)S(1)}, u32[]{:S(2)}, u32[]{:S(2)}) collective-permute-start(f32[40,384]{1,0:T(8,128)S(1)} %fusion.4), channel_id=1, source_target_pairs={{0,16},{8,24},{16,0},{24,8},{1,17},{9,25},{17,1},{25,9},{2,18},{10... | collective-permute-start | bytes 184328 | tf_op jit(solution)/shard_map/ppermute | solution.py:25
  310.6 4.5 %collective-permute-start.10 = (f32[40,384]{1,0:T(8,128)S(1)}, f32[40,384]{1,0:T(8,128)S(1)}, u32[]{:S(2)}, u32[]{:S(2)}) collective-permute-start(f32[40,384]{1,0:T(8,128)S(1)} %add.144), channel_id=1, source_target_pairs={{0,1},{1,0},{2,3},{3,2},{4,5},{5,4},{6,7},{7,6},{8,9},{9,8},{10,11... | collective-permute-start | bytes 184328 | tf_op jit(solution)/shard_map/ppermute | solution.py:25
  315.1 5.2 %collective-permute-start.11 = (f32[40,384]{1,0:T(8,128)S(1)}, f32[40,384]{1,0:T(8,128)S(1)}, u32[]{:S(2)}, u32[]{:S(2)}) collective-permute-start(f32[40,384]{1,0:T(8,128)S(1)} %add.145), channel_id=1, source_target_pairs={{0,2},{1,3},{2,0},{3,1},{4,6},{5,7},{6,4},{7,5},{8,10},{9,11},{10,... | collective-permute-start | bytes 184328 | tf_op jit(solution)/shard_map/ppermute | solution.py:25
  320.2 5.2 %collective-permute-start.12 = (f32[40,384]{1,0:T(8,128)S(1)}, f32[40,384]{1,0:T(8,128)S(1)}, u32[]{:S(2)}, u32[]{:S(2)}) collective-permute-start(f32[40,384]{1,0:T(8,128)S(1)} %add.146), channel_id=1, source_target_pairs={{0,4},{1,5},{2,6},{3,7},{4,0},{5,1},{6,2},{7,3},{8,12},{9,13},{10,... | collective-permute-start | bytes 184328 | tf_op jit(solution)/shard_map/ppermute | solution.py:25

commit v2 on v1

v2 whole, which is shorter than its diff:
```python
import jax
import jax.numpy as jnp
import ml_dtypes
import numpy as np
from jax import lax
from jax.experimental import pallas as pl
from jax.experimental.pallas import tpu as pltpu
from jax.sharding import PartitionSpec as P

KSIZE = 15
REACH = KSIZE // 2
EDGE = 8
LANES = 128
GROUP = 8
MIB = 2**20
F32, BF16 = jnp.float32, jnp.bfloat16


def swap(block, axis, bit):
    count = lax.axis_size(axis)
    return lax.ppermute(block, axis, [(i, i ^ bit) for i in range(count)])


def swap_across(block, axis):
    count = lax.axis_size(axis)
    pairs = [(i, i + 1) for i in range(1, count - 1, 2)]
    return lax.ppermute(block, axis, pairs + [(j, i) for i, j in pairs])


def tie(value, *others):
    return lax.optimization_barrier((value, *others))[0]


def halo_rows(block):
    place = lax.axis_index("th") % 2
    far = block.shape[0] - REACH
    near = swap(lax.dynamic_slice_in_dim(block, (1 - place) * far, REACH, 0), "th", 1)
    other = swap_across(lax.dynamic_slice_in_dim(block, place * far, REACH, 0), "th")
    return near, other


def halo_cols(block, near, other):
    place = lax.axis_index("tw") % 2
    far = block.shape[1] - EDGE

    def edge(at):
        return jnp.concatenate(
            [lax.dynamic_slice_in_dim(v, at * far, EDGE, 1) for v in (block, near, other)], axis=0
        )

    edges = edge(1 - place), edge(place)
    return swap(edges[0], "tw", 1), swap_across(edges[1], "tw"), edges


def two_parts(matrix):
    high = matrix.astype(ml_dtypes.bfloat16)
    low = (matrix - high.astype(np.float64)).astype(ml_dtypes.bfloat16)
    return np.concatenate([high, low], axis=1)


def transforms(width):
    size = width + 2 * EDGE
    half = size // 2
    place = np.concatenate([EDGE + np.arange(width), np.arange(EDGE), EDGE + width + np.arange(EDGE)])
    freq = np.arange(half)[:, None]

    def angle(n):
        return 2 * np.pi * ((freq * n[None, :]) % size) / size

    lower = -np.sin(angle(place))
    lower[0] = np.cos(np.pi * place)
    forward = np.concatenate([np.cos(angle(place)), lower])
    swapped = np.concatenate([forward[:, :width], forward[:, width + EDGE :], forward[:, width : width + EDGE]], axis=1)

    def back(n):
        real = 2 * np.cos(angle(n)) / size
        imag = -2 * np.sin(angle(n)) / size
        real[0] = 1 / size
        imag[0] = np.cos(np.pi * n) / size
        return np.concatenate([real, imag]).T

    ahead = back(1 + np.arange(width))
    behind = back(KSIZE + np.arange(width))
    lag = np.arange(KSIZE) - REACH
    real, high, imag = (np.zeros((KSIZE + 1, half)) for _ in range(3))
    real[:KSIZE] = (2 * np.cos(angle(lag)) / size).T
    high[:KSIZE] = real[:KSIZE]
    imag[:KSIZE] = (-2 * np.sin(angle(lag)) / size).T
    real[:KSIZE, 0] = 1 / size
    high[:KSIZE, 0] = np.cos(np.pi * lag) / size
    imag[:KSIZE, 0] = 0
    lags = np.concatenate([real, high, imag], axis=1).astype(np.float32)
    tap = np.arange(KSIZE + 1)
    real = np.cos(angle(tap))
    imag = np.sin(angle(tap))
    high = real.copy()
    high[0] = np.cos(np.pi * tap)
    response = np.concatenate([real, imag, high]).astype(np.float32)
    return (
        two_parts(forward), two_parts(swapped), two_parts(forward[:, :width]), two_parts(ahead), two_parts(behind),
        lags, response,
    )


def powers(rate, freq, log_step):
    step = jnp.exp(log_step)
    decay = jnp.exp(-jnp.exp(rate) * step)
    phase = freq * step
    return decay * jnp.cos(phase), decay * jnp.sin(phase), step


def dot(a, b, precision=None):
    return lax.dot_general(
        a, b, (((1,), (0,)), ((), ())), precision=precision, preferred_element_type=F32
    )


def taps_kernel(zr_ref, zi_ref, cr_ref, ci_ref, response_ref, taps_ref, factor_ref):
    half = factor_ref.shape[1]
    for d in range(2):
        zr, zi = zr_ref[d], zi_ref[d]
        cr, ci = cr_ref[d], ci_ref[d]
        ur, ui = jnp.ones_like(zr), jnp.zeros_like(zr)
        for m in range(KSIZE):
            taps_ref[d, m] = 2.0 * jnp.sum(cr * ur - ci * ui, axis=0)
            ur, ui = ur * zr - ui * zi, ur * zi + ui * zr
        taps_ref[d, KSIZE] = jnp.zeros_like(taps_ref[d, KSIZE])
    factor = dot(response_ref[...], taps_ref[1], lax.Precision.HIGHEST)
    for k in range(3):
        factor_ref[k] = factor[k * half : (k + 1) * half]


def taps_grad_kernel(
    zr_ref, zi_ref, cr_ref, ci_ref, rate_ref, freq_ref, step_ref, g_ref,
    d_rate_ref, d_freq_ref, d_cr_ref, d_ci_ref, d_step_ref,
):
    for d in range(2):
        zr, zi = zr_ref[d], zi_ref[d]
        cr, ci = cr_ref[d], ci_ref[d]
        ur, ui = jnp.ones_like(zr), jnp.zeros_like(zr)
        su, sv = jnp.zeros_like(zr), jnp.zeros_like(zr)
        mu, mv = jnp.zeros_like(zr), jnp.zeros_like(zr)
        for m in range(KSIZE):
            g = 2.0 * g_ref[d * (KSIZE + 1) + m][None, :]
            gu, gv = g * ur, g * ui
            su, sv = su + gu, sv + gv
            if m:
                mu, mv = mu + float(m) * gu, mv + float(m) * gv
            ur, ui = ur * zr - ui * zi, ur * zi + ui * zr
        step = step_ref[d][None, :]
        freq = freq_ref[d]
        d_freq = -step * (cr * mv + ci * mu)
        d_rate = -jnp.exp(rate_ref[d]) * step * (cr * mu - ci * mv)
        d_cr_ref[d] = su
        d_ci_ref[d] = -sv
        d_freq_ref[d] = d_freq
        d_rate_ref[d] = d_rate
        d_step_ref[d] = jnp.sum(d_rate + freq * d_freq, axis=0)


def load_rows(ext, source_ref, centre, near, other):
    height = centre.shape[0]
    ext[height + 2 * REACH] = jnp.zeros(ext.shape[1:], F32)
    for i in range(REACH):
        ext[source_ref[height * KSIZE] + i] = near[i].astype(F32)
        ext[source_ref[height * KSIZE + 1] + i] = other[i].astype(F32)

    def row(r, _):
        for k in range(4):
            ext[4 * r + k + REACH] = centre[4 * r + k].astype(F32)
        return 0

    lax.fori_loop(0, height // 4, row, 0)


def fold(v):
    return jnp.sum(v.reshape(v.shape[0] // 8, 8, v.shape[1]), axis=0)


def rows_kernel(source_ref, taps_ref, centre, near, other, partial_ref, ext):
    height = centre.shape[0]
    load_rows(ext, source_ref, centre, near, other)
    taps = [taps_ref[0, i][None, :] for i in range(KSIZE)]

    def row(r, _):
        for k in range(2):
            at = 2 * r + k
            total = taps[0] * ext[source_ref[at * KSIZE]]
            for i in range(1, KSIZE):
                total = total + taps[i] * ext[source_ref[at * KSIZE + i]]
            partial_ref[at] = total.astype(BF16)
        return 0

    lax.fori_loop(0, height // 2, row, 0)


def twice(v):
    return jnp.concatenate([v, v], axis=0)


def filtered(spectrum, factor, conjugate):
    half = factor[0].shape[0]
    real, imag = spectrum[:half], spectrum[half:]
    a, b, top = factor
    cross = b * imag
    across = b * real
    if conjugate:
        return jnp.concatenate([a * real + cross, top * imag - across], axis=0).astype(BF16)
    return jnp.concatenate([a * real - cross, top * imag + across], axis=0).astype(BF16)


def cols_kernel(
    source_ref, taps_ref, skip_ref, factor_ref, forward_ref, ahead_ref,
    partial_ref, image_ref, near, other,
    mixed_ref, spectrum_ref, sides, side_partial,
):
    step = pl.program_id(0)
    full = near.shape[0]
    height = full - 2 * REACH

    @pl.when(step == 0)
    def _():
        sides[full] = jnp.zeros(sides.shape[1:], F32)
        for part, at in ((near, 0), (other, EDGE)):
            for i in range(2 * REACH):
                base = source_ref[height * KSIZE + i // REACH] + i % REACH
                sides[base, at : at + EDGE] = part[height + i].astype(F32)

            def place(r, _):
                sides[r + REACH, at : at + EDGE] = part[r].astype(F32)
                return 0

            lax.fori_loop(0, height, place, 0)

        taps = [taps_ref[0, i][None, :] for i in range(KSIZE)]

        def row(r, _):
            total = taps[0] * sides[source_ref[r * KSIZE]]
            for i in range(1, KSIZE):
                total = total + taps[i] * sides[source_ref[r * KSIZE + i]]
            side_partial[r] = total.astype(BF16)
            return 0

        lax.fori_loop(0, height, row, 0)

    factor = [factor_ref[k] for k in range(3)]
    skip = skip_ref[...]
    for k in range(GROUP):
        line = jnp.concatenate([partial_ref[k], side_partial[step * GROUP + k]], axis=0)
        spectrum = dot(forward_ref[...], twice(line))
        spectrum_ref[k] = spectrum.astype(BF16)
        mixed = dot(ahead_ref[...], twice(filtered(spectrum, factor, False)))
        mixed_ref[k] = mixed + skip * image_ref[k].astype(F32)


def cols_grad_kernel(
    own_ref, lags_ref, d_mixed_ref, spectrum_ref, image_ref, sums_ref, totals, skip_total
):
    step = pl.program_id(0)
    half = totals.shape[1]

    @pl.when(step == 0)
    def _():
        totals[...] = jnp.zeros(totals.shape, F32)
        skip_total[...] = jnp.zeros(skip_total.shape, F32)

    for k in range(GROUP):
        d = d_mixed_ref[k]
        spectrum = dot(own_ref[...], twice(d))
        real, imag = spectrum[:half], spectrum[half:]
        other = spectrum_ref[k].astype(F32)
        other_real, other_imag = other[:half], other[half:]
        totals[0] += real * other_real
        totals[1] += imag * other_imag
        totals[2] += real * other_imag - imag * other_real
        skip_total[...] += fold(d.astype(F32) * image_ref[k].astype(F32))

    @pl.when(step == pl.num_programs(0) - 1)
    def _():
        both = jnp.concatenate([totals[0], totals[1], totals[2]], axis=0)
        sums_ref[...] = dot(lags_ref[...], both, lax.Precision.HIGHEST)
        sums_ref[KSIZE : KSIZE + 1] = jnp.sum(skip_total[...], axis=0, keepdims=True)


def cols_back_kernel(
    source_ref, factor_ref, forward_ref, behind_ref,
    centre, row_near, row_other, col_near, col_other, image, image_near, image_other,
    d_partial_ref, sums_ref, ext, d_partial, row_sums,
):
    height, width = centre.shape[0], centre.shape[1]
    load_rows(ext, source_ref, image, image_near, image_other)
    batch = 4
    factor = [jnp.concatenate([factor_ref[k]] * batch, axis=1) for k in range(3)]
    row_sums[...] = jnp.zeros(row_sums.shape, F32)

    def line(own, one, two):
        both = jnp.concatenate([one.astype(F32), two.astype(F32)], axis=0).astype(BF16)
        return jnp.concatenate([own, both], axis=0)

    def transformed(lines):
        spectrum = dot(forward_ref[...], twice(jnp.concatenate(lines, axis=1)))
        some = [f[:, : spectrum.shape[1]] for f in factor]
        return dot(behind_ref[...], twice(filtered(spectrum, some, True)))

    def group(g):
        found = transformed(
            [line(centre[r], col_near[r], col_other[r]) for r in (batch * g + k for k in range(batch))]
        )
        for k in range(batch):
            row = found[:, k * LANES : (k + 1) * LANES]
            d_partial[batch * g + k] = row
            d_partial_ref[REACH + batch * g + k] = row.astype(BF16)

    def grads(g):
        for k in range(batch):
            r = batch * g + k
            d = d_partial[r]
            for i in range(KSIZE):
                row_sums[i] += fold(d * ext[source_ref[r * KSIZE + i]])

    group(0)

    def both(g, _):
        group(g)
        grads(g - 1)
        return 0

    lax.fori_loop(1, height // batch, both, 0)
    grads(height // batch - 1)
    for n, rows in enumerate((row_near, row_other)):
        to = source_ref[height * KSIZE + n]
        base = height + n * REACH
        for at in range(0, REACH, batch):
            some = range(at, min(at + batch, REACH))
            found = transformed([line(rows[i], col_near[base + i], col_other[base + i]) for i in some])
            for k, i in enumerate(some):
                d_partial_ref[to + i] = found[:, k * LANES : (k + 1) * LANES].astype(BF16)
    sums_ref[0:KSIZE] = jnp.sum(row_sums[...], axis=1)
    sums_ref[KSIZE : KSIZE + 1] = jnp.zeros((1, LANES), F32)


def rows_back_kernel(source_ref, taps_ref, skip_ref, d_partial_ref, d_mixed_ref, grad_ref, *rest):
    image_grad_ref, ext = rest[-2:]
    step = pl.program_id(0)
    count = d_mixed_ref.shape[0]
    full = d_partial_ref.shape[0]

    @pl.when(step == 0)
    def _():
        ext[full] = jnp.zeros(ext.shape[1:], F32)

        def place(r, _):
            for k in range(2):
                ext[2 * r + k] = d_partial_ref[2 * r + k].astype(F32)
            return 0

        lax.fori_loop(0, full // 2, place, 0)

    taps = [taps_ref[0, i][None, :] for i in range(KSIZE)]
    skip = skip_ref[...]

    def row(r, _):
        for k in range(2):
            at = 2 * r + k
            total = grad_ref[at].astype(F32) + skip * d_mixed_ref[at].astype(F32)
            for i in range(KSIZE):
                place = (step * count + at) * KSIZE + KSIZE - 1 - i
                total = total + taps[i] * ext[source_ref[place]]
            image_grad_ref[at] = total.astype(BF16)
        return 0

    lax.fori_loop(0, count // 2, row, 0)


def feed_kernel(
    mixed_ref, image_ref, grad_ref, w_in_ref, w_out_t_ref, w_in_t_ref, w_out_ref,
    b_in_ref, vectors_ref,
    output_ref, d_mixed_ref, weights_ref, b_sums_ref, sums_ref,
    act_ref, d_pre_ref,
):
    step = pl.program_id(0)
    chans, hidden = w_in_ref.shape
    piece = 512

    @pl.when(step == 0)
    def _():
        weights_ref[...] = jnp.zeros(weights_ref.shape, F32)
        b_sums_ref[...] = jnp.zeros(b_sums_ref.shape, F32)
        sums_ref[...] = jnp.zeros(sums_ref.shape, F32)

    gain, bias = vectors_ref[0:1], vectors_ref[1:2]
    b_out, scale = vectors_ref[2:3], vectors_ref[3:4]
    mixed = mixed_ref[...]
    mean = jnp.mean(mixed, axis=-1, keepdims=True)
    centred = mixed - mean
    var = jnp.mean(centred * centred, axis=-1, keepdims=True)
    inverse = lax.rsqrt(var + 1e-06)
    xhat = centred * inverse
    normed = (xhat * gain + bias).astype(BF16)
    grad = grad_ref[...].astype(F32)
    d_branch = (scale * grad).astype(BF16)
    normed_t = normed.T
    d_branch_t = d_branch.T
    ones = jnp.ones((8, normed.shape[0]), BF16)
    for k in range(0, hidden, piece):
        cut = slice(k, k + piece)
        pre = dot(normed, w_in_ref[:, cut]) + b_in_ref[:, cut]
        d_act = dot(d_branch, w_out_t_ref[:, cut])
        half = 0.5 + 0.5 * lax.erf(pre * 0.7071067811865476)
        bell = jnp.exp(pre * pre * -0.5) * 0.3989422804014327
        act = (pre * half).astype(BF16)
        d_pre = (d_act * (half + pre * bell)).astype(BF16)
        act_ref[:, cut] = act
        d_pre_ref[:, cut] = d_pre
        weights_ref[0:chans, cut] += dot(normed_t, d_pre)
        weights_ref[chans : 2 * chans, cut] += dot(d_branch_t, act)
        b_sums_ref[:, cut] += dot(ones, d_pre)
    branch = dot(act_ref[...], w_out_ref[...]) + b_out
    output_ref[...] = (image_ref[...].astype(F32) + scale * branch).astype(BF16)
    d_normed = dot(d_pre_ref[...], w_in_t_ref[...])
    g = d_normed * gain
    g_mean = jnp.mean(g, axis=-1, keepdims=True)
    g_xhat = jnp.mean(g * xhat, axis=-1, keepdims=True)
    d_mixed_ref[...] = ((g - g_mean - xhat * g_xhat) * inverse).astype(BF16)
    sums_ref[0] += fold(d_normed * xhat)
    sums_ref[1] += fold(d_normed)
    sums_ref[2] += fold(d_branch.astype(F32))
    sums_ref[3] += fold(grad * branch)


def whole(shape):
    return pl.BlockSpec(shape, lambda *_: (0,) * len(shape))


def lane_block(*lead):
    return pl.BlockSpec((*lead, LANES), lambda c: (0,) * len(lead) + (c,))


def row_block(*rest):
    return pl.BlockSpec((GROUP, *rest), lambda r: (r,) + (0,) * len(rest))


SCALARS = pl.BlockSpec(memory_space=pltpu.SMEM)


def params():
    return pltpu.CompilerParams(vmem_limit_bytes=60 * MIB)


def cost(us):
    return pl.CostEstimate(flops=int(us * 1e8), bytes_accessed=int(us * 1e5), transcendentals=0)


def mesh_steps():
    def bits(axis):
        return [(axis, 1 << k) for k in range(lax.axis_size(axis).bit_length() - 1)]

    (core, *high), low = bits("th"), bits("tw")
    mixed = [step for pair in zip(high, low) for step in pair]
    return [core] + mixed + high[len(low) :] + low[len(high) :]


def swap_two(block, first, second):
    if first[0] == second[0]:
        return swap(block, first[0], first[1] + second[1])
    bits = dict([first, second])
    high, low = lax.axis_size("th"), lax.axis_size("tw")
    pairs = [
        (i * low + j, (i ^ bits["th"]) * low + (j ^ bits["tw"])) for i in range(high) for j in range(low)
    ]
    return lax.ppermute(block, ("th", "tw"), pairs)


def place_in(steps):
    place = 0
    for n, (axis, bit) in enumerate(steps):
        place = place + lax.rem(lax.axis_index(axis) // bit, 2) * (1 << n)
    return place


def exchanges(steps):
    if len(steps) == 1:
        return [lambda v: swap(v, *steps[0])]
    return [lambda v: swap(v, *steps[0]), lambda v: swap(v, *steps[1]), lambda v: swap_two(v, *steps)]


def scatter(block, steps, kind, beside):
    place = place_in(steps)
    count = 1 << len(steps)
    size = block.shape[0] // count
    total = lax.dynamic_slice_in_dim(block, place * size, size, 0)
    gives = [
        lax.dynamic_slice_in_dim(block, (place ^ k) * size, size, 0).astype(kind) for k in range(1, count)
    ]
    takes = [send(give) for send, give in zip(exchanges(steps), gives)]
    done = beside(gives)
    for take in takes:
        total = total + tie(take, *done).astype(F32)
    return total


def gather(block, steps, beside):
    place = place_in(steps)
    takes = [send(block) for send in exchanges(steps)]
    done = beside([block])
    parts = [block] + [tie(take, *done) for take in takes]
    rows = []
    for q in range(len(parts)):
        found = parts[-1]
        for k in range(len(parts) - 1):
            found = jnp.where((place ^ q) == k, parts[k], found)
        rows.append(found)
    return jnp.concatenate(rows, axis=0)


def finish_kernel(side_ref, own_ref, other_ref, w_in_ref, w_out_ref):
    side = side_ref[0]

    @pl.when(side == 0)
    def _():
        w_in_ref[...] = own_ref[...].astype(F32)
        w_out_ref[...] = other_ref[...].astype(F32).T

    @pl.when(side == 1)
    def _():
        w_in_ref[...] = other_ref[...].astype(F32)
        w_out_ref[...] = own_ref[...].astype(F32).T


def per_device(
    image, image_heights, rate_log, freq, coef_re, coef_im, log_step, skip, ln_gain, ln_bias,
    w_in, b_in, w_out, b_out, layer_scale, out_grad,
):
    height, width, chans = image.shape
    hidden = w_in.shape[1]
    pixels = height * width
    full = height + 2 * REACH
    size = width + 2 * EDGE
    half = size // 2
    blocks = chans // LANES
    groups = height // GROUP
    straight, swapped, own, ahead, behind, lags, response = transforms(width)
    forward = jnp.where(lax.axis_index("tw") % 2 == 1, straight, swapped)

    row_near, row_other = halo_rows(image)
    col_near, col_other, _ = halo_cols(image, row_near, row_other)

    first, second = image_heights[0], image_heights[0] + image_heights[1]
    start = lax.axis_index("th") * height

    def ident(r):
        return (r >= first).astype(jnp.int32) + (r >= second).astype(jnp.int32)

    row = jnp.arange(height, dtype=jnp.int32)[:, None]
    tap = jnp.arange(KSIZE, dtype=jnp.int32)[None, :]
    source = jnp.where(
        ident(start + row) == ident(start + row + tap - REACH), row + tap, full
    ).reshape(-1)
    base = jnp.where(jnp.arange(2) == lax.axis_index("th") % 2, REACH + height, 0)
    source = jnp.concatenate([source, base.astype(jnp.int32)])

    rate_t, freq_t, cr_t, ci_t = (v.transpose(0, 2, 1) for v in (rate_log, freq, coef_re, coef_im))
    zr, zi, step = powers(rate_t, freq_t, log_step[:, None, :])
    step = step[:, 0]
    taps, factor = pl.pallas_call(
        taps_kernel,
        out_shape=[
            jax.ShapeDtypeStruct((2, KSIZE + 1, chans), F32),
            jax.ShapeDtypeStruct((3, half, chans), F32),
        ],
        name="taps",
    )(zr, zi, cr_t, ci_t, response)

    skip_row = skip[None, :]
    tile_shape = (height, width, chans)
    partial = pl.pallas_call(
        rows_kernel,
        grid=(blocks,),
        in_specs=[
            SCALARS, lane_block(2, KSIZE + 1), lane_block(height, width),
            lane_block(REACH, width), lane_block(REACH, width),
        ],
        out_specs=lane_block(height, width),
        out_shape=jax.ShapeDtypeStruct(tile_shape, BF16),
        scratch_shapes=[pltpu.VMEM((full + 1, width, LANES), F32)],
        compiler_params=params(),
        cost_estimate=cost(14),
        name="rows_forward",
    )(source, taps, image, row_near, row_other)

    mixed, spectrum = pl.pallas_call(
        cols_kernel,
        grid=(groups,),
        in_specs=[
            SCALARS, whole((2, KSIZE + 1, chans)), whole((1, chans)), whole((3, half, chans)),
            whole((size, 2 * size)), whole((width, 2 * size)),
            row_block(width, chans), row_block(width, chans),
            whole((full, EDGE, chans)), whole((full, EDGE, chans)),
        ],
        out_specs=[row_block(width, chans), row_block(size, chans)],
        out_shape=[
            jax.ShapeDtypeStruct(tile_shape, F32),
            jax.ShapeDtypeStruct((height, size, chans), BF16),
        ],
        scratch_shapes=[
            pltpu.VMEM((full + 1, 2 * EDGE, chans), F32),
            pltpu.VMEM((height, 2 * EDGE, chans), BF16),
        ],
        compiler_params=params(),
        cost_estimate=cost(14),
        name="cols_forward",
    )(
        source, taps, skip_row, factor, forward, ahead, partial, image,
        col_near, col_other,
    )

    tile = 768
    pixel_block = pl.BlockSpec((tile, chans), lambda i: (i, 0))
    vectors = jnp.stack([ln_gain, ln_bias, b_out, layer_scale])
    output, d_mixed, weights, b_sums, sums = pl.pallas_call(
        feed_kernel,
        grid=(pixels // tile,),
        in_specs=[
            pixel_block, pixel_block, pixel_block,
            whole((chans, hidden)), whole((chans, hidden)), whole((hidden, chans)), whole((hidden, chans)),
            whole((1, hidden)), whole((4, chans)),
        ],
        out_specs=[
            pixel_block, pixel_block, whole((2 * chans, hidden)), whole((8, hidden)), whole((4, 8, chans)),
        ],
        out_shape=[
            jax.ShapeDtypeStruct((pixels, chans), BF16),
            jax.ShapeDtypeStruct((pixels, chans), BF16),
            jax.ShapeDtypeStruct((2 * chans, hidden), F32),
            jax.ShapeDtypeStruct((8, hidden), F32),
            jax.ShapeDtypeStruct((4, 8, chans), F32),
        ],
        scratch_shapes=[pltpu.VMEM((tile, hidden), BF16), pltpu.VMEM((tile, hidden), BF16)],
        compiler_params=params(),
        cost_estimate=cost(70),
        name="feed_forward",
    )(
        mixed.reshape(pixels, chans), image.reshape(pixels, chans), out_grad.reshape(pixels, chans),
        w_in, w_out.T, w_in.T, w_out, b_in[None, :], vectors,
    )
    output = output.reshape(tile_shape)
    d_mixed = d_mixed.reshape(tile_shape)

    grad_row_near, grad_row_other = halo_rows(d_mixed)
    grad_col_near, grad_col_other, edges = halo_cols(d_mixed, grad_row_near, grad_row_other)

    core, *others = mesh_steps()
    phases = [others[k : k + 2] for k in range(0, len(others), 2)]
    found = []

    def cols_grad(sent):
        found.append(
            pl.pallas_call(
                cols_grad_kernel,
                grid=(groups,),
                in_specs=[
                    whole((size, 2 * width)), whole((KSIZE + 1, 3 * half)),
                    row_block(width, chans), row_block(size, chans), row_block(width, chans),
                ],
                out_specs=whole((KSIZE + 1, chans)),
                out_shape=jax.ShapeDtypeStruct((KSIZE + 1, chans), F32),
                scratch_shapes=[pltpu.VMEM((3, half, chans), F32), pltpu.VMEM((8, chans), F32)],
                compiler_params=params(),
                cost_estimate=cost(8),
                name="cols_grad",
            )(own, lags, tie(d_mixed, *sent, *edges), spectrum, image)
        )
        return []

    weights = scatter(weights, [core], F32, cols_grad)
    (col_sums,) = found

    def cols_back(sent):
        both = pl.pallas_call(
            cols_back_kernel,
            grid=(blocks,),
            in_specs=[
                SCALARS, lane_block(3, half), whole((size, 2 * size)), whole((width, 2 * size)),
                lane_block(height, width), lane_block(REACH, width), lane_block(REACH, width),
                lane_block(full, EDGE), lane_block(full, EDGE),
                lane_block(height, width), lane_block(REACH, width), lane_block(REACH, width),
            ],
            out_specs=[lane_block(full, width), lane_block(KSIZE + 1)],
            out_shape=[
                jax.ShapeDtypeStruct((full, width, chans), BF16),
                jax.ShapeDtypeStruct((KSIZE + 1, chans), F32),
            ],
            scratch_shapes=[
                pltpu.VMEM((full + 1, width, LANES), F32),
                pltpu.VMEM((height, width, LANES), F32),
                pltpu.VMEM((KSIZE, 8, LANES), F32),
            ],
            compiler_params=params(),
            cost_estimate=cost(20),
            name="cols_back",
        )(
            source, factor, forward, behind, tie(d_mixed, *sent), grad_row_near, grad_row_other,
            grad_col_near, grad_col_other, image, row_near, row_other,
        )
        found.extend(both)
        return both

    weights = scatter(weights, phases[0], BF16, cols_back)
    _, d_partial, row_sums = found

    small = jnp.concatenate(
        [row_sums, col_sums, jnp.sum(sums, axis=1), b_sums[0].reshape(hidden // chans, chans)], axis=0
    )

    def rows_back(block, before, *waits):
        at = pl.BlockSpec((height // 4, width, LANES), lambda r: (r, 0, block))
        lanes = lambda *lead: pl.BlockSpec((*lead, LANES), lambda r: (0,) * len(lead) + (block,))
        return pl.pallas_call(
            rows_back_kernel,
            grid=(4,),
            in_specs=[
                SCALARS, lanes(2, KSIZE + 1), lanes(1), lanes(full, width), at, at,
                *([] if before is None else [pl.BlockSpec(memory_space=pl.ANY)]),
            ],
            out_specs=at,
            out_shape=jax.ShapeDtypeStruct(tile_shape, BF16),
            scratch_shapes=[pltpu.VMEM((full + 1, width, LANES), F32)],
            compiler_params=params(),
            cost_estimate=cost(6),
            input_output_aliases={} if before is None else {6: 0},
            name="rows_back",
        )(
            source, taps, tie(skip_row, *waits), d_partial, d_mixed, out_grad,
            *([] if before is None else [before]),
        )

    small = small + swap(small, *core)
    waiting = list(phases)

    def beside(block, before):
        def work(sent):
            nonlocal small
            takes = []
            if waiting:
                takes = [send(small) for send in exchanges(waiting.pop(0))]
            some = rows_back(block, before, *sent, small)
            for take in takes:
                small = small + tie(take, some)
            found.append(some)
            return [some]

        return work

    for n, later in enumerate(phases[1:]):
        weights = scatter(weights, later, F32, beside(0, None) if n == 0 else lambda _: [])
    weights = weights.astype(BF16)
    for n, later in enumerate(reversed(phases[1:])):
        weights = gather(weights, later, beside(1, found[-1]) if n == 0 else lambda _: [])
    for later in waiting:
        small = sum([send(small) for send in exchanges(later)], small)
    waiting.clear()
    weights = gather(tie(weights, small), phases[0], beside(2, found[-1]))
    image_grad = found[-1]
    cut = hidden // 4
    half_block = pl.BlockSpec((chans, cut), lambda k: (0, k))
    d_win, d_wout = pl.pallas_call(
        finish_kernel,
        grid=(4,),
        in_specs=[SCALARS, half_block, half_block],
        out_specs=[half_block, pl.BlockSpec((cut, chans), lambda k: (k, 0))],
        out_shape=[
            jax.ShapeDtypeStruct((chans, hidden), F32),
            jax.ShapeDtypeStruct((hidden, chans), F32),
        ],
        compiler_params=params(),
        cost_estimate=cost(3),
        name="weight_grads",
    )(place_in([core])[None], weights, swap(weights, *core))
    d_skip = small[2 * KSIZE + 1]
    n_sums = 2 * KSIZE + 2
    d_gain, d_bias, d_bout, d_scale = (small[n_sums + i] for i in range(4))
    d_bin = small[n_sums + 4 :].reshape(hidden)

    mode_shape = jax.ShapeDtypeStruct(zr.shape, F32)
    g_rate, g_freq, g_re, g_im, g_step = pl.pallas_call(
        taps_grad_kernel,
        out_shape=[mode_shape] * 4 + [jax.ShapeDtypeStruct((2, chans), F32)],
        name="taps_grad",
    )(zr, zi, cr_t, ci_t, rate_t, freq_t, step, small[:n_sums])
    g_rate, g_freq, g_re, g_im = (v.transpose(0, 2, 1) for v in (g_rate, g_freq, g_re, g_im))
    return (
        output, image_grad, g_rate, g_freq, g_re, g_im, g_step, d_skip, d_gain, d_bias,
        d_win, d_bin, d_wout, d_bout, d_scale,
    )


def solution(mesh):
    tiled = P("th", "tw", None)
    return jax.shard_map(
        per_device,
        mesh=mesh,
        in_specs=(tiled,) + (P(),) * 14 + (tiled,),
        out_specs=(tiled, tiled) + (P(),) * 13,
        check_vma=False,
    )
```

time: 335 us -> 285 us (0.85)
  waiting for transfers between devices: 64.4 us -> 8.18 us
  Pallas kernels: 178 us -> 188 us
  starting transfers between devices: 57 us -> 49.4 us
  other arithmetic: 11.4 us -> 15.3 us
    ppermute x15 -> x22, waiting for transfers between devices: 56.2 us -> 8.16 us  [swap(): return lax.ppermute(block, axis, [(i, i ^ bit) for i in range(count)])]
    ppermute x8 -> x7, starting transfers between devices: 20.8 us -> 9.36 us  [the longest x3 5.7 us: swap_two(): return lax.ppermute(block, ('th', 'tw'), pairs)]
    pallas_call x3 -> x9, Pallas kernels: 98.8 us -> 110 us  [the longest x1 34.6 us: cols_back(): pl.pallas_call(cols_back_kernel, grid=(blocks,), in_specs=[SCALARS, lane_...]
    ppermute x8 -> x7, waiting for transfers between devices: 8.24 us -> 0.02 us  [the longest x4 0.01 us: swap_across(): return lax.ppermute(block, axis, pairs + [(j, i) for i, j in pairs])]
    dynamic_slice x5 -> x10, local copies, waits for them, and re-layouts: 1.62 us -> 8.91 us  [the longest x2 4.55 us: halo_rows(): lax.dynamic_slice_in_dim(block, place * far, REACH, 0)]
    slice x9 -> x1, local copies, waits for them, and re-layouts: 6 us -> 0.74 us  [per_device(): small[:n_sums]]
    add x5, other arithmetic: 0.85 us -> 5.61 us  [the longest x2 3.84 us: scatter(): total = total + tie(take, *done).astype(F32)]
    ppermute x15 -> x22, starting transfers between devices: 36.2 us -> 40 us  [swap(): return lax.ppermute(block, axis, [(i, i ^ bit) for i in range(count)])]
  transfers between devices with their start and end apart: 23 -> 29, of which waited for: 14 -> 3; matrix products, arithmetic and copies ran while one was open for 6% -> 10% of each run, Pallas kernels for 20% -> 30%
where the time goes in v2:
time: 285 us; the launch traced here: 284 us
  Pallas kernels  188 us (66%)
  starting transfers between devices  49.4 us (17%)
  local copies, waits for them, and re-layouts  20.9 us (7%)
  other arithmetic  15.3 us (5%)
  waiting for transfers between devices  8.18 us (3%)
    pallas_call x1, Pallas kernels, per_device(): pl.pallas_call(feed_kernel, grid=(pixels // tile,), in_specs=[pixel_block...  75.5 us
    ppermute x22, starting transfers between devices, swap(): return lax.ppermute(block, axis, [(i, i ^ bit) for i in range(count)])  40 us
    pallas_call x1, Pallas kernels, cols_back(): pl.pallas_call(cols_back_kernel, grid=(blocks,), in_specs=[SCALARS, lane_...  34.6 us
    pallas_call x3, Pallas kernels, rows_back(): pl.pallas_call(rows_back_kernel, grid=(4,), in_specs=[SCALARS, lanes(2, K...  22.1 us
    pallas_call x1, Pallas kernels, per_device(): pl.pallas_call(cols_kernel, grid=(groups,), in_specs=[SCALARS, whole((2,...  22.1 us
    pallas_call x1, Pallas kernels, per_device(): pl.pallas_call(rows_kernel, grid=(blocks,), in_specs=[SCALARS, lane_block...  14 us
    pallas_call x1, Pallas kernels, cols_grad(): pl.pallas_call(cols_grad_kernel, grid=(groups,), in_specs=[whole((size, 2...  9.92 us
    ppermute x22, waiting for transfers between devices, swap(): return lax.ppermute(block, axis, [(i, i ^ bit) for i in range(count)])  8.16 us
  transfers between devices with their start and end apart: 29, of which 3 were waited for; matrix products, arithmetic and copies ran while one was open for 10% of the time, Pallas kernels for 30%

profile of v2, /device:TPU:0, one launch (start us, length us, event | category | flops | bytes accessed | tf_op | source)
XLA Modules:
  0.0 284.0 jit_solution(1705870536542419859)
XLA Ops:
  0.7 2.3 constant_dynamic-slice_fusion.18
  4.1 1.3 fusion.4
  9.0 1.2 constant_dynamic-slice_fusion.14
  10.3 1.1 sine_multiply_fusion
  11.4 0.8 pad_maximum_fusion.1
  12.2 2.7 collective-permute-start.2
  14.9 0.9 pad_maximum_fusion.2
  15.8 1.4 collective-permute-start.3
  18.5 1.4 copy.43
  19.9 1.4 copy.42
  22.0 2.6 taps.1
  25.9 14.0 %rows_forward.1.partial_ref = bf16[64,96,384]{2,1,0:T(8,128)(2,1)} custom-call(s32[962]{0:T(1024)} %pad_add_fusion.source_ref, f32[2,16,384]{2,1,0:T(8,128)} %get-tuple-element.57.taps_ref, bf16[64,96,384]{2,1,0:T(8,128)(2,1)} %image_ref.3, bf16[7,96,384]{2,1,0:T(8,128)(2,1)} %copy-done.1, bf16[7,96,384]{2,1,0:T(8,128)(2,1)} %copy-done.2), custom_call_target="tpu_custom_call" | custom-call | flops 1400000000 | bytes 1400000 | tf_op jit(solution)/shard_map/rows_forward/pallas_call | solution.py:576
  39.9 22.1 %cols_forward.1 = (f32[64,96,384]{2,1,0:T(8,128)}, bf16[64,112,384]{2,1,0:T(8,128)(2,1)}) custom-call(s32[962]{0:T(1024)} %pad_add_fusion.source_ref, f32[2,16,384]{2,1,0:T(8,128)} %get-tuple-element.57.taps_ref, f32[1,384]{1,0:T(1,128)} %broadcast_in_dim.27.skip_ref, f32[3,56,384]{2,1,0:T(8,128)} %get-tuple-element.58.factor_ref, ...), custom_call_target="tpu_custom_call" | custom-call | flops 1400000000 | bytes 1400000 | tf_op jit(solution)/shard_map/cols_forward/pallas_call | solution.py:591
  61.9 75.5 %feed_forward.1 = (bf16[6144,384]{1,0:T(8,128)(2,1)}, bf16[6144,384]{1,0:T(8,128)(2,1)}, f32[768,1536]{1,0:T(8,128)}, f32[8,1536]{1,0:T(8,128)}, f32[4,8,384]{2,1,0:T(8,128)}) custom-call(f32[6144,384]{1,0:T(8,128)} %bitcast.39, bf16[6144,384]{1,0:T(8,128)(2,1)} %bitcast.29, bf16[6144,384]{1,0:T(8,128)(2,1)} %bitcast.30, bf16[384,1536]{1,0:T(8,128)(2,1)} %w_in_ref.1, ...), custom_call_target="tpu_custom_call" | custom-call | flops 7000000000 | bytes 7000000 | tf_op jit(solution)/shard_map/feed_forward/pallas_call | solution.py:620
  137.4 1.8 constant_dynamic-slice_fusion.11
  139.2 2.8 %collective-permute-start.4 = (f32[384,1536]{1,0:T(8,128)S(1)}, f32[384,1536]{1,0:T(8,128)}, u32[]{:S(2)}, u32[]{:S(2)}) collective-permute-start(f32[384,1536]{1,0:T(8,128)S(1)} %constant_dynamic-slice_fusion.11), channel_id=1, source_target_pairs={{0,8},{8,0},{16,24},{24,16},{1,9},{9,1},{17,25},{25,17},{2,10},{10... | collective-permute-start | bytes 7077896 | tf_op jit(solution)/shard_map/ppermute | solution.py:21
  142.1 2.3 constant_dynamic-slice_fusion.9
  146.0 1.2 constant_dynamic-slice_fusion.5
  147.3 1.0 pad_maximum_fusion.4
  148.3 0.9 collective-permute-start.9
  149.2 0.9 pad_maximum_fusion.3
  150.0 4.7 %collective-permute-start.8 = (bf16[78,8,384]{2,1,0:T(8,128)(2,1)}, bf16[78,8,384]{2,1,0:T(8,128)(2,1)}, u32[]{:S(2)}, u32[]{:S(2)}) collective-permute-start(bf16[78,8,384]{2,1,0:T(8,128)(2,1)} %pad_maximum_fusion.3), channel_id=1, source_target_pairs={{0,1},{1,0},{2,3},{3,2},{4,5},{5,4},{6,7},{7,6},{8,9},{9,8},{10,11... | collective-permute-start | bytes 1437704 | tf_op jit(solution)/shard_map/ppermute | solution.py:21
  154.8 9.9 %cols_grad.1 = f32[16,384]{1,0:T(8,128)} custom-call(bf16[112,192]{1,0:T(8,128)(2,1)} %constant.140.clone.own_ref, f32[16,168]{1,0:T(8,128)} %constant.141.clone.lags_ref, bf16[64,96,384]{2,1,0:T(8,128)(2,1)} %bitcast.24, bf16[64,112,384]{2,1,0:T(8,128)(2,1)} %get-tuple-element.70.spectrum_ref, bf16[64,96,384]{2,1,0:T(8,128)(2,1)} %image_ref.3), custom_call_target="tpu_custom_call" | custom-call | flops 800000000 | bytes 800000 | tf_op jit(solution)/shard_map/cols_grad/pallas_call | solution.py:658
  164.7 2.8 dynamic-slice_add_fusion
  168.3 10.0 %collective-permute-start.5 = (bf16[96,1536]{1,0:T(8,128)(2,1)}, bf16[96,1536]{1,0:T(8,128)(2,1)S(1)}, u32[]{:S(2)}, u32[]{:S(2)}) collective-permute-start(bf16[96,1536]{1,0:T(8,128)(2,1)} %get-tuple-element.114), channel_id=1, source_target_pairs={{0,16},{8,24},{16,0},{24,8},{1,17},{9,25},{17,1},{25,9},{2,18},{10... | collective-permute-start | bytes 884744 | tf_op jit(solution)/shard_map/ppermute | solution.py:21
  178.3 1.5 collective-permute-start.11
  180.6 34.6 %cols_back.1 = (bf16[78,96,384]{2,1,0:T(8,128)(2,1)}, f32[16,384]{1,0:T(8,128)}) custom-call(s32[962]{0:T(1024)} %pad_add_fusion.source_ref, f32[3,56,384]{2,1,0:T(8,128)} %get-tuple-element.58.factor_ref, bf16[112,224]{1,0:T(8,128)(2,1)} %broadcast_select_fusion.forward_ref, bf16[96,224]{1,0:T(8,128)(2,1)} %constant.142.clone.behind_ref, ...), custom_call_target="tpu_custom_call" | custom-call | flops 2000000000 | bytes 2000000 | tf_op jit(solution)/shard_map/cols_back/pallas_call | solution.py:679
  215.2 1.4 pad_maximum_fusion.6
  216.6 1.6 collective-permute-done.13
  219.0 2.1 collective-permute-start.17
  221.1 1.5 collective-permute-start.19
  222.6 1.1 convert_add_fusion
  223.8 1.6 collective-permute-start.12
  225.4 2.6 collective-permute-start.14
  228.0 7.4 %rows_back.3.rest_0_ = bf16[64,96,384]{2,1,0:T(8,128)(2,1)} custom-call(s32[962]{0:T(1024)} %pad_add_fusion.source_ref, f32[2,16,384]{2,1,0:T(8,128)} %get-tuple-element.57.taps_ref, f32[1,384]{1,0:T(1,128)} %broadcast_in_dim.27.skip_ref, bf16[78,96,384]{2,1,0:T(8,128)(2,1)} %get-tuple-element.64.d_partial_ref, bf16[64,96,384]{2,1,0:T(8,128)(2,1)} %bitcast.26, ...), custom_call_target="tpu_custom_call" | custom-call | flops 600000000 | bytes 600000 | tf_op jit(solution)/shard_map/rows_back/pallas_call | solution.py:718
  236.0 0.9 add_add_fusion.1
  237.4 3.4 %collective-permute-start.23 = (f32[40,384]{1,0:T(8,128)S(1)}, f32[40,384]{1,0:T(8,128)S(1)}, u32[]{:S(2)}, u32[]{:S(2)}) collective-permute-start(f32[40,384]{1,0:T(8,128)S(1)} %add_add_fusion.1), channel_id=1, source_target_pairs={{0,4},{1,5},{2,6},{3,7},{4,0},{5,1},{6,2},{7,3},{8,12},{9,13},{10,... | collective-permute-start | bytes 184328 | tf_op jit(solution)/shard_map/ppermute | solution.py:21
  241.4 2.0 collective-permute-done.15
  243.4 1.4 collective-permute-start.21
  244.8 4.5 %collective-permute-start.20 = (bf16[24,1536]{1,0:T(8,128)(2,1)S(1)}, bf16[24,1536]{1,0:T(8,128)(2,1)S(1)}, u32[]{:S(2)}, u32[]{:S(2)}) collective-permute-start(bf16[24,1536]{1,0:T(8,128)(2,1)S(1)} %add_convert_fusion), channel_id=1, source_target_pairs={{0,2},{1,3},{2,0},{3,1},{4,6},{5,7},{6,4},{7,5},{8,10},{9,11},{10,... | collective-permute-start | bytes 221192 | tf_op jit(solution)/shard_map/ppermute | solution.py:21
  249.3 7.4 %rows_back.4.rest_0_ = bf16[64,96,384]{2,1,0:T(8,128)(2,1)} custom-call(s32[962]{0:T(1024)} %pad_add_fusion.source_ref, f32[2,16,384]{2,1,0:T(8,128)} %get-tuple-element.57.taps_ref, f32[1,384]{1,0:T(1,128)} %broadcast_in_dim.27.skip_ref, bf16[78,96,384]{2,1,0:T(8,128)(2,1)} %get-tuple-element.64.d_partial_ref, ...), custom_call_target="tpu_custom_call", output_to_operand_aliasing={{}: (6, {})} | custom-call | flops 600000000 | bytes 600000 | tf_op jit(solution)/shard_map/rows_back/pallas_call | solution.py:718
  256.6 1.4 collective-permute-start.16
  258.1 4.5 %collective-permute-done.16 = bf16[24,1536]{1,0:T(8,128)(2,1)S(1)} collective-permute-done((bf16[24,1536]{1,0:T(8,128)(2,1)S(1)}, bf16[24,1536]{1,0:T(8,128)(2,1)S(1)}, u32[]{:S(2)}, u32[]{:S(2)}) %collective-permute-start.16) | collective-permute-done | bytes 73760 | tf_op jit(solution)/shard_map/ppermute | solution.py:21
  262.7 2.7 collective-permute-start.27
  266.2 7.4 %rows_back.5 = bf16[64,96,384]{2,1,0:T(8,128)(2,1)} custom-call(s32[962]{0:T(1024)} %pad_add_fusion.source_ref, f32[2,16,384]{2,1,0:T(8,128)} %get-tuple-element.57.taps_ref, f32[1,384]{1,0:T(1,128)} %broadcast_in_dim.27.skip_ref, bf16[78,96,384]{2,1,0:T(8,128)(2,1)} %get-tuple-element.64.d_partial_ref, ...), custom_call_target="tpu_custom_call", output_to_operand_aliasing={{}: (6, {})} | custom-call | flops 600000000 | bytes 600000 | tf_op jit(solution)/shard_map/rows_back/pallas_call | solution.py:718
  275.3 2.5 taps_grad.1
  278.5 1.0 copy-done.3
  279.5 4.5 %weight_grads.1 = (f32[384,1536]{1,0:T(8,128)}, f32[1536,384]{1,0:T(8,128)}) custom-call(s32[1]{0:T(128)} %bitcast.17.side_ref, bf16[384,1536]{1,0:T(8,128)(2,1)} %copy-done, bf16[384,1536]{1,0:T(8,128)(2,1)} %copy-done.3), custom_call_target="tpu_custom_call" | custom-call | flops 300000000 | bytes 300000 | tf_op jit(solution)/shard_map/weight_grads/pallas_call | solution.py:766
  (118 shorter events, 15.7 us)
Async XLA Ops:
  0.6 9.6 %copy-start.10 = (f32[2,384,32]{1,2,0:T(8,128)S(1)}, f32[2,384,32]{1,2,0:T(8,128)}, u32[]{:S(2)}) copy-start(f32[2,384,32]{1,2,0:T(8,128)} %param.25) | copy-start | bytes 294916
  0.7 9.6 %copy-start.9 = (f32[2,384,32]{1,2,0:T(8,128)S(1)}, f32[2,384,32]{1,2,0:T(8,128)}, u32[]{:S(2)}) copy-start(f32[2,384,32]{1,2,0:T(8,128)} %param.26) | copy-start | bytes 294916
  3.0 14.9 %copy-start.18 = (f32[384]{0:T(512)S(1)}, f32[384]{0:T(512)}, u32[]{:S(2)}) copy-start(f32[384]{0:T(512)} %param.30) | copy-start | bytes 4612
  3.0 15.4 %copy-start.4 = (bf16[384,1536]{1,0:T(8,128)(2,1)S(1)}, bf16[384,1536]{1,0:T(8,128)(2,1)}, u32[]{:S(2)}) copy-start(bf16[384,1536]{1,0:T(8,128)(2,1)} %w_in_ref.1) | copy-start | bytes 3538948
  3.0 8.3 %collective-permute-start = (bf16[7,96,384]{2,1,0:T(8,128)(2,1)}, bf16[7,96,384]{2,1,0:T(8,128)(2,1)S(1)}, u32[]{:S(2)}, u32[]{:S(2)}) collective-permute-start(bf16[7,96,384]{2,1,0:T(8,128)(2,1)} %get-tuple-element.111), channel_id=1, source_target_pairs={{0,8},{8,0},{16,24},{24,16},{1,9},{9,1},{17,25},{25,17},{2,10},{10... | collective-permute-start | bytes 1548296 | tf_op jit(solution)/shard_map/ppermute | solution.py:21
  3.5 7.9 %collective-permute-start.1 = (bf16[7,96,384]{2,1,0:T(8,128)(2,1)}, bf16[7,96,384]{2,1,0:T(8,128)(2,1)S(1)}, u32[]{:S(2)}, u32[]{:S(2)}) collective-permute-start(bf16[7,96,384]{2,1,0:T(8,128)(2,1)} %get-tuple-element.110), channel_id=1, source_target_pairs={{8,16},{16,8},{9,17},{17,9},{10,18},{18,10},{11,19},{19,11},{12,20... | collective-permute-start | bytes 1548296 | tf_op jit(solution)/shard_map/ppermute | solution.py:27
  11.3 8.6 %copy-start.5 = (bf16[1536,384]{1,0:T(8,128)(2,1)S(1)}, bf16[1536,384]{1,0:T(8,128)(2,1)}, u32[]{:S(2)}) copy-start(bf16[1536,384]{1,0:T(8,128)(2,1)} %w_out_ref.1) | copy-start | bytes 3538948
  11.3 10.0 %copy-start.1 = (bf16[7,96,384]{2,1,0:T(8,128)(2,1)}, bf16[7,96,384]{2,1,0:T(8,128)(2,1)S(1)}, u32[]{:S(2)}) copy-start(bf16[7,96,384]{2,1,0:T(8,128)(2,1)S(1)} %collective-permute-done.near.image_near) | copy-start | bytes 1548292
  11.3 10.0 %copy-start.2 = (bf16[7,96,384]{2,1,0:T(8,128)(2,1)}, bf16[7,96,384]{2,1,0:T(8,128)(2,1)S(1)}, u32[]{:S(2)}) copy-start(bf16[7,96,384]{2,1,0:T(8,128)(2,1)S(1)} %collective-permute-done.1.other.image_other) | copy-start | bytes 1548292
  12.2 27.6 %collective-permute-start.2 = (bf16[78,8,384]{2,1,0:T(8,128)(2,1)}, bf16[78,8,384]{2,1,0:T(8,128)(2,1)}, u32[]{:S(2)}, u32[]{:S(2)}) collective-permute-start(bf16[78,8,384]{2,1,0:T(8,128)(2,1)} %pad_maximum_fusion.1), channel_id=1, source_target_pairs={{0,1},{1,0},{2,3},{3,2},{4,5},{5,4},{6,7},{7,6},{8,9},{9,8},{10,11... | collective-permute-start | bytes 1437704 | tf_op jit(solution)/shard_map/ppermute | solution.py:21
  15.8 24.1 %collective-permute-start.3 = (bf16[78,8,384]{2,1,0:T(8,128)(2,1)}, bf16[78,8,384]{2,1,0:T(8,128)(2,1)}, u32[]{:S(2)}, u32[]{:S(2)}) collective-permute-start(bf16[78,8,384]{2,1,0:T(8,128)(2,1)} %pad_maximum_fusion.2), channel_id=1, source_target_pairs={{1,2},{3,4},{5,6},{2,1},{4,3},{6,5},{9,10},{11,12},{13,14},{10,9},... | collective-permute-start | bytes 1437704 | tf_op jit(solution)/shard_map/ppermute | solution.py:27
  18.4 2.9 %copy-start.19 = (f32[384]{0:T(512)S(1)}, f32[384]{0:T(512)}, u32[]{:S(2)}) copy-start(f32[384]{0:T(512)} %param.31) | copy-start | bytes 4612
  18.4 2.9 %copy-start.20 = (f32[384]{0:T(512)S(1)}, f32[384]{0:T(512)}, u32[]{:S(2)}) copy-start(f32[384]{0:T(512)} %param.32) | copy-start | bytes 4612
  18.4 3.0 %copy-start.21 = (f32[384]{0:T(512)S(1)}, f32[384]{0:T(512)}, u32[]{:S(2)}) copy-start(f32[384]{0:T(512)} %param.36) | copy-start | bytes 4612
  18.4 3.0 %copy-start.22 = (f32[384]{0:T(512)S(1)}, f32[384]{0:T(512)}, u32[]{:S(2)}) copy-start(f32[384]{0:T(512)} %param.37) | copy-start | bytes 4612
  18.4 3.0 %copy-start.17 = (f32[1536]{0:T(1024)S(1)}, f32[1536]{0:T(1024)}, u32[]{:S(2)}) copy-start(f32[1536]{0:T(1024)} %param.34) | copy-start | bytes 18436
  18.5 6.8 %copy-start.13 = (bf16[112,224]{1,0:T(8,128)(2,1)S(1)}, bf16[112,224]{1,0:T(8,128)(2,1)}, u32[]{:S(2)}) copy-start(bf16[112,224]{1,0:T(8,128)(2,1)} %constant.136.clone) | copy-start | bytes 150532
  18.5 6.8 %copy-start.14 = (bf16[112,224]{1,0:T(8,128)(2,1)S(1)}, bf16[112,224]{1,0:T(8,128)(2,1)}, u32[]{:S(2)}) copy-start(bf16[112,224]{1,0:T(8,128)(2,1)} %constant.137.clone) | copy-start | bytes 150532
  137.4 8.5 %copy-start.15 = (f32[4,8,384]{2,1,0:T(8,128)S(1)}, f32[4,8,384]{2,1,0:T(8,128)}, u32[]{:S(2)}) copy-start(f32[4,8,384]{2,1,0:T(8,128)} %get-tuple-element.71) | copy-start | bytes 147460
  139.2 25.5 %collective-permute-start.4 = (f32[384,1536]{1,0:T(8,128)S(1)}, f32[384,1536]{1,0:T(8,128)}, u32[]{:S(2)}, u32[]{:S(2)}) collective-permute-start(f32[384,1536]{1,0:T(8,128)S(1)} %constant_dynamic-slice_fusion.11), channel_id=1, source_target_pairs={{0,8},{8,0},{16,24},{24,16},{1,9},{9,1},{17,25},{25,17},{2,10},{10... | collective-permute-start | bytes 7077896 | tf_op jit(solution)/shard_map/ppermute | solution.py:21
  144.3 2.9 %collective-permute-start.6 = (bf16[7,96,384]{2,1,0:T(8,128)(2,1)}, bf16[7,96,384]{2,1,0:T(8,128)(2,1)S(1)}, u32[]{:S(2)}, u32[]{:S(2)}) collective-permute-start(bf16[7,96,384]{2,1,0:T(8,128)(2,1)} %get-tuple-element.107), channel_id=1, source_target_pairs={{0,8},{8,0},{16,24},{24,16},{1,9},{9,1},{17,25},{25,17},{2,10},{10... | collective-permute-start | bytes 1548296 | tf_op jit(solution)/shard_map/ppermute | solution.py:21
  144.4 2.9 %collective-permute-start.7 = (bf16[7,96,384]{2,1,0:T(8,128)(2,1)}, bf16[7,96,384]{2,1,0:T(8,128)(2,1)S(1)}, u32[]{:S(2)}, u32[]{:S(2)}) collective-permute-start(bf16[7,96,384]{2,1,0:T(8,128)(2,1)} %get-tuple-element.106), channel_id=1, source_target_pairs={{8,16},{16,8},{9,17},{17,9},{10,18},{18,10},{11,19},{19,11},{12,20... | collective-permute-start | bytes 1548296 | tf_op jit(solution)/shard_map/ppermute | solution.py:27
  147.2 17.5 %copy-start.6 = (bf16[7,96,384]{2,1,0:T(8,128)(2,1)}, bf16[7,96,384]{2,1,0:T(8,128)(2,1)S(1)}, u32[]{:S(2)}) copy-start(bf16[7,96,384]{2,1,0:T(8,128)(2,1)S(1)} %collective-permute-done.6.row_near) | copy-start | bytes 1548292
  147.3 17.4 %copy-start.7 = (bf16[7,96,384]{2,1,0:T(8,128)(2,1)}, bf16[7,96,384]{2,1,0:T(8,128)(2,1)S(1)}, u32[]{:S(2)}) copy-start(bf16[7,96,384]{2,1,0:T(8,128)(2,1)S(1)} %collective-permute-done.7.row_other) | copy-start | bytes 1548292
  148.3 31.5 %collective-permute-start.9 = (bf16[78,8,384]{2,1,0:T(8,128)(2,1)}, bf16[78,8,384]{2,1,0:T(8,128)(2,1)S(1)}, u32[]{:S(2)}, u32[]{:S(2)}) collective-permute-start(bf16[78,8,384]{2,1,0:T(8,128)(2,1)} %pad_maximum_fusion.4), channel_id=1, source_target_pairs={{1,2},{3,4},{5,6},{2,1},{4,3},{6,5},{9,10},{11,12},{13,14},{10,9},... | collective-permute-start | bytes 1437704 | tf_op jit(solution)/shard_map/ppermute | solution.py:27
  150.0 29.8 %collective-permute-start.8 = (bf16[78,8,384]{2,1,0:T(8,128)(2,1)}, bf16[78,8,384]{2,1,0:T(8,128)(2,1)}, u32[]{:S(2)}, u32[]{:S(2)}) collective-permute-start(bf16[78,8,384]{2,1,0:T(8,128)(2,1)} %pad_maximum_fusion.3), channel_id=1, source_target_pairs={{0,1},{1,0},{2,3},{3,2},{4,5},{5,4},{6,7},{7,6},{8,9},{9,8},{10,11... | collective-permute-start | bytes 1437704 | tf_op jit(solution)/shard_map/ppermute | solution.py:21
  168.3 52.8 %collective-permute-start.5 = (bf16[96,1536]{1,0:T(8,128)(2,1)}, bf16[96,1536]{1,0:T(8,128)(2,1)S(1)}, u32[]{:S(2)}, u32[]{:S(2)}) collective-permute-start(bf16[96,1536]{1,0:T(8,128)(2,1)} %get-tuple-element.114), channel_id=1, source_target_pairs={{0,16},{8,24},{16,0},{24,8},{1,17},{9,25},{17,1},{25,9},{2,18},{10... | collective-permute-start | bytes 884744 | tf_op jit(solution)/shard_map/ppermute | solution.py:21
  178.3 44.3 %collective-permute-start.10 = (bf16[96,1536]{1,0:T(8,128)(2,1)S(1)}, bf16[96,1536]{1,0:T(8,128)(2,1)S(1)}, u32[]{:S(2)}, u32[]{:S(2)}) collective-permute-start(bf16[96,1536]{1,0:T(8,128)(2,1)S(1)} %get-tuple-element.112), channel_id=1, source_target_pairs={{0,1},{1,0},{2,3},{3,2},{4,5},{5,4},{6,7},{7,6},{8,9},{9,8},{10,11... | collective-permute-start | bytes 884744 | tf_op jit(solution)/shard_map/ppermute | solution.py:21
  178.3 36.9 %copy-start.11 = (f32[16,384]{1,0:T(8,128)S(1)}, f32[16,384]{1,0:T(8,128)}, u32[]{:S(2)}) copy-start(f32[16,384]{1,0:T(8,128)} %cols_grad.1) | copy-start | bytes 73732
  178.3 44.3 %collective-permute-start.11 = (bf16[96,1536]{1,0:T(8,128)(2,1)S(1)}, bf16[96,1536]{1,0:T(8,128)(2,1)}, u32[]{:S(2)}, u32[]{:S(2)}) collective-permute-start(bf16[96,1536]{1,0:T(8,128)(2,1)S(1)} %get-tuple-element.113), channel_id=1, source_target_pairs={{0,17},{1,16},{2,19},{3,18},{4,21},{5,20},{6,23},{7,22},{8,25},{9,... | collective-permute-start | bytes 884744 | tf_op jit(solution)/shard_map/ppermute | solution.py:471
  216.6 1.6 collective-permute-start.13
  219.0 16.4 %collective-permute-start.17 = (f32[40,384]{1,0:T(8,128)S(1)}, f32[40,384]{1,0:T(8,128)S(1)}, u32[]{:S(2)}, u32[]{:S(2)}) collective-permute-start(f32[40,384]{1,0:T(8,128)S(1)} %fusion.3), channel_id=1, source_target_pairs={{0,16},{8,24},{16,0},{24,8},{1,17},{9,25},{17,1},{25,9},{2,18},{10... | collective-permute-start | bytes 184328 | tf_op jit(solution)/shard_map/ppermute | solution.py:21
  221.1 14.6 %collective-permute-start.18 = (f32[40,384]{1,0:T(8,128)S(1)}, f32[40,384]{1,0:T(8,128)}, u32[]{:S(2)}, u32[]{:S(2)}) collective-permute-start(f32[40,384]{1,0:T(8,128)S(1)} %fusion.3), channel_id=1, source_target_pairs={{0,1},{1,0},{2,3},{3,2},{4,5},{5,4},{6,7},{7,6},{8,9},{9,8},{10,11... | collective-permute-start | bytes 184328 | tf_op jit(solution)/shard_map/ppermute | solution.py:21
  221.1 14.9 %collective-permute-start.19 = (f32[40,384]{1,0:T(8,128)S(1)}, f32[40,384]{1,0:T(8,128)}, u32[]{:S(2)}, u32[]{:S(2)}) collective-permute-start(f32[40,384]{1,0:T(8,128)S(1)} %fusion.3), channel_id=1, source_target_pairs={{0,17},{1,16},{2,19},{3,18},{4,21},{5,20},{6,23},{7,22},{8,25},{9,... | collective-permute-start | bytes 184328 | tf_op jit(solution)/shard_map/ppermute | solution.py:471
  223.8 17.1 %collective-permute-start.12 = (f32[24,1536]{1,0:T(8,128)S(1)}, f32[24,1536]{1,0:T(8,128)S(1)}, u32[]{:S(2)}, u32[]{:S(2)}) collective-permute-start(f32[24,1536]{1,0:T(8,128)S(1)} %get-tuple-element.121), channel_id=1, source_target_pairs={{0,2},{1,3},{2,0},{3,1},{4,6},{5,7},{6,4},{7,5},{8,10},{9,11},{10,... | collective-permute-start | bytes 442376 | tf_op jit(solution)/shard_map/ppermute | solution.py:21
  225.4 16.0 %collective-permute-start.14 = (f32[24,1536]{1,0:T(8,128)S(1)}, f32[24,1536]{1,0:T(8,128)S(1)}, u32[]{:S(2)}, u32[]{:S(2)}) collective-permute-start(f32[24,1536]{1,0:T(8,128)S(1)} %get-tuple-element.119), channel_id=1, source_target_pairs={{0,4},{1,5},{2,6},{3,7},{4,0},{5,1},{6,2},{7,3},{8,12},{9,13},{10,... | collective-permute-start | bytes 442376 | tf_op jit(solution)/shard_map/ppermute | solution.py:21
  235.4 8.0 %collective-permute-start.15 = (f32[24,1536]{1,0:T(8,128)S(1)}, f32[24,1536]{1,0:T(8,128)S(1)}, u32[]{:S(2)}, u32[]{:S(2)}) collective-permute-start(f32[24,1536]{1,0:T(8,128)S(1)} %get-tuple-element.120), channel_id=1, source_target_pairs={{0,6},{1,7},{2,4},{3,5},{4,2},{5,3},{6,0},{7,1},{8,14},{9,15},{10,... | collective-permute-start | bytes 442376 | tf_op jit(solution)/shard_map/ppermute | solution.py:21
  236.9 19.7 %collective-permute-start.22 = (f32[40,384]{1,0:T(8,128)S(1)}, f32[40,384]{1,0:T(8,128)S(1)}, u32[]{:S(2)}, u32[]{:S(2)}) collective-permute-start(f32[40,384]{1,0:T(8,128)S(1)} %add_add_fusion.1), channel_id=1, source_target_pairs={{0,2},{1,3},{2,0},{3,1},{4,6},{5,7},{6,4},{7,5},{8,10},{9,11},{10,... | collective-permute-start | bytes 184328 | tf_op jit(solution)/shard_map/ppermute | solution.py:21
  237.4 20.6 %collective-permute-start.23 = (f32[40,384]{1,0:T(8,128)S(1)}, f32[40,384]{1,0:T(8,128)S(1)}, u32[]{:S(2)}, u32[]{:S(2)}) collective-permute-start(f32[40,384]{1,0:T(8,128)S(1)} %add_add_fusion.1), channel_id=1, source_target_pairs={{0,4},{1,5},{2,6},{3,7},{4,0},{5,1},{6,2},{7,3},{8,12},{9,13},{10,... | collective-permute-start | bytes 184328 | tf_op jit(solution)/shard_map/ppermute | solution.py:21
  240.8 17.2 %collective-permute-start.24 = (f32[40,384]{1,0:T(8,128)S(1)}, f32[40,384]{1,0:T(8,128)S(1)}, u32[]{:S(2)}, u32[]{:S(2)}) collective-permute-start(f32[40,384]{1,0:T(8,128)S(1)} %add_add_fusion.1), channel_id=1, source_target_pairs={{0,6},{1,7},{2,4},{3,5},{4,2},{5,3},{6,0},{7,1},{8,14},{9,15},{10,... | collective-permute-start | bytes 184328 | tf_op jit(solution)/shard_map/ppermute | solution.py:21
  243.4 14.7 %collective-permute-start.21 = (bf16[24,1536]{1,0:T(8,128)(2,1)S(1)}, bf16[24,1536]{1,0:T(8,128)(2,1)S(1)}, u32[]{:S(2)}, u32[]{:S(2)}) collective-permute-start(bf16[24,1536]{1,0:T(8,128)(2,1)S(1)} %add_convert_fusion), channel_id=1, source_target_pairs={{0,6},{1,7},{2,4},{3,5},{4,2},{5,3},{6,0},{7,1},{8,14},{9,15},{10,... | collective-permute-start | bytes 221192 | tf_op jit(solution)/shard_map/ppermute | solution.py:21
  244.8 13.3 %collective-permute-start.20 = (bf16[24,1536]{1,0:T(8,128)(2,1)S(1)}, bf16[24,1536]{1,0:T(8,128)(2,1)S(1)}, u32[]{:S(2)}, u32[]{:S(2)}) collective-permute-start(bf16[24,1536]{1,0:T(8,128)(2,1)S(1)} %add_convert_fusion), channel_id=1, source_target_pairs={{0,2},{1,3},{2,0},{3,1},{4,6},{5,7},{6,4},{7,5},{8,10},{9,11},{10,... | collective-permute-start | bytes 221192 | tf_op jit(solution)/shard_map/ppermute | solution.py:21
  256.6 6.0 %collective-permute-start.16 = (bf16[24,1536]{1,0:T(8,128)(2,1)S(1)}, bf16[24,1536]{1,0:T(8,128)(2,1)S(1)}, u32[]{:S(2)}, u32[]{:S(2)}) collective-permute-start(bf16[24,1536]{1,0:T(8,128)(2,1)S(1)} %add_convert_fusion), channel_id=1, source_target_pairs={{0,4},{1,5},{2,6},{3,7},{4,0},{5,1},{6,2},{7,3},{8,12},{9,13},{10,... | collective-permute-start | bytes 221192 | tf_op jit(solution)/shard_map/ppermute | solution.py:21
  262.7 10.9 %collective-permute-start.27 = (bf16[96,1536]{1,0:T(8,128)(2,1)S(1)}, bf16[96,1536]{1,0:T(8,128)(2,1)S(1)}, u32[]{:S(2)}, u32[]{:S(2)}) collective-permute-start(bf16[96,1536]{1,0:T(8,128)(2,1)S(1)} %pad_maximum_fusion.5), channel_id=1, source_target_pairs={{0,17},{1,16},{2,19},{3,18},{4,21},{5,20},{6,23},{7,22},{8,25},{9,... | collective-permute-start | bytes 884744 | tf_op jit(solution)/shard_map/ppermute | solution.py:471
  265.4 8.3 %collective-permute-start.26 = (bf16[96,1536]{1,0:T(8,128)(2,1)S(1)}, bf16[96,1536]{1,0:T(8,128)(2,1)S(1)}, u32[]{:S(2)}, u32[]{:S(2)}) collective-permute-start(bf16[96,1536]{1,0:T(8,128)(2,1)S(1)} %pad_maximum_fusion.5), channel_id=1, source_target_pairs={{0,16},{8,24},{16,0},{24,8},{1,17},{9,25},{17,1},{25,9},{2,18},{10... | collective-permute-start | bytes 884744 | tf_op jit(solution)/shard_map/ppermute | solution.py:21
  265.7 7.9 %collective-permute-start.25 = (bf16[96,1536]{1,0:T(8,128)(2,1)S(1)}, bf16[96,1536]{1,0:T(8,128)(2,1)S(1)}, u32[]{:S(2)}, u32[]{:S(2)}) collective-permute-start(bf16[96,1536]{1,0:T(8,128)(2,1)S(1)} %pad_maximum_fusion.5), channel_id=1, source_target_pairs={{0,1},{1,0},{2,3},{3,2},{4,5},{5,4},{6,7},{7,6},{8,9},{9,8},{10,11... | collective-permute-start | bytes 884744 | tf_op jit(solution)/shard_map/ppermute | solution.py:21
  273.9 4.6 %copy-start = (bf16[384,1536]{1,0:T(8,128)(2,1)}, bf16[384,1536]{1,0:T(8,128)(2,1)S(1)}, u32[]{:S(2)}) copy-start(bf16[384,1536]{1,0:T(8,128)(2,1)S(1)} %pad_maximum_fusion.own_ref) | copy-start | bytes 3538948
  273.9 4.6 %collective-permute-start.28 = (bf16[384,1536]{1,0:T(8,128)(2,1)S(1)}, bf16[384,1536]{1,0:T(8,128)(2,1)S(1)}, u32[]{:S(2)}, u32[]{:S(2)}) collective-permute-start(bf16[384,1536]{1,0:T(8,128)(2,1)S(1)} %pad_maximum_fusion.own_ref), channel_id=1, source_target_pairs={{0,8},{8,0},{16,24},{24,16},{1,9},{9,1},{17,25},{25,17},{2,10},{10... | collective-permute-start | bytes 3538952 | tf_op jit(solution)/shard_map/ppermute | solution.py:21
  (4 other events, 3.6 us)

commit v3 on v2

--- a/solution.py
+++ b/solution.py
@@ -1,3 +1,5 @@
+import functools
+
 import jax
 import jax.numpy as jnp
 import ml_dtypes
@@ -11,7 +13,8 @@
 REACH = KSIZE // 2
 EDGE = 8
 LANES = 128
-GROUP = 8
+GROUP = 16
+PAIR = 2
 MIB = 2**20
 F32, BF16 = jnp.float32, jnp.bfloat16
 
@@ -39,14 +42,13 @@
     return near, other
 
 
-def halo_cols(block, near, other):
+def halo_cols(*blocks):
     place = lax.axis_index("tw") % 2
-    far = block.shape[1] - EDGE
+    far = blocks[0].shape[1] - EDGE
 
     def edge(at):
-        return jnp.concatenate(
-            [lax.dynamic_slice_in_dim(v, at * far, EDGE, 1) for v in (block, near, other)], axis=0
-        )
+        parts = [lax.dynamic_slice_in_dim(v, at * far, EDGE, 1) for v in blocks]
+        return jnp.concatenate(parts, axis=0)
 
     edges = edge(1 - place), edge(place)
     return swap(edges[0], "tw", 1), swap_across(edges[1], "tw"), edges
@@ -109,10 +111,8 @@
     return decay * jnp.cos(phase), decay * jnp.sin(phase), step
 
 
-def dot(a, b, precision=None):
-    return lax.dot_general(
-        a, b, (((1,), (0,)), ((), ())), precision=precision, preferred_element_type=F32
-    )
+def dot(a, b, precision=None, dims=((1,), (0,))):
+    return lax.dot_general(a, b, (dims, ((), ())), precision=precision, preferred_element_type=F32)
 
 
 def taps_kernel(zr_ref, zi_ref, cr_ref, ci_ref, response_ref, taps_ref, factor_ref):
@@ -209,71 +209,84 @@
     return jnp.concatenate([a * real - cross, top * imag + across], axis=0).astype(BF16)
 
 
+def side_by_side(values):
+    return jnp.concatenate(values, axis=1)
+
+
 def cols_kernel(
     source_ref, taps_ref, skip_ref, factor_ref, forward_ref, ahead_ref,
     partial_ref, image_ref, near, other,
-    mixed_ref, spectrum_ref, sides, side_partial,
+    mixed_ref, spectrum_ref, sides,
 ):
     step = pl.program_id(0)
     full = near.shape[0]
     height = full - 2 * REACH
+    chans = skip_ref.shape[1]
 
     @pl.when(step == 0)
     def _():
         sides[full] = jnp.zeros(sides.shape[1:], F32)
-        for part, at in ((near, 0), (other, EDGE)):
-            for i in range(2 * REACH):
-                base = source_ref[height * KSIZE + i // REACH] + i % REACH
-                sides[base, at : at + EDGE] = part[height + i].astype(F32)
-
-            def place(r, _):
-                sides[r + REACH, at : at + EDGE] = part[r].astype(F32)
-                return 0
-
-            lax.fori_loop(0, height, place, 0)
-
-        taps = [taps_ref[0, i][None, :] for i in range(KSIZE)]
-
-        def row(r, _):
-            total = taps[0] * sides[source_ref[r * KSIZE]]
-            for i in range(1, KSIZE):
-                total = total + taps[i] * sides[source_ref[r * KSIZE + i]]
-            side_partial[r] = total.astype(BF16)
+        for i in range(2 * REACH):
+            base = source_ref[height * KSIZE + i // REACH] + i % REACH
+            sides[base] = jnp.concatenate(
+                [near[height + i].astype(F32), other[height + i].astype(F32)], axis=0
+            )
+
+        def place(r, _):
+            for k in range(4):
+                at = 4 * r + k
+                sides[at + REACH] = jnp.concatenate(
+                    [near[at].astype(F32), other[at].astype(F32)], axis=0
+                )
             return 0
 
-        lax.fori_loop(0, height, row, 0)
-
-    factor = [factor_ref[k] for k in range(3)]
+        lax.fori_loop(0, height // 4, place, 0)
+
+    taps = [taps_ref[0, i][None, :] for i in range(KSIZE)]
+    factor = paired(factor_ref)
     skip = skip_ref[...]
-    for k in range(GROUP):
-        line = jnp.concatenate([partial_ref[k], side_partial[step * GROUP + k]], axis=0)
-        spectrum = dot(forward_ref[...], twice(line))
-        spectrum_ref[k] = spectrum.astype(BF16)
+
+    def line(k):
+        at = (step * GROUP + k) * KSIZE
+        total = taps[0] * sides[source_ref[at]]
+        for i in range(1, KSIZE):
+            total = total + taps[i] * sides[source_ref[at + i]]
+        return jnp.concatenate([partial_ref[k], total.astype(BF16)], axis=0)
+
+    for k in range(0, GROUP, PAIR):
+        lines = side_by_side([line(k + n) for n in range(PAIR)])
+        spectrum = dot(forward_ref[...], twice(lines))
         mixed = dot(ahead_ref[...], twice(filtered(spectrum, factor, False)))
-        mixed_ref[k] = mixed + skip * image_ref[k].astype(F32)
+        for n in range(PAIR):
+            cut = slice(n * chans, (n + 1) * chans)
+            spectrum_ref[k + n] = spectrum[:, cut].astype(BF16)
+            mixed_ref[k + n] = mixed[:, cut] + skip * image_ref[k + n].astype(F32)
 
 
 def cols_grad_kernel(
     own_ref, lags_ref, d_mixed_ref, spectrum_ref, image_ref, sums_ref, totals, skip_total
 ):
     step = pl.program_id(0)
-    half = totals.shape[1]
+    half, chans = totals.shape[1], totals.shape[2]
 
     @pl.when(step == 0)
     def _():
         totals[...] = jnp.zeros(totals.shape, F32)
         skip_total[...] = jnp.zeros(skip_total.shape, F32)
 
-    for k in range(GROUP):
-        d = d_mixed_ref[k]
-        spectrum = dot(own_ref[...], twice(d))
-        real, imag = spectrum[:half], spectrum[half:]
-        other = spectrum_ref[k].astype(F32)
-        other_real, other_imag = other[:half], other[half:]
-        totals[0] += real * other_real
-        totals[1] += imag * other_imag
-        totals[2] += real * other_imag - imag * other_real
-        skip_total[...] += fold(d.astype(F32) * image_ref[k].astype(F32))
+    for k in range(0, GROUP, PAIR):
+        rows = [d_mixed_ref[k + n] for n in range(PAIR)]
+        spectra = dot(own_ref[...], twice(side_by_side(rows)))
+        found = []
+        for n in range(PAIR):
+            spectrum = spectra[:, n * chans : (n + 1) * chans]
+            real, imag = spectrum[:half], spectrum[half:]
+            other = spectrum_ref[k + n].astype(F32)
+            other_real, other_imag = other[:half], other[half:]
+            found.append((real * other_real, imag * other_imag, real * other_imag - imag * other_real))
+            skip_total[...] += fold(rows[n].astype(F32) * image_ref[k + n].astype(F32))
+        for m in range(3):
+            totals[m] += sum(f[m] for f in found[1:]) + found[0][m]
 
     @pl.when(step == pl.num_programs(0) - 1)
     def _():
@@ -282,80 +295,94 @@
         sums_ref[KSIZE : KSIZE + 1] = jnp.sum(skip_total[...], axis=0, keepdims=True)
 
 
+def transformed_back(factor, forward_ref, behind_ref, lines):
+    chans = factor[0].shape[1] // PAIR
+    beside = [jnp.concatenate([near.astype(F32), other.astype(F32)], axis=0).astype(BF16) for _, near, other in lines]
+    wide = side_by_side([jnp.concatenate([line[0], side], axis=0) for line, side in zip(lines, beside)])
+    spectrum = dot(forward_ref[...], twice(wide))
+    some = [f[:, : spectrum.shape[1]] for f in factor]
+    found = dot(behind_ref[...], twice(filtered(spectrum, some, True))).astype(BF16)
+    return [found[:, n * chans : (n + 1) * chans] for n in range(len(lines))]
+
+
+def paired(factor_ref):
+    return [side_by_side([factor_ref[k]] * PAIR) for k in range(3)]
+
+
 def cols_back_kernel(
-    source_ref, factor_ref, forward_ref, behind_ref,
-    centre, row_near, row_other, col_near, col_other, image, image_near, image_other,
-    d_partial_ref, sums_ref, ext, d_partial, row_sums,
+    factor_ref, forward_ref, behind_ref, d_mixed_ref, row_near, col_near, col_other, d_partial_ref, d_near_ref
 ):
-    height, width = centre.shape[0], centre.shape[1]
-    load_rows(ext, source_ref, image, image_near, image_other)
-    batch = 4
-    factor = [jnp.concatenate([factor_ref[k]] * batch, axis=1) for k in range(3)]
-    row_sums[...] = jnp.zeros(row_sums.shape, F32)
-
-    def line(own, one, two):
-        both = jnp.concatenate([one.astype(F32), two.astype(F32)], axis=0).astype(BF16)
-        return jnp.concatenate([own, both], axis=0)
-
-    def transformed(lines):
-        spectrum = dot(forward_ref[...], twice(jnp.concatenate(lines, axis=1)))
-        some = [f[:, : spectrum.shape[1]] for f in factor]
-        return dot(behind_ref[...], twice(filtered(spectrum, some, True)))
-
-    def group(g):
-        found = transformed(
-            [line(centre[r], col_near[r], col_other[r]) for r in (batch * g + k for k in range(batch))]
+    step = pl.program_id(0)
+    height = col_near.shape[0] - REACH
+    factor = paired(factor_ref)
+    for k in range(0, GROUP, PAIR):
+        places = [(k + n, step * GROUP + k + n) for n in range(PAIR)]
+        found = transformed_back(
+            factor, forward_ref, behind_ref, [(d_mixed_ref[i], col_near[at], col_other[at]) for i, at in places]
         )
-        for k in range(batch):
-            row = found[:, k * LANES : (k + 1) * LANES]
-            d_partial[batch * g + k] = row
-            d_partial_ref[REACH + batch * g + k] = row.astype(BF16)
-
-    def grads(g):
-        for k in range(batch):
-            r = batch * g + k
-            d = d_partial[r]
+        for n in range(PAIR):
+            d_partial_ref[k + n] = found[n]
+
+    @pl.when(step == pl.num_programs(0) - 1)
+    def _():
+        for k in range(0, REACH, PAIR):
+            some = range(k, min(k + PAIR, REACH))
+            found = transformed_back(
+                factor, forward_ref, behind_ref,
+                [(row_near[i], col_near[height + i], col_other[height + i]) for i in some],
+            )
+            for i, value in zip(some, found):
+                d_near_ref[i] = value
+
+
+def strip_back_kernel(factor_ref, forward_ref, behind_ref, rows, near, other, d_rows_ref):
+    factor = paired(factor_ref)
+    for k in range(0, REACH, PAIR):
+        some = range(k, min(k + PAIR, REACH))
+        found = transformed_back(
+            factor, forward_ref, behind_ref, [(rows[i], near[i], other[i]) for i in some]
+        )
+        for i, value in zip(some, found):
+            d_rows_ref[i] = value
+
+
+def rows_grad_kernel(source_ref, d_partial_ref, image, near, other, sums_ref, ext):
+    height = d_partial_ref.shape[0]
+    load_rows(ext, source_ref, image, near, other)
+
+    def row(r, totals):
+        totals = list(totals)
+        for k in range(2):
+            at = 2 * r + k
+            d = d_partial_ref[at].astype(F32)
             for i in range(KSIZE):
-                row_sums[i] += fold(d * ext[source_ref[r * KSIZE + i]])
-
-    group(0)
-
-    def both(g, _):
-        group(g)
-        grads(g - 1)
+                totals[i] = totals[i] + fold(d * ext[source_ref[at * KSIZE + i]])
+        return tuple(totals)
+
+    zero = jnp.zeros((8, LANES), F32)
+    totals = lax.fori_loop(0, height // 2, row, (zero,) * KSIZE)
+    for i in range(KSIZE):
+        sums_ref[i : i + 1] = jnp.sum(totals[i], axis=0, keepdims=True)
+    sums_ref[KSIZE : KSIZE + 1] = jnp.zeros((1, LANES), F32)
+
+
+def rows_back_kernel(
+    first, source_ref, taps_ref, skip_ref, d_partial_ref, near, other, d_mixed_ref, grad_ref, *rest
+):
+    image_grad_ref, ext = rest[-2:]
+    count = d_mixed_ref.shape[0]
+    height = d_partial_ref.shape[0]
+    ext[height + 2 * REACH] = jnp.zeros(ext.shape[1:], F32)
+    for i in range(REACH):
+        ext[source_ref[height * KSIZE] + i] = near[i].astype(F32)
+        ext[source_ref[height * KSIZE + 1] + i] = other[i].astype(F32)
+    low, high = max(first - REACH, 0), min(first + count + REACH, height)
+
+    def place(r, _):
+        ext[r + REACH] = d_partial_ref[r].astype(F32)
         return 0
 
-    lax.fori_loop(1, height // batch, both, 0)
-    grads(height // batch - 1)
-    for n, rows in enumerate((row_near, row_other)):
-        to = source_ref[height * KSIZE + n]
-        base = height + n * REACH
-        for at in range(0, REACH, batch):
-            some = range(at, min(at + batch, REACH))
-            found = transformed([line(rows[i], col_near[base + i], col_other[base + i]) for i in some])
-            for k, i in enumerate(some):
-                d_partial_ref[to + i] = found[:, k * LANES : (k + 1) * LANES].astype(BF16)
-    sums_ref[0:KSIZE] = jnp.sum(row_sums[...], axis=1)
-    sums_ref[KSIZE : KSIZE + 1] = jnp.zeros((1, LANES), F32)
-
-
-def rows_back_kernel(source_ref, taps_ref, skip_ref, d_partial_ref, d_mixed_ref, grad_ref, *rest):
-    image_grad_ref, ext = rest[-2:]
-    step = pl.program_id(0)
-    count = d_mixed_ref.shape[0]
-    full = d_partial_ref.shape[0]
-
-    @pl.when(step == 0)
-    def _():
-        ext[full] = jnp.zeros(ext.shape[1:], F32)
-
-        def place(r, _):
-            for k in range(2):
-                ext[2 * r + k] = d_partial_ref[2 * r + k].astype(F32)
-            return 0
-
-        lax.fori_loop(0, full // 2, place, 0)
-
+    lax.fori_loop(low, high, place, 0, unroll=3)
     taps = [taps_ref[0, i][None, :] for i in range(KSIZE)]
     skip = skip_ref[...]
 
@@ -364,8 +391,7 @@
             at = 2 * r + k
             total = grad_ref[at].astype(F32) + skip * d_mixed_ref[at].astype(F32)
             for i in range(KSIZE):
-                place = (step * count + at) * KSIZE + KSIZE - 1 - i
-                total = total + taps[i] * ext[source_ref[place]]
+                total = total + taps[i] * ext[source_ref[(first + at) * KSIZE + KSIZE - 1 - i]]
             image_grad_ref[at] = total.astype(BF16)
         return 0
 
@@ -373,14 +399,13 @@
 
 
 def feed_kernel(
-    mixed_ref, image_ref, grad_ref, w_in_ref, w_out_t_ref, w_in_t_ref, w_out_ref,
-    b_in_ref, vectors_ref,
+    mixed_ref, image_ref, grad_ref, w_in_ref, w_out_ref, b_in_ref, gain_ref, bias_ref, b_out_ref, scale_ref,
     output_ref, d_mixed_ref, weights_ref, b_sums_ref, sums_ref,
     act_ref, d_pre_ref,
 ):
     step = pl.program_id(0)
     chans, hidden = w_in_ref.shape
-    piece = 512
+    piece = 256
 
     @pl.when(step == 0)
     def _():
@@ -388,8 +413,8 @@
         b_sums_ref[...] = jnp.zeros(b_sums_ref.shape, F32)
         sums_ref[...] = jnp.zeros(sums_ref.shape, F32)
 
-    gain, bias = vectors_ref[0:1], vectors_ref[1:2]
-    b_out, scale = vectors_ref[2:3], vectors_ref[3:4]
+    gain, bias, b_out, scale = (ref[...][None, :] for ref in (gain_ref, bias_ref, b_out_ref, scale_ref))
+    b_in = b_in_ref[...][None, :]
     mixed = mixed_ref[...]
     mean = jnp.mean(mixed, axis=-1, keepdims=True)
     centred = mixed - mean
@@ -399,25 +424,25 @@
     normed = (xhat * gain + bias).astype(BF16)
     grad = grad_ref[...].astype(F32)
     d_branch = (scale * grad).astype(BF16)
-    normed_t = normed.T
+    normed_t = jnp.concatenate([normed.T, jnp.ones((16, normed.shape[0]), BF16)], axis=0)
     d_branch_t = d_branch.T
-    ones = jnp.ones((8, normed.shape[0]), BF16)
     for k in range(0, hidden, piece):
         cut = slice(k, k + piece)
-        pre = dot(normed, w_in_ref[:, cut]) + b_in_ref[:, cut]
-        d_act = dot(d_branch, w_out_t_ref[:, cut])
+        pre = dot(normed, w_in_ref[:, cut]) + b_in[:, cut]
+        d_act = dot(d_branch, w_out_ref[cut, :], dims=((1,), (1,)))
         half = 0.5 + 0.5 * lax.erf(pre * 0.7071067811865476)
         bell = jnp.exp(pre * pre * -0.5) * 0.3989422804014327
         act = (pre * half).astype(BF16)
         d_pre = (d_act * (half + pre * bell)).astype(BF16)
         act_ref[:, cut] = act
         d_pre_ref[:, cut] = d_pre
-        weights_ref[0:chans, cut] += dot(normed_t, d_pre)
+        found = dot(normed_t, d_pre)
+        weights_ref[0:chans, cut] += found[:chans]
+        b_sums_ref[:, cut] += found[chans : chans + 8]
         weights_ref[chans : 2 * chans, cut] += dot(d_branch_t, act)
-        b_sums_ref[:, cut] += dot(ones, d_pre)
-    branch = dot(act_ref[...], w_out_ref[...]) + b_out
+    branch = dot(w_out_ref[...], act_ref[...], dims=((0,), (1,))).T + b_out
     output_ref[...] = (image_ref[...].astype(F32) + scale * branch).astype(BF16)
-    d_normed = dot(d_pre_ref[...], w_in_t_ref[...])
+    d_normed = dot(w_in_ref[...], d_pre_ref[...], dims=((1,), (1,))).T
     g = d_normed * gain
     g_mean = jnp.mean(g, axis=-1, keepdims=True)
     g_xhat = jnp.mean(g * xhat, axis=-1, keepdims=True)
@@ -551,13 +576,11 @@
     def ident(r):
         return (r >= first).astype(jnp.int32) + (r >= second).astype(jnp.int32)
 
-    row = jnp.arange(height, dtype=jnp.int32)[:, None]
-    tap = jnp.arange(KSIZE, dtype=jnp.int32)[None, :]
-    source = jnp.where(
-        ident(start + row) == ident(start + row + tap - REACH), row + tap, full
-    ).reshape(-1)
-    base = jnp.where(jnp.arange(2) == lax.axis_index("th") % 2, REACH + height, 0)
-    source = jnp.concatenate([source, base.astype(jnp.int32)])
+    entry = jnp.arange(height * KSIZE + 2, dtype=jnp.int32)
+    row, tap = entry // KSIZE, entry % KSIZE
+    source = jnp.where(ident(start + row) == ident(start + row + tap - REACH), row + tap, full)
+    place = lax.axis_index("th") % 2
+    source = jnp.where(row < height, source, jnp.where(tap == place, REACH + height, 0))
 
     rate_t, freq_t, cr_t, ci_t = (v.transpose(0, 2, 1) for v in (rate_log, freq, coef_re, coef_im))
     zr, zi, step = powers(rate_t, freq_t, log_step[:, None, :])
@@ -602,10 +625,7 @@
             jax.ShapeDtypeStruct(tile_shape, F32),
             jax.ShapeDtypeStruct((height, size, chans), BF16),
         ],
-        scratch_shapes=[
-            pltpu.VMEM((full + 1, 2 * EDGE, chans), F32),
-            pltpu.VMEM((height, 2 * EDGE, chans), BF16),
-        ],
+        scratch_shapes=[pltpu.VMEM((full + 1, 2 * EDGE, chans), F32)],
         compiler_params=params(),
         cost_estimate=cost(14),
         name="cols_forward",
@@ -614,16 +634,14 @@
         col_near, col_other,
     )
 
-    tile = 768
+    tile = 1536
     pixel_block = pl.BlockSpec((tile, chans), lambda i: (i, 0))
-    vectors = jnp.stack([ln_gain, ln_bias, b_out, layer_scale])
     output, d_mixed, weights, b_sums, sums = pl.pallas_call(
         feed_kernel,
         grid=(pixels // tile,),
         in_specs=[
             pixel_block, pixel_block, pixel_block,
-            whole((chans, hidden)), whole((chans, hidden)), whole((hidden, chans)), whole((hidden, chans)),
-            whole((1, hidden)), whole((4, chans)),
+            whole((chans, hidden)), whole((hidden, chans)), whole((hidden,)), *[whole((chans,))] * 4,
         ],
         out_specs=[
             pixel_block, pixel_block, whole((2 * chans, hidden)), whole((8, hidden)), whole((4, 8, chans)),
@@ -641,13 +659,13 @@
         name="feed_forward",
     )(
         mixed.reshape(pixels, chans), image.reshape(pixels, chans), out_grad.reshape(pixels, chans),
-        w_in, w_out.T, w_in.T, w_out, b_in[None, :], vectors,
+        w_in, w_out, b_in, ln_gain, ln_bias, b_out, layer_scale,
     )
     output = output.reshape(tile_shape)
     d_mixed = d_mixed.reshape(tile_shape)
 
     grad_row_near, grad_row_other = halo_rows(d_mixed)
-    grad_col_near, grad_col_other, edges = halo_cols(d_mixed, grad_row_near, grad_row_other)
+    grad_col_near, grad_col_other, edges = halo_cols(d_mixed, grad_row_near)
 
     core, *others = mesh_steps()
     phases = [others[k : k + 2] for k in range(0, len(others), 2)]
@@ -676,91 +694,118 @@
     (col_sums,) = found
 
     def cols_back(sent):
-        both = pl.pallas_call(
-            cols_back_kernel,
+        found.extend(
+            pl.pallas_call(
+                cols_back_kernel,
+                grid=(groups,),
+                in_specs=[
+                    whole((3, half, chans)), whole((size, 2 * size)), whole((width, 2 * size)),
+                    row_block(width, chans), whole((REACH, width, chans)),
+                    whole((full - REACH, EDGE, chans)), whole((full - REACH, EDGE, chans)),
+                ],
+                out_specs=[row_block(width, chans), whole((REACH, width, chans))],
+                out_shape=[
+                    jax.ShapeDtypeStruct(tile_shape, BF16),
+                    jax.ShapeDtypeStruct((REACH, width, chans), BF16),
+                ],
+                compiler_params=params(),
+                cost_estimate=cost(12),
+                name="cols_back",
+            )(
+                factor, forward, behind, tie(d_mixed, *sent), grad_row_near, grad_col_near, grad_col_other,
+            )
+        )
+        return found[1:]
+
+    weights = scatter(tie(weights, col_sums), phases[0], BF16, cols_back)
+    d_partial, d_near = found[1:]
+    grad_near_strip, grad_other_strip, strips = halo_cols(tie(grad_row_other, col_sums))
+
+    def rows_grad(sent):
+        found.append(
+            pl.pallas_call(
+                rows_grad_kernel,
+                grid=(blocks,),
+                in_specs=[
+                    SCALARS, lane_block(height, width), lane_block(height, width),
+                    lane_block(REACH, width), lane_block(REACH, width),
+                ],
+                out_specs=lane_block(KSIZE + 1),
+                out_shape=jax.ShapeDtypeStruct((KSIZE + 1, chans), F32),
+                scratch_shapes=[pltpu.VMEM((full + 1, width, LANES), F32)],
+                compiler_params=params(),
+                cost_estimate=cost(14),
+                name="rows_grad",
+            )(source, tie(d_partial, *sent, *strips), image, row_near, row_other)
+        )
+        return found[-1:]
+
+    weights = scatter(weights, phases[1], F32, rows_grad)
+    row_sums = found[-1]
+    for later in phases[2:]:
+        weights = scatter(weights, later, F32, lambda _: [])
+    small = jnp.concatenate(
+        [
+            tie(row_sums, weights, grad_near_strip, grad_other_strip),
+            col_sums, jnp.sum(sums, axis=1), b_sums[0].reshape(hidden // chans, chans),
+        ],
+        axis=0,
+    )
+    small = small + swap(small, *core)
+    takes = [send(small) for send in exchanges(phases[0])]
+    d_other = pl.pallas_call(
+        strip_back_kernel,
+        out_shape=jax.ShapeDtypeStruct((REACH, width, chans), BF16),
+        compiler_params=params(),
+        cost_estimate=cost(3),
+        name="strip_back",
+    )(tie(factor, small), forward, behind, grad_row_other, grad_near_strip, grad_other_strip)
+    small = sum([tie(take, d_other) for take in takes], small)
+
+    def rows_back(part, before, *waits):
+        count = height // 2
+        at = pl.BlockSpec((count, width, LANES), lambda c: (part, 0, c))
+        return pl.pallas_call(
+            functools.partial(rows_back_kernel, part * count),
             grid=(blocks,),
             in_specs=[
-                SCALARS, lane_block(3, half), whole((size, 2 * size)), whole((width, 2 * size)),
-                lane_block(height, width), lane_block(REACH, width), lane_block(REACH, width),
-                lane_block(full, EDGE), lane_block(full, EDGE),
-                lane_block(height, width), lane_block(REACH, width), lane_block(REACH, width),
-            ],
-            out_specs=[lane_block(full, width), lane_block(KSIZE + 1)],
-            out_shape=[
-                jax.ShapeDtypeStruct((full, width, chans), BF16),
-                jax.ShapeDtypeStruct((KSIZE + 1, chans), F32),
-            ],
-            scratch_shapes=[
-                pltpu.VMEM((full + 1, width, LANES), F32),
-                pltpu.VMEM((height, width, LANES), F32),
-                pltpu.VMEM((KSIZE, 8, LANES), F32),
-            ],
-            compiler_params=params(),
-            cost_estimate=cost(20),
-            name="cols_back",
-        )(
-            source, factor, forward, behind, tie(d_mixed, *sent), grad_row_near, grad_row_other,
-            grad_col_near, grad_col_other, image, row_near, row_other,
-        )
-        found.extend(both)
-        return both
-
-    weights = scatter(weights, phases[0], BF16, cols_back)
-    _, d_partial, row_sums = found
-
-    small = jnp.concatenate(
-        [row_sums, col_sums, jnp.sum(sums, axis=1), b_sums[0].reshape(hidden // chans, chans)], axis=0
-    )
-
-    def rows_back(block, before, *waits):
-        at = pl.BlockSpec((height // 4, width, LANES), lambda r: (r, 0, block))
-        lanes = lambda *lead: pl.BlockSpec((*lead, LANES), lambda r: (0,) * len(lead) + (block,))
-        return pl.pallas_call(
-            rows_back_kernel,
-            grid=(4,),
-            in_specs=[
-                SCALARS, lanes(2, KSIZE + 1), lanes(1), lanes(full, width), at, at,
+                SCALARS, lane_block(2, KSIZE + 1), lane_block(1), lane_block(height, width),
+                lane_block(REACH, width), lane_block(REACH, width), at, at,
                 *([] if before is None else [pl.BlockSpec(memory_space=pl.ANY)]),
             ],
             out_specs=at,
             out_shape=jax.ShapeDtypeStruct(tile_shape, BF16),
             scratch_shapes=[pltpu.VMEM((full + 1, width, LANES), F32)],
             compiler_params=params(),
-            cost_estimate=cost(6),
-            input_output_aliases={} if before is None else {6: 0},
+            cost_estimate=cost(8),
+            input_output_aliases={} if before is None else {8: 0},
             name="rows_back",
         )(
-            source, taps, tie(skip_row, *waits), d_partial, d_mixed, out_grad,
+            source, taps, tie(skip_row, *waits), d_partial, d_near, d_other, d_mixed, out_grad,
             *([] if before is None else [before]),
         )
 
-    small = small + swap(small, *core)
-    waiting = list(phases)
-
-    def beside(block, before):
+    weights = weights.astype(BF16)
+    backwards = list(reversed(phases))
+    early, *late = others[2:]
+
+    def beside(part, *before):
         def work(sent):
-            nonlocal small
-            takes = []
-            if waiting:
-                takes = [send(small) for send in exchanges(waiting.pop(0))]
-            some = rows_back(block, before, *sent, small)
-            for take in takes:
-                small = small + tie(take, some)
-            found.append(some)
-            return [some]
+            found.append(rows_back(part, *(before or [None]), *sent, small))
+            return found[-1:]
 
         return work
 
-    for n, later in enumerate(phases[1:]):
-        weights = scatter(weights, later, F32, beside(0, None) if n == 0 else lambda _: [])
-    weights = weights.astype(BF16)
-    for n, later in enumerate(reversed(phases[1:])):
-        weights = gather(weights, later, beside(1, found[-1]) if n == 0 else lambda _: [])
-    for later in waiting:
-        small = sum([send(small) for send in exchanges(later)], small)
-    waiting.clear()
-    weights = gather(tie(weights, small), phases[0], beside(2, found[-1]))
+    take = swap(small, *early)
+    for n, later in enumerate(backwards[:-1]):
+        weights = gather(weights, later, beside(0) if n == 0 else lambda _: [])
+    small = small + tie(take, found[-1])
+    for later in late[:-1]:
+        small = small + swap(small, *later)
+    take = swap(small, *late[-1])
+    weights = gather(weights, phases[0], beside(1, found[-1]))
     image_grad = found[-1]
+    small = small + tie(take, image_grad)
     cut = hidden // 4
     half_block = pl.BlockSpec((chans, cut), lambda k: (0, k))
     d_win, d_wout = pl.pallas_call(

time: 285 us -> 249 us (0.87)
  Pallas kernels: 188 us -> 158 us
  waiting for transfers between devices: 8.18 us -> 14.3 us
  local copies, waits for them, and re-layouts: 20.9 us -> 16.5 us
  starting transfers between devices: 49.4 us -> 45 us
  other arithmetic: 15.3 us -> 11.2 us
    pallas_call x1, Pallas kernels: 75.5 us -> 63.8 us  [per_device(): pl.pallas_call(feed_kernel, grid=(pixels // tile,), in_specs=[pixel_block...]
    pallas_call x1, Pallas kernels: 22.1 us -> 13.5 us  [per_device(): pl.pallas_call(cols_kernel, grid=(groups,), in_specs=[SCALARS, whole((2,...]
    pallas_call x4 -> x5, Pallas kernels: 56.7 us -> 48.9 us  [the longest x2 19.4 us: rows_back(): pl.pallas_call(functools.partial(rows_back_kernel, part * count), grid=(b...]
    ppermute x22, waiting for transfers between devices: 8.16 us -> 14.2 us  [swap(): return lax.ppermute(block, axis, [(i, i ^ bit) for i in range(count)])]
    ppermute x22, starting transfers between devices: 40 us -> 36.3 us  [swap(): return lax.ppermute(block, axis, [(i, i ^ bit) for i in range(count)])]
    concatenate x6 -> x5, other arithmetic: 5.6 us -> 2.7 us  [the longest x4 1.94 us: edge(): return jnp.concatenate(parts, axis=0)]
  transfers between devices with their start and end apart: 29 -> 30, of which waited for: 3 -> 6; matrix products, arithmetic and copies ran while one was open for 10% -> 7% of each run, Pallas kernels for 30% -> 31%
where the time goes in v3:
time: 249 us; the launch traced here: 248 us
  Pallas kernels  158 us (63%)
  starting transfers between devices  45 us (18%)
  local copies, waits for them, and re-layouts  16.5 us (7%)
  waiting for transfers between devices  14.3 us (6%)
  other arithmetic  11.2 us (4%)
    pallas_call x1, Pallas kernels, per_device(): pl.pallas_call(feed_kernel, grid=(pixels // tile,), in_specs=[pixel_block...  63.8 us
    ppermute x22, starting transfers between devices, swap(): return lax.ppermute(block, axis, [(i, i ^ bit) for i in range(count)])  36.3 us
    pallas_call x2, Pallas kernels, rows_back(): pl.pallas_call(functools.partial(rows_back_kernel, part * count), grid=(b...  19.4 us
    pallas_call x1, Pallas kernels, rows_grad(): pl.pallas_call(rows_grad_kernel, grid=(blocks,), in_specs=[SCALARS, lane_...  14.3 us
    ppermute x22, waiting for transfers between devices, swap(): return lax.ppermute(block, axis, [(i, i ^ bit) for i in range(count)])  14.2 us
    pallas_call x1, Pallas kernels, per_device(): pl.pallas_call(rows_kernel, grid=(blocks,), in_specs=[SCALARS, lane_block...  14 us
    pallas_call x1, Pallas kernels, per_device(): pl.pallas_call(cols_kernel, grid=(groups,), in_specs=[SCALARS, whole((2,...  13.5 us
    pallas_call x1, Pallas kernels, cols_back(): pl.pallas_call(cols_back_kernel, grid=(groups,), in_specs=[whole((3, half...  12.2 us
  transfers between devices with their start and end apart: 30, of which 6 were waited for; matrix products, arithmetic and copies ran while one was open for 7% of the time, Pallas kernels for 31%

profile of v3, /device:TPU:0, one launch (start us, length us, event | category | flops | bytes accessed | tf_op | source)
XLA Modules:
  0.0 247.8 jit_solution(9412690067025904933)
XLA Ops:
  0.7 1.3 constant_dynamic-slice_fusion.18
  4.0 1.2 constant_dynamic-slice_fusion.14
  5.3 1.1 sine_multiply_fusion
  6.5 2.6 %collective-permute-start.2 = (bf16[78,8,384]{2,1,0:T(8,128)(2,1)S(1)}, bf16[78,8,384]{2,1,0:T(8,128)(2,1)S(1)}, u32[]{:S(2)}, u32[]{:S(2)}) collective-permute-start(bf16[78,8,384]{2,1,0:T(8,128)(2,1)S(1)} %pad_maximum_fusion.1), channel_id=1, source_target_pairs={{0,1},{1,0},{2,3},{3,2},{4,5},{5,4},{6,7},{7,6},{8,9},{9,8},{10,11... | collective-permute-start | bytes 1437704 | tf_op jit(solution)/shard_map/ppermute | solution.py:24
  12.3 2.6 %taps.1 = (f32[2,16,384]{2,1,0:T(8,128)}, f32[3,56,384]{2,1,0:T(8,128)}) custom-call(f32[2,32,384]{2,1,0:T(8,128)} %get-tuple-element.139.zr_ref, f32[2,32,384]{2,1,0:T(8,128)} %get-tuple-element.138.zi_ref, f32[2,32,384]{2,1,0:T(8,128)} %bitcast.30, f32[2,32,384]{2,1,0:T(8,128)} %bitcast.32, f32[168,16]{1,0:T(8,128)} %constant.158.clone.response_ref), custom_call_target="tpu_custom_call" | custom-call | tf_op jit(solution)/shard_map/taps/pallas_call | solution.py:588
  15.0 1.3 fusion.11.source_ref
  16.9 14.0 %rows_forward.1.partial_ref = bf16[64,96,384]{2,1,0:T(8,128)(2,1)} custom-call(s32[962]{0:T(1024)} %fusion.11.source_ref, f32[2,16,384]{2,1,0:T(8,128)} %get-tuple-element.59.taps_ref, bf16[64,96,384]{2,1,0:T(8,128)(2,1)} %image.1, bf16[7,96,384]{2,1,0:T(8,128)(2,1)} %copy-done.1, bf16[7,96,384]{2,1,0:T(8,128)(2,1)} %copy-done.2), custom_call_target="tpu_custom_call" | custom-call | flops 1400000000 | bytes 1400000 | tf_op jit(solution)/shard_map/rows_forward/pallas_call | solution.py:599
  31.8 13.5 %cols_forward.1 = (f32[64,96,384]{2,1,0:T(8,128)}, bf16[64,112,384]{2,1,0:T(8,128)(2,1)}) custom-call(s32[962]{0:T(1024)} %fusion.11.source_ref, f32[2,16,384]{2,1,0:T(8,128)} %get-tuple-element.59.taps_ref, f32[1,384]{1,0:T(1,128)} %broadcast_in_dim.19.skip_ref, f32[3,56,384]{2,1,0:T(8,128)} %get-tuple-element.82.factor_ref, ...), custom_call_target="tpu_custom_call" | custom-call | flops 1400000000 | bytes 1400000 | tf_op jit(solution)/shard_map/cols_forward/pallas_call | solution.py:614
  45.2 63.8 %feed_forward.1 = (bf16[6144,384]{1,0:T(8,128)(2,1)}, bf16[6144,384]{1,0:T(8,128)(2,1)}, f32[768,1536]{1,0:T(8,128)}, f32[8,1536]{1,0:T(8,128)}, f32[4,8,384]{2,1,0:T(8,128)}) custom-call(f32[6144,384]{1,0:T(8,128)} %bitcast.34, bf16[6144,384]{1,0:T(8,128)(2,1)} %bitcast.26, bf16[6144,384]{1,0:T(8,128)(2,1)} %bitcast.27, bf16[384,1536]{1,0:T(8,128)(2,1)} %w_in_ref.1, ...), custom_call_target="tpu_custom_call" | custom-call | flops 7000000000 | bytes 7000000 | tf_op jit(solution)/shard_map/feed_forward/pallas_call | solution.py:639
  109.0 1.8 constant_dynamic-slice_fusion.11
  110.9 7.2 %collective-permute-start.4 = (f32[384,1536]{1,0:T(8,128)S(1)}, f32[384,1536]{1,0:T(8,128)}, u32[]{:S(2)}, u32[]{:S(2)}) collective-permute-start(f32[384,1536]{1,0:T(8,128)S(1)} %constant_dynamic-slice_fusion.11), channel_id=1, source_target_pairs={{0,8},{8,0},{16,24},{24,16},{1,9},{9,1},{17,25},{25,17},{2,10},{10... | collective-permute-start | bytes 7077896 | tf_op jit(solution)/shard_map/ppermute | solution.py:24
  118.0 2.2 constant_dynamic-slice_fusion.2
  121.0 1.2 constant_dynamic-slice_fusion.7
  122.2 0.9 collective-permute-done.5.row_near
  123.2 1.0 pad_maximum_fusion.4
  124.1 1.4 collective-permute-start.8
  125.6 0.8 pad_maximum_fusion.3
  126.4 4.7 %collective-permute-start.7 = (bf16[71,8,384]{2,1,0:T(8,128)(2,1)}, bf16[71,8,384]{2,1,0:T(8,128)(2,1)}, u32[]{:S(2)}, u32[]{:S(2)}) collective-permute-start(bf16[71,8,384]{2,1,0:T(8,128)(2,1)} %pad_maximum_fusion.3), channel_id=1, source_target_pairs={{0,1},{1,0},{2,3},{3,2},{4,5},{5,4},{6,7},{7,6},{8,9},{9,8},{10,11... | collective-permute-start | bytes 1308680 | tf_op jit(solution)/shard_map/ppermute | solution.py:24
  131.1 8.6 %cols_grad.1 = f32[16,384]{1,0:T(8,128)} custom-call(bf16[112,192]{1,0:T(8,128)(2,1)} %constant.160.clone.own_ref, f32[16,168]{1,0:T(8,128)} %constant.161.clone.lags_ref, bf16[64,96,384]{2,1,0:T(8,128)(2,1)} %bitcast.22, bf16[64,112,384]{2,1,0:T(8,128)(2,1)} %get-tuple-element.66.spectrum_ref, bf16[64,96,384]{2,1,0:T(8,128)(2,1)} %image.1), custom_call_target="tpu_custom_call" | custom-call | flops 800000000 | bytes 800000 | tf_op jit(solution)/shard_map/cols_grad/pallas_call | solution.py:676
  139.8 2.8 %dynamic-slice_add_fusion = f32[384,1536]{1,0:T(8,128)S(1)} fusion(f32[384,1536]{1,0:T(8,128)} %collective-permute-done.4, f32[768,1536]{1,0:T(8,128)} %get-tuple-element.63, s32[]{:T(128)S(6)} %select_n.295), kind=kLoop, calls=%fused_computation | loop fusion | flops 589824 | bytes 7077892 | tf_op jit(solution)/shard_map/add | solution.py:523
  142.5 1.0 dynamic-slice_convert_fusion.1
  143.5 2.4 collective-permute-start.6
  145.9 1.5 collective-permute-start.10
  147.4 0.8 slice_reduce_fusion
  148.3 2.6 %collective-permute-done.7.col_near = bf16[71,8,384]{2,1,0:T(8,128)(2,1)} collective-permute-done((bf16[71,8,384]{2,1,0:T(8,128)(2,1)}, bf16[71,8,384]{2,1,0:T(8,128)(2,1)}, u32[]{:S(2)}, u32[]{:S(2)}) %collective-permute-start.7) | collective-permute-done | bytes 436256 | tf_op jit(solution)/shard_map/ppermute | solution.py:24
  150.9 12.2 %cols_back.1 = (bf16[64,96,384]{2,1,0:T(8,128)(2,1)}, bf16[7,96,384]{2,1,0:T(8,128)(2,1)}) custom-call(f32[3,56,384]{2,1,0:T(8,128)} %get-tuple-element.82.factor_ref, bf16[112,224]{1,0:T(8,128)(2,1)} %broadcast_select_fusion.forward_ref, bf16[96,224]{1,0:T(8,128)(2,1)} %constant.162.clone.behind_ref, bf16[64,96,384]{2,1,0:T(8,128)(2,1)} %bitcast.23, ...), custom_call_target="tpu_custom_call" | custom-call | flops 1200000000 | bytes 1200000 | tf_op jit(solution)/shard_map/cols_back/pallas_call | solution.py:698
  164.6 1.3 convert_add_fusion
  165.9 1.6 collective-permute-start.11
  167.5 2.4 collective-permute-start.13
  170.4 2.6 %collective-permute-start.16 = (bf16[7,8,384]{2,1,0:T(8,128)(2,1)S(1)}, bf16[7,8,384]{2,1,0:T(8,128)(2,1)S(1)}, u32[]{:S(2)}, u32[]{:S(2)}) collective-permute-start(bf16[7,8,384]{2,1,0:T(8,128)(2,1)S(1)} %get-tuple-element.127), channel_id=1, source_target_pairs={{0,1},{1,0},{2,3},{3,2},{4,5},{5,4},{6,7},{7,6},{8,9},{9,8},{10,11... | collective-permute-start | bytes 129032 | tf_op jit(solution)/shard_map/ppermute | solution.py:24
  172.9 0.8 collective-permute-start.17
  173.7 14.3 %rows_grad.1 = f32[16,384]{1,0:T(8,128)} custom-call(s32[962]{0:T(1024)} %fusion.11.source_ref, bf16[64,96,384]{2,1,0:T(8,128)(2,1)} %get-tuple-element.75.d_partial_ref, bf16[64,96,384]{2,1,0:T(8,128)(2,1)} %image.1, bf16[7,96,384]{2,1,0:T(8,128)(2,1)} %copy-done.1, bf16[7,96,384]{2,1,0:T(8,128)(2,1)} %copy-done.2), custom_call_target="tpu_custom_call" | custom-call | flops 1400000000 | bytes 1400000 | tf_op jit(solution)/shard_map/rows_grad/pallas_call | solution.py:726
  188.9 1.2 collective-permute-done.18
  190.9 1.1 collective-permute-start.19
  192.0 3.4 %collective-permute-start.20 = (f32[40,384]{1,0:T(8,128)S(1)}, f32[40,384]{1,0:T(8,128)S(1)}, u32[]{:S(2)}, u32[]{:S(2)}) collective-permute-start(f32[40,384]{1,0:T(8,128)S(1)} %fusion.13), channel_id=1, source_target_pairs={{0,1},{1,0},{2,3},{3,2},{4,5},{5,4},{6,7},{7,6},{8,9},{9,8},{10,11... | collective-permute-start | bytes 184328 | tf_op jit(solution)/shard_map/ppermute | solution.py:24
  195.8 2.4 collective-permute-start.23
  198.4 3.0 %strip_back.1.other = bf16[7,96,384]{2,1,0:T(8,128)(2,1)} custom-call(f32[3,56,384]{2,1,0:T(8,128)} %get-tuple-element.82.factor_ref, bf16[112,224]{1,0:T(8,128)(2,1)} %broadcast_select_fusion.forward_ref, bf16[96,224]{1,0:T(8,128)(2,1)} %constant.162.clone.behind_ref, bf16[7,96,384]{2,1,0:T(8,128)(2,1)} %copy-done.4, bf16[7,8,384]{2,1,0:T(8,128)(2,1)} %copy-done.16, ...), custom_call_target="tpu_custom_call" | custom-call | flops 300000000 | bytes 300000 | tf_op jit(solution)/shard_map/strip_back/pallas_call | solution.py:756
  201.4 1.8 collective-permute-start.15
  203.2 9.7 %rows_back.2.rest_0_ = bf16[64,96,384]{2,1,0:T(8,128)(2,1)} custom-call(s32[962]{0:T(1024)} %fusion.11.source_ref, f32[2,16,384]{2,1,0:T(8,128)} %get-tuple-element.59.taps_ref, f32[1,384]{1,0:T(1,128)} %broadcast_in_dim.19.skip_ref, bf16[64,96,384]{2,1,0:T(8,128)(2,1)} %get-tuple-element.75.d_partial_ref, bf16[7,96,384]{2,1,0:T(8,128)(2,1)} %get-tuple-element.70.near, ...), custom_call_target="tpu_custom_call" | custom-call | flops 800000000 | bytes 800000 | tf_op jit(solution)/shard_map/rows_back/pallas_call | solution.py:768
  213.0 2.5 %collective-permute-start.28 = (bf16[96,1536]{1,0:T(8,128)(2,1)S(1)}, bf16[96,1536]{1,0:T(8,128)(2,1)S(1)}, u32[]{:S(2)}, u32[]{:S(2)}) collective-permute-start(bf16[96,1536]{1,0:T(8,128)(2,1)S(1)} %pad_maximum_fusion.5), channel_id=1, source_target_pairs={{0,17},{1,16},{2,19},{3,18},{4,21},{5,20},{6,23},{7,22},{8,25},{9,... | collective-permute-start | bytes 884744 | tf_op jit(solution)/shard_map/ppermute | solution.py:496
  215.5 1.0 collective-permute-start.27
  217.3 3.5 %collective-permute-done.24 = f32[40,384]{1,0:T(8,128)S(1)} collective-permute-done((f32[40,384]{1,0:T(8,128)S(1)}, f32[40,384]{1,0:T(8,128)S(1)}, u32[]{:S(2)}, u32[]{:S(2)}) %collective-permute-start.24) | collective-permute-done | bytes 61472 | tf_op jit(solution)/shard_map/ppermute | solution.py:24
  220.8 9.7 %rows_back.3 = bf16[64,96,384]{2,1,0:T(8,128)(2,1)} custom-call(s32[962]{0:T(1024)} %fusion.11.source_ref, f32[2,16,384]{2,1,0:T(8,128)} %get-tuple-element.59.taps_ref, f32[1,384]{1,0:T(1,128)} %broadcast_in_dim.19.skip_ref, bf16[64,96,384]{2,1,0:T(8,128)(2,1)} %get-tuple-element.75.d_partial_ref, ...), custom_call_target="tpu_custom_call", output_to_operand_aliasing={{}: (8, {})} | custom-call | flops 800000000 | bytes 800000 | tf_op jit(solution)/shard_map/rows_back/pallas_call | solution.py:768
  231.2 1.2 collective-permute-start.25
  232.3 5.5 %collective-permute-done.25 = f32[40,384]{1,0:T(8,128)S(1)} collective-permute-done((f32[40,384]{1,0:T(8,128)S(1)}, f32[40,384]{1,0:T(8,128)S(1)}, u32[]{:S(2)}, u32[]{:S(2)}) %collective-permute-start.25) | collective-permute-done | bytes 61472 | tf_op jit(solution)/shard_map/ppermute | solution.py:24
  239.1 2.5 %taps_grad.1 = (f32[2,32,384]{2,1,0:T(8,128)}, f32[2,32,384]{2,1,0:T(8,128)}, f32[2,32,384]{2,1,0:T(8,128)}, f32[2,32,384]{2,1,0:T(8,128)}, f32[2,384]{1,0:T(2,128)}) custom-call(f32[2,32,384]{2,1,0:T(8,128)} %get-tuple-element.139.zr_ref, f32[2,32,384]{2,1,0:T(8,128)} %get-tuple-element.138.zi_ref, f32[2,32,384]{2,1,0:T(8,128)} %bitcast.31, ...), custom_call_target="tpu_custom_call" | custom-call | tf_op jit(solution)/shard_map/taps_grad/pallas_call | solution.py:830
  242.2 1.0 copy-done.3
  243.2 4.5 %weight_grads.1 = (f32[384,1536]{1,0:T(8,128)}, f32[1536,384]{1,0:T(8,128)}) custom-call(s32[1]{0:T(128)} %bitcast.15.side_ref, bf16[384,1536]{1,0:T(8,128)(2,1)} %copy-done, bf16[384,1536]{1,0:T(8,128)(2,1)} %copy-done.3), custom_call_target="tpu_custom_call" | custom-call | flops 300000000 | bytes 300000 | tf_op jit(solution)/shard_map/weight_grads/pallas_call | solution.py:811
  (107 shorter events, 13.7 us)
Async XLA Ops:
  0.6 4.6 %copy-start.9 = (f32[2,384,32]{1,2,0:T(8,128)S(1)}, f32[2,384,32]{1,2,0:T(8,128)}, u32[]{:S(2)}) copy-start(f32[2,384,32]{1,2,0:T(8,128)} %param.25) | copy-start | bytes 294916
  0.7 4.6 %copy-start.8 = (f32[2,384,32]{1,2,0:T(8,128)S(1)}, f32[2,384,32]{1,2,0:T(8,128)}, u32[]{:S(2)}) copy-start(f32[2,384,32]{1,2,0:T(8,128)} %param.26) | copy-start | bytes 294916
  2.0 7.8 %copy-start.20 = (s32[3]{0:T(128)S(1)}, s32[3]{0:T(128)}, u32[]{:S(2)}) copy-start(s32[3]{0:T(128)} %param.24) | copy-start | bytes 40
  2.1 8.4 %copy-start.19 = (f32[384]{0:T(512)S(1)}, f32[384]{0:T(512)}, u32[]{:S(2)}) copy-start(f32[384]{0:T(512)} %param.30) | copy-start | bytes 4612
  2.1 4.3 %collective-permute-start = (bf16[7,96,384]{2,1,0:T(8,128)(2,1)S(1)}, bf16[7,96,384]{2,1,0:T(8,128)(2,1)S(1)}, u32[]{:S(2)}, u32[]{:S(2)}) collective-permute-start(bf16[7,96,384]{2,1,0:T(8,128)(2,1)S(1)} %get-tuple-element.115), channel_id=1, source_target_pairs={{0,8},{8,0},{16,24},{24,16},{1,9},{9,1},{17,25},{25,17},{2,10},{10... | collective-permute-start | bytes 1548296 | tf_op jit(solution)/shard_map/ppermute | solution.py:24
  2.6 3.8 %collective-permute-start.1 = (bf16[7,96,384]{2,1,0:T(8,128)(2,1)S(1)}, bf16[7,96,384]{2,1,0:T(8,128)(2,1)S(1)}, u32[]{:S(2)}, u32[]{:S(2)}) collective-permute-start(bf16[7,96,384]{2,1,0:T(8,128)(2,1)S(1)} %get-tuple-element.114), channel_id=1, source_target_pairs={{8,16},{16,8},{9,17},{17,9},{10,18},{18,10},{11,19},{19,11},{12,20... | collective-permute-start | bytes 1548296 | tf_op jit(solution)/shard_map/ppermute | solution.py:30
  4.0 11.0 %copy-start.18 = (f32[2,384]{1,0:T(2,128)}, f32[2,384]{1,0:T(2,128)S(1)}, u32[]{:S(2)}) copy-start(f32[2,384]{1,0:T(2,128)S(1)} %exp.11.step_ref) | copy-start | bytes 9220
  4.0 12.2 %copy-start.13 = (bf16[112,224]{1,0:T(8,128)(2,1)S(1)}, bf16[112,224]{1,0:T(8,128)(2,1)}, u32[]{:S(2)}) copy-start(bf16[112,224]{1,0:T(8,128)(2,1)} %constant.156.clone) | copy-start | bytes 150532
  4.0 12.2 %copy-start.14 = (bf16[112,224]{1,0:T(8,128)(2,1)S(1)}, bf16[112,224]{1,0:T(8,128)(2,1)}, u32[]{:S(2)}) copy-start(bf16[112,224]{1,0:T(8,128)(2,1)} %constant.157.clone) | copy-start | bytes 150532
  6.3 10.5 %copy-start.1 = (bf16[7,96,384]{2,1,0:T(8,128)(2,1)}, bf16[7,96,384]{2,1,0:T(8,128)(2,1)S(1)}, u32[]{:S(2)}) copy-start(bf16[7,96,384]{2,1,0:T(8,128)(2,1)S(1)} %collective-permute-done.near) | copy-start | bytes 1548292
  6.4 10.5 %copy-start.2 = (bf16[7,96,384]{2,1,0:T(8,128)(2,1)}, bf16[7,96,384]{2,1,0:T(8,128)(2,1)S(1)}, u32[]{:S(2)}) copy-start(bf16[7,96,384]{2,1,0:T(8,128)(2,1)S(1)} %collective-permute-done.1.other) | copy-start | bytes 1548292
  6.5 24.3 %collective-permute-start.2 = (bf16[78,8,384]{2,1,0:T(8,128)(2,1)S(1)}, bf16[78,8,384]{2,1,0:T(8,128)(2,1)S(1)}, u32[]{:S(2)}, u32[]{:S(2)}) collective-permute-start(bf16[78,8,384]{2,1,0:T(8,128)(2,1)S(1)} %pad_maximum_fusion.1), channel_id=1, source_target_pairs={{0,1},{1,0},{2,3},{3,2},{4,5},{5,4},{6,7},{7,6},{8,9},{9,8},{10,11... | collective-permute-start | bytes 1437704 | tf_op jit(solution)/shard_map/ppermute | solution.py:24
  9.2 21.7 %collective-permute-start.3 = (bf16[78,8,384]{2,1,0:T(8,128)(2,1)S(1)}, bf16[78,8,384]{2,1,0:T(8,128)(2,1)S(1)}, u32[]{:S(2)}, u32[]{:S(2)}) collective-permute-start(bf16[78,8,384]{2,1,0:T(8,128)(2,1)S(1)} %pad_maximum_fusion.2), channel_id=1, source_target_pairs={{1,2},{3,4},{5,6},{2,1},{4,3},{6,5},{9,10},{11,12},{13,14},{10,9},... | collective-permute-start | bytes 1437704 | tf_op jit(solution)/shard_map/ppermute | solution.py:30
  30.8 0.9 copy-start.7
  110.9 28.9 %collective-permute-start.4 = (f32[384,1536]{1,0:T(8,128)S(1)}, f32[384,1536]{1,0:T(8,128)}, u32[]{:S(2)}, u32[]{:S(2)}) collective-permute-start(f32[384,1536]{1,0:T(8,128)S(1)} %constant_dynamic-slice_fusion.11), channel_id=1, source_target_pairs={{0,8},{8,0},{16,24},{24,16},{1,9},{9,1},{17,25},{25,17},{2,10},{10... | collective-permute-start | bytes 7077896 | tf_op jit(solution)/shard_map/ppermute | solution.py:24
  120.3 2.9 %collective-permute-start.5 = (bf16[7,96,384]{2,1,0:T(8,128)(2,1)}, bf16[7,96,384]{2,1,0:T(8,128)(2,1)S(1)}, u32[]{:S(2)}, u32[]{:S(2)}) collective-permute-start(bf16[7,96,384]{2,1,0:T(8,128)(2,1)} %get-tuple-element.109), channel_id=1, source_target_pairs={{0,8},{8,0},{16,24},{24,16},{1,9},{9,1},{17,25},{25,17},{2,10},{10... | collective-permute-start | bytes 1548296 | tf_op jit(solution)/shard_map/ppermute | solution.py:24
  120.3 25.6 %collective-permute-start.12 = (bf16[7,96,384]{2,1,0:T(8,128)(2,1)}, bf16[7,96,384]{2,1,0:T(8,128)(2,1)S(1)}, u32[]{:S(2)}, u32[]{:S(2)}) collective-permute-start(bf16[7,96,384]{2,1,0:T(8,128)(2,1)} %get-tuple-element.108), channel_id=1, source_target_pairs={{8,16},{16,8},{9,17},{17,9},{10,18},{18,10},{11,19},{19,11},{12,20... | collective-permute-start | bytes 1548296 | tf_op jit(solution)/shard_map/ppermute | solution.py:30
  123.2 16.6 %copy-start.5 = (bf16[7,96,384]{2,1,0:T(8,128)(2,1)}, bf16[7,96,384]{2,1,0:T(8,128)(2,1)S(1)}, u32[]{:S(2)}) copy-start(bf16[7,96,384]{2,1,0:T(8,128)(2,1)S(1)} %collective-permute-done.5.row_near) | copy-start | bytes 1548292
  124.1 24.1 %collective-permute-start.8 = (bf16[71,8,384]{2,1,0:T(8,128)(2,1)}, bf16[71,8,384]{2,1,0:T(8,128)(2,1)}, u32[]{:S(2)}, u32[]{:S(2)}) collective-permute-start(bf16[71,8,384]{2,1,0:T(8,128)(2,1)} %pad_maximum_fusion.4), channel_id=1, source_target_pairs={{1,2},{3,4},{5,6},{2,1},{4,3},{6,5},{9,10},{11,12},{13,14},{10,9},... | collective-permute-start | bytes 1308680 | tf_op jit(solution)/shard_map/ppermute | solution.py:30
  126.4 24.5 %collective-permute-start.7 = (bf16[71,8,384]{2,1,0:T(8,128)(2,1)}, bf16[71,8,384]{2,1,0:T(8,128)(2,1)}, u32[]{:S(2)}, u32[]{:S(2)}) collective-permute-start(bf16[71,8,384]{2,1,0:T(8,128)(2,1)} %pad_maximum_fusion.3), channel_id=1, source_target_pairs={{0,1},{1,0},{2,3},{3,2},{4,5},{5,4},{6,7},{7,6},{8,9},{9,8},{10,11... | collective-permute-start | bytes 1308680 | tf_op jit(solution)/shard_map/ppermute | solution.py:24
  139.8 8.5 %copy-start.15 = (f32[4,8,384]{2,1,0:T(8,128)S(1)}, f32[4,8,384]{2,1,0:T(8,128)}, u32[]{:S(2)}) copy-start(f32[4,8,384]{2,1,0:T(8,128)} %get-tuple-element.80) | copy-start | bytes 147460
  143.5 19.6 %collective-permute-start.6 = (bf16[96,1536]{1,0:T(8,128)(2,1)}, bf16[96,1536]{1,0:T(8,128)(2,1)S(1)}, u32[]{:S(2)}, u32[]{:S(2)}) collective-permute-start(bf16[96,1536]{1,0:T(8,128)(2,1)} %get-tuple-element.118), channel_id=1, source_target_pairs={{0,16},{8,24},{16,0},{24,8},{1,17},{9,25},{17,1},{25,9},{2,18},{10... | collective-permute-start | bytes 884744 | tf_op jit(solution)/shard_map/ppermute | solution.py:24
  145.9 17.6 %collective-permute-start.9 = (bf16[96,1536]{1,0:T(8,128)(2,1)}, bf16[96,1536]{1,0:T(8,128)(2,1)S(1)}, u32[]{:S(2)}, u32[]{:S(2)}) collective-permute-start(bf16[96,1536]{1,0:T(8,128)(2,1)} %get-tuple-element.116), channel_id=1, source_target_pairs={{0,1},{1,0},{2,3},{3,2},{4,5},{5,4},{6,7},{7,6},{8,9},{9,8},{10,11... | collective-permute-start | bytes 884744 | tf_op jit(solution)/shard_map/ppermute | solution.py:24
  145.9 24.4 %copy-start.4 = (bf16[7,96,384]{2,1,0:T(8,128)(2,1)}, bf16[7,96,384]{2,1,0:T(8,128)(2,1)S(1)}, u32[]{:S(2)}) copy-start(bf16[7,96,384]{2,1,0:T(8,128)(2,1)S(1)} %collective-permute-done.12.rows) | copy-start | bytes 1548292
  145.9 18.6 %collective-permute-start.10 = (bf16[96,1536]{1,0:T(8,128)(2,1)}, bf16[96,1536]{1,0:T(8,128)(2,1)}, u32[]{:S(2)}, u32[]{:S(2)}) collective-permute-start(bf16[96,1536]{1,0:T(8,128)(2,1)} %get-tuple-element.117), channel_id=1, source_target_pairs={{0,17},{1,16},{2,19},{3,18},{4,21},{5,20},{6,23},{7,22},{8,25},{9,... | collective-permute-start | bytes 884744 | tf_op jit(solution)/shard_map/ppermute | solution.py:496
  165.9 22.1 %collective-permute-start.11 = (f32[24,1536]{1,0:T(8,128)S(1)}, f32[24,1536]{1,0:T(8,128)S(1)}, u32[]{:S(2)}, u32[]{:S(2)}) collective-permute-start(f32[24,1536]{1,0:T(8,128)S(1)} %get-tuple-element.125), channel_id=1, source_target_pairs={{0,2},{1,3},{2,0},{3,1},{4,6},{5,7},{6,4},{7,5},{8,10},{9,11},{10,... | collective-permute-start | bytes 442376 | tf_op jit(solution)/shard_map/ppermute | solution.py:24
  167.5 20.5 %collective-permute-start.13 = (f32[24,1536]{1,0:T(8,128)S(1)}, f32[24,1536]{1,0:T(8,128)S(1)}, u32[]{:S(2)}, u32[]{:S(2)}) collective-permute-start(f32[24,1536]{1,0:T(8,128)S(1)} %get-tuple-element.123), channel_id=1, source_target_pairs={{0,4},{1,5},{2,6},{3,7},{4,0},{5,1},{6,2},{7,3},{8,12},{9,13},{10,... | collective-permute-start | bytes 442376 | tf_op jit(solution)/shard_map/ppermute | solution.py:24
  170.0 18.1 %collective-permute-start.14 = (f32[24,1536]{1,0:T(8,128)S(1)}, f32[24,1536]{1,0:T(8,128)S(1)}, u32[]{:S(2)}, u32[]{:S(2)}) collective-permute-start(f32[24,1536]{1,0:T(8,128)S(1)} %get-tuple-element.124), channel_id=1, source_target_pairs={{0,6},{1,7},{2,4},{3,5},{4,2},{5,3},{6,0},{7,1},{8,14},{9,15},{10,... | collective-permute-start | bytes 442376 | tf_op jit(solution)/shard_map/ppermute | solution.py:24
  170.4 17.7 %collective-permute-start.16 = (bf16[7,8,384]{2,1,0:T(8,128)(2,1)S(1)}, bf16[7,8,384]{2,1,0:T(8,128)(2,1)S(1)}, u32[]{:S(2)}, u32[]{:S(2)}) collective-permute-start(bf16[7,8,384]{2,1,0:T(8,128)(2,1)S(1)} %get-tuple-element.127), channel_id=1, source_target_pairs={{0,1},{1,0},{2,3},{3,2},{4,5},{5,4},{6,7},{7,6},{8,9},{9,8},{10,11... | collective-permute-start | bytes 129032 | tf_op jit(solution)/shard_map/ppermute | solution.py:24
  172.9 15.2 %copy-start.12 = (f32[16,384]{1,0:T(8,128)S(1)}, f32[16,384]{1,0:T(8,128)}, u32[]{:S(2)}) copy-start(f32[16,384]{1,0:T(8,128)} %cols_grad.1) | copy-start | bytes 73732
  172.9 15.2 %collective-permute-start.17 = (bf16[7,8,384]{2,1,0:T(8,128)(2,1)S(1)}, bf16[7,8,384]{2,1,0:T(8,128)(2,1)S(1)}, u32[]{:S(2)}, u32[]{:S(2)}) collective-permute-start(bf16[7,8,384]{2,1,0:T(8,128)(2,1)S(1)} %get-tuple-element.126), channel_id=1, source_target_pairs={{1,2},{3,4},{5,6},{2,1},{4,3},{6,5},{9,10},{11,12},{13,14},{10,9},... | collective-permute-start | bytes 129032 | tf_op jit(solution)/shard_map/ppermute | solution.py:30
  188.1 10.3 %copy-start.16 = (bf16[7,8,384]{2,1,0:T(8,128)(2,1)}, bf16[7,8,384]{2,1,0:T(8,128)(2,1)S(1)}, u32[]{:S(2)}) copy-start(bf16[7,8,384]{2,1,0:T(8,128)(2,1)S(1)} %collective-permute-done.16.near) | copy-start | bytes 129028
  188.1 10.3 %copy-start.17 = (bf16[7,8,384]{2,1,0:T(8,128)(2,1)}, bf16[7,8,384]{2,1,0:T(8,128)(2,1)S(1)}, u32[]{:S(2)}) copy-start(bf16[7,8,384]{2,1,0:T(8,128)(2,1)S(1)} %collective-permute-done.17.other) | copy-start | bytes 129028
  188.9 1.2 collective-permute-start.18
  190.9 10.5 %collective-permute-start.19 = (f32[40,384]{1,0:T(8,128)S(1)}, f32[40,384]{1,0:T(8,128)S(1)}, u32[]{:S(2)}, u32[]{:S(2)}) collective-permute-start(f32[40,384]{1,0:T(8,128)S(1)} %fusion.13), channel_id=1, source_target_pairs={{0,16},{8,24},{16,0},{24,8},{1,17},{9,25},{17,1},{25,9},{2,18},{10... | collective-permute-start | bytes 184328 | tf_op jit(solution)/shard_map/ppermute | solution.py:24
  192.0 11.3 %collective-permute-start.20 = (f32[40,384]{1,0:T(8,128)S(1)}, f32[40,384]{1,0:T(8,128)S(1)}, u32[]{:S(2)}, u32[]{:S(2)}) collective-permute-start(f32[40,384]{1,0:T(8,128)S(1)} %fusion.13), channel_id=1, source_target_pairs={{0,1},{1,0},{2,3},{3,2},{4,5},{5,4},{6,7},{7,6},{8,9},{9,8},{10,11... | collective-permute-start | bytes 184328 | tf_op jit(solution)/shard_map/ppermute | solution.py:24
  195.3 7.9 %collective-permute-start.21 = (f32[40,384]{1,0:T(8,128)S(1)}, f32[40,384]{1,0:T(8,128)S(1)}, u32[]{:S(2)}, u32[]{:S(2)}) collective-permute-start(f32[40,384]{1,0:T(8,128)S(1)} %fusion.13), channel_id=1, source_target_pairs={{0,17},{1,16},{2,19},{3,18},{4,21},{5,20},{6,23},{7,22},{8,25},{9,... | collective-permute-start | bytes 184328 | tf_op jit(solution)/shard_map/ppermute | solution.py:496
  195.8 17.1 %collective-permute-start.23 = (bf16[24,1536]{1,0:T(8,128)(2,1)S(1)}, bf16[24,1536]{1,0:T(8,128)(2,1)S(1)}, u32[]{:S(2)}, u32[]{:S(2)}) collective-permute-start(bf16[24,1536]{1,0:T(8,128)(2,1)S(1)} %add_add_fusion), channel_id=1, source_target_pairs={{0,6},{1,7},{2,4},{3,5},{4,2},{5,3},{6,0},{7,1},{8,14},{9,15},{10,... | collective-permute-start | bytes 221192 | tf_op jit(solution)/shard_map/ppermute | solution.py:24
  198.2 14.7 %collective-permute-start.22 = (bf16[24,1536]{1,0:T(8,128)(2,1)S(1)}, bf16[24,1536]{1,0:T(8,128)(2,1)S(1)}, u32[]{:S(2)}, u32[]{:S(2)}) collective-permute-start(bf16[24,1536]{1,0:T(8,128)(2,1)S(1)} %add_add_fusion), channel_id=1, source_target_pairs={{0,2},{1,3},{2,0},{3,1},{4,6},{5,7},{6,4},{7,5},{8,10},{9,11},{10,... | collective-permute-start | bytes 221192 | tf_op jit(solution)/shard_map/ppermute | solution.py:24
  201.4 11.5 %collective-permute-start.15 = (bf16[24,1536]{1,0:T(8,128)(2,1)S(1)}, bf16[24,1536]{1,0:T(8,128)(2,1)S(1)}, u32[]{:S(2)}, u32[]{:S(2)}) collective-permute-start(bf16[24,1536]{1,0:T(8,128)(2,1)S(1)} %add_add_fusion), channel_id=1, source_target_pairs={{0,4},{1,5},{2,6},{3,7},{4,0},{5,1},{6,2},{7,3},{8,12},{9,13},{10,... | collective-permute-start | bytes 221192 | tf_op jit(solution)/shard_map/ppermute | solution.py:24
  213.0 17.5 %collective-permute-start.28 = (bf16[96,1536]{1,0:T(8,128)(2,1)S(1)}, bf16[96,1536]{1,0:T(8,128)(2,1)S(1)}, u32[]{:S(2)}, u32[]{:S(2)}) collective-permute-start(bf16[96,1536]{1,0:T(8,128)(2,1)S(1)} %pad_maximum_fusion.5), channel_id=1, source_target_pairs={{0,17},{1,16},{2,19},{3,18},{4,21},{5,20},{6,23},{7,22},{8,25},{9,... | collective-permute-start | bytes 884744 | tf_op jit(solution)/shard_map/ppermute | solution.py:496
  215.5 15.0 %collective-permute-start.27 = (bf16[96,1536]{1,0:T(8,128)(2,1)S(1)}, bf16[96,1536]{1,0:T(8,128)(2,1)S(1)}, u32[]{:S(2)}, u32[]{:S(2)}) collective-permute-start(bf16[96,1536]{1,0:T(8,128)(2,1)S(1)} %pad_maximum_fusion.5), channel_id=1, source_target_pairs={{0,16},{8,24},{16,0},{24,8},{1,17},{9,25},{17,1},{25,9},{2,18},{10... | collective-permute-start | bytes 884744 | tf_op jit(solution)/shard_map/ppermute | solution.py:24
  216.6 14.0 %collective-permute-start.26 = (bf16[96,1536]{1,0:T(8,128)(2,1)S(1)}, bf16[96,1536]{1,0:T(8,128)(2,1)S(1)}, u32[]{:S(2)}, u32[]{:S(2)}) collective-permute-start(bf16[96,1536]{1,0:T(8,128)(2,1)S(1)} %pad_maximum_fusion.5), channel_id=1, source_target_pairs={{0,1},{1,0},{2,3},{3,2},{4,5},{5,4},{6,7},{7,6},{8,9},{9,8},{10,11... | collective-permute-start | bytes 884744 | tf_op jit(solution)/shard_map/ppermute | solution.py:24
  216.6 4.2 %collective-permute-start.24 = (f32[40,384]{1,0:T(8,128)S(1)}, f32[40,384]{1,0:T(8,128)S(1)}, u32[]{:S(2)}, u32[]{:S(2)}) collective-permute-start(f32[40,384]{1,0:T(8,128)S(1)} %add_add_fusion.1), channel_id=1, source_target_pairs={{0,2},{1,3},{2,0},{3,1},{4,6},{5,7},{6,4},{7,5},{8,10},{9,11},{10,... | collective-permute-start | bytes 184328 | tf_op jit(solution)/shard_map/ppermute | solution.py:24
  231.1 11.1 %copy-start = (bf16[384,1536]{1,0:T(8,128)(2,1)}, bf16[384,1536]{1,0:T(8,128)(2,1)S(1)}, u32[]{:S(2)}) copy-start(bf16[384,1536]{1,0:T(8,128)(2,1)S(1)} %pad_maximum_fusion.own_ref) | copy-start | bytes 3538948
  231.1 11.1 %collective-permute-start.29 = (bf16[384,1536]{1,0:T(8,128)(2,1)S(1)}, bf16[384,1536]{1,0:T(8,128)(2,1)S(1)}, u32[]{:S(2)}, u32[]{:S(2)}) collective-permute-start(bf16[384,1536]{1,0:T(8,128)(2,1)S(1)} %pad_maximum_fusion.own_ref), channel_id=1, source_target_pairs={{0,8},{8,0},{16,24},{24,16},{1,9},{9,1},{17,25},{25,17},{2,10},{10... | collective-permute-start | bytes 3538952 | tf_op jit(solution)/shard_map/ppermute | solution.py:24
  231.2 6.6 %collective-permute-start.25 = (f32[40,384]{1,0:T(8,128)S(1)}, f32[40,384]{1,0:T(8,128)S(1)}, u32[]{:S(2)}, u32[]{:S(2)}) collective-permute-start(f32[40,384]{1,0:T(8,128)S(1)} %add.190), channel_id=1, source_target_pairs={{0,4},{1,5},{2,6},{3,7},{4,0},{5,1},{6,2},{7,3},{8,12},{9,13},{10,... | collective-permute-start | bytes 184328 | tf_op jit(solution)/shard_map/ppermute | solution.py:24
  242.2 1.0 copy-start.3
  (3 other events, 2.2 us)

commit v4 on v3

v4 whole, which is shorter than its diff:
```python
import functools

import jax
import jax.numpy as jnp
import ml_dtypes
import numpy as np
from jax import lax
from jax.experimental import pallas as pl
from jax.experimental.pallas import tpu as pltpu
from jax.sharding import PartitionSpec as P

KSIZE = 15
REACH = KSIZE // 2
EDGE = 8
LANES = 128
GROUP = 16
PAIR = 2
MIB = 2**20
F32, BF16 = jnp.float32, jnp.bfloat16


def swap(block, axis, bit):
    count = lax.axis_size(axis)
    return lax.ppermute(block, axis, [(i, i ^ bit) for i in range(count)])


def swap_across(block, axis):
    count = lax.axis_size(axis)
    pairs = [(i, i + 1) for i in range(1, count - 1, 2)]
    return lax.ppermute(block, axis, pairs + [(j, i) for i, j in pairs])


def tie(value, *others):
    return lax.optimization_barrier((value, *others))[0]


def halo_rows(block):
    place = lax.axis_index("th") % 2
    far = block.shape[0] - REACH
    near = swap(lax.dynamic_slice_in_dim(block, (1 - place) * far, REACH, 0), "th", 1)
    other = swap_across(lax.dynamic_slice_in_dim(block, place * far, REACH, 0), "th")
    return near, other


def halo_cols(*blocks):
    place = lax.axis_index("tw") % 2
    far = blocks[0].shape[1] - EDGE

    def edge(at):
        parts = [lax.dynamic_slice_in_dim(v, at * far, EDGE, 1) for v in blocks]
        return jnp.concatenate(parts, axis=0)

    edges = edge(1 - place), edge(place)
    return swap(edges[0], "tw", 1), swap_across(edges[1], "tw"), edges


def two_parts(matrix):
    high = matrix.astype(ml_dtypes.bfloat16)
    low = (matrix - high.astype(np.float64)).astype(ml_dtypes.bfloat16)
    return np.concatenate([high, low], axis=1)


def transforms(width):
    size = width + 2 * EDGE
    half = size // 2
    place = np.concatenate([EDGE + np.arange(width), np.arange(EDGE), EDGE + width + np.arange(EDGE)])
    freq = np.arange(half)[:, None]

    def angle(n):
        return 2 * np.pi * ((freq * n[None, :]) % size) / size

    lower = -np.sin(angle(place))
    lower[0] = np.cos(np.pi * place)
    forward = np.concatenate([np.cos(angle(place)), lower])
    swapped = np.concatenate([forward[:, :width], forward[:, width + EDGE :], forward[:, width : width + EDGE]], axis=1)

    def back(n):
        real = 2 * np.cos(angle(n)) / size
        imag = -2 * np.sin(angle(n)) / size
        real[0] = 1 / size
        imag[0] = np.cos(np.pi * n) / size
        return np.concatenate([real, imag]).T

    ahead = back(1 + np.arange(width))
    behind = back(KSIZE + np.arange(width))
    lag = np.arange(KSIZE) - REACH
    real, high, imag = (np.zeros((KSIZE + 1, half)) for _ in range(3))
    real[:KSIZE] = (2 * np.cos(angle(lag)) / size).T
    high[:KSIZE] = real[:KSIZE]
    imag[:KSIZE] = (-2 * np.sin(angle(lag)) / size).T
    real[:KSIZE, 0] = 1 / size
    high[:KSIZE, 0] = np.cos(np.pi * lag) / size
    imag[:KSIZE, 0] = 0
    lags = np.concatenate([real, high, imag], axis=1).astype(np.float32)
    tap = np.arange(KSIZE + 1)
    real = np.cos(angle(tap))
    imag = np.sin(angle(tap))
    high = real.copy()
    high[0] = np.cos(np.pi * tap)
    response = np.concatenate([real, imag, high]).astype(np.float32)
    return (
        two_parts(forward), two_parts(swapped), two_parts(forward[:, :width]), two_parts(ahead), two_parts(behind),
        lags, response,
    )


def dot(a, b, precision=None, dims=((1,), (0,))):
    return lax.dot_general(a, b, (dims, ((), ())), precision=precision, preferred_element_type=F32)


def taps_kernel(
    height, heights_ref, rate_ref, freq_ref, cr_ref, ci_ref, log_step_ref, response_ref, straight_ref, swapped_ref,
    taps_ref, factor_ref, forward_ref, source_ref, zr_ref, zi_ref,
):
    half = factor_ref.shape[1]
    for d in range(2):
        step = jnp.exp(log_step_ref[d])[None, :]
        decay = jnp.exp(-jnp.exp(rate_ref[d]) * step)
        phase = freq_ref[d] * step
        zr, zi = decay * jnp.cos(phase), decay * jnp.sin(phase)
        zr_ref[d], zi_ref[d] = zr, zi
        cr, ci = cr_ref[d], ci_ref[d]
        ur, ui = jnp.ones_like(zr), jnp.zeros_like(zr)
        for m in range(KSIZE):
            taps_ref[d, m] = 2.0 * jnp.sum(cr * ur - ci * ui, axis=0)
            ur, ui = ur * zr - ui * zi, ur * zi + ui * zr
        taps_ref[d, KSIZE] = jnp.zeros_like(taps_ref[d, KSIZE])
    factor = dot(response_ref[...], taps_ref[1], lax.Precision.HIGHEST)
    for k in range(3):
        factor_ref[k] = factor[k * half : (k + 1) * half]
    high, right = lax.axis_index("th"), lax.rem(lax.axis_index("tw"), 2)
    place = lax.rem(high, 2)

    @pl.when(right == 1)
    def _():
        forward_ref[...] = straight_ref[...]

    @pl.when(right == 0)
    def _():
        forward_ref[...] = swapped_ref[...]

    row = lax.broadcasted_iota(jnp.int32, source_ref.shape, 0)
    lane = lax.broadcasted_iota(jnp.int32, source_ref.shape, 1)
    first, second = heights_ref[0], heights_ref[0] + heights_ref[1]
    here = row + high * height
    there = here + lane - REACH
    same = ((here >= first) == (there >= first)) & ((here >= second) == (there >= second))
    source = jnp.where(same, row + lane, height + 2 * REACH)
    last = jnp.where(lane == place, REACH + height, 0)
    last = jnp.where(lane == 2, place, jnp.where(lane == 3, right, last))
    source_ref[...] = jnp.where(row < height, source, last)


def taps_grad_kernel(
    zr_ref, zi_ref, cr_ref, ci_ref, rate_ref, freq_ref, step_ref, g_ref,
    d_rate_ref, d_freq_ref, d_cr_ref, d_ci_ref, d_step_ref, d_b_in_ref, *vector_refs,
):
    chans = g_ref.shape[1]
    for k, vector_ref in enumerate(vector_refs):
        vector_ref[...] = g_ref[2 * KSIZE + 1 + k]
    for k in range(d_b_in_ref.shape[0] // chans):
        d_b_in_ref[k * chans : (k + 1) * chans] = g_ref[2 * KSIZE + 1 + len(vector_refs) + k]
    for d in range(2):
        zr, zi = zr_ref[d], zi_ref[d]
        cr, ci = cr_ref[d], ci_ref[d]
        ur, ui = jnp.ones_like(zr), jnp.zeros_like(zr)
        su, sv = jnp.zeros_like(zr), jnp.zeros_like(zr)
        mu, mv = jnp.zeros_like(zr), jnp.zeros_like(zr)
        for m in range(KSIZE):
            g = 2.0 * g_ref[d * (KSIZE + 1) + m][None, :]
            gu, gv = g * ur, g * ui
            su, sv = su + gu, sv + gv
            if m:
                mu, mv = mu + float(m) * gu, mv + float(m) * gv
            ur, ui = ur * zr - ui * zi, ur * zi + ui * zr
        step = jnp.exp(step_ref[d])[None, :]
        freq = freq_ref[d]
        d_freq = -step * (cr * mv + ci * mu)
        d_rate = -jnp.exp(rate_ref[d]) * step * (cr * mu - ci * mv)
        d_cr_ref[d] = su
        d_ci_ref[d] = -sv
        d_freq_ref[d] = d_freq
        d_rate_ref[d] = d_rate
        d_step_ref[d] = jnp.sum(d_rate + freq * d_freq, axis=0)


AHEAD = REACH + 3


def start_rows(ext, source_ref, centre, near, other):
    height = centre.shape[0]
    ext[height + 2 * REACH] = jnp.zeros(ext.shape[1:], F32)
    for i in range(REACH):
        ext[source_ref[height, 0] + i] = near[i].astype(F32)
        ext[source_ref[height, 1] + i] = other[i].astype(F32)
    for i in range(AHEAD):
        ext[REACH + i] = centre[i].astype(F32)


def next_rows(ext, centre, r):
    for k in range(2):
        at = jnp.minimum(2 * r + AHEAD + k, centre.shape[0] - 1)
        ext[REACH + at] = centre[at].astype(F32)


def load_rows(ext, at, centre):
    def place(r, _):
        for k in range(4):
            ext[at + 4 * r + k] = centre[4 * r + k].astype(F32)
        return 0

    lax.fori_loop(0, centre.shape[0] // 4, place, 0)


def fold(v):
    return jnp.sum(v.reshape(v.shape[0] // 8, 8, v.shape[1]), axis=0)


def rows_kernel(source_ref, taps_ref, centre, near, other, partial_ref, ext):
    height = centre.shape[0]
    start_rows(ext, source_ref, centre, near, other)
    load_rows(ext, REACH, centre)
    taps = [taps_ref[0, i][None, :] for i in range(KSIZE)]

    def row(r, _):
        for k in range(4):
            at = 4 * r + k
            total = taps[0] * ext[source_ref[at, 0]]
            for i in range(1, KSIZE):
                total = total + taps[i] * ext[source_ref[at, i]]
            partial_ref[at] = total.astype(BF16)
        return 0

    lax.fori_loop(0, height // 4, row, 0)


def twice(v):
    return jnp.concatenate([v, v], axis=0)


def filtered(spectrum, factor, conjugate):
    half = factor[0].shape[0]
    real, imag = spectrum[:half], spectrum[half:]
    a, b, top = factor
    cross = b * imag
    across = b * real
    if conjugate:
        return jnp.concatenate([a * real + cross, top * imag - across], axis=0).astype(BF16)
    return jnp.concatenate([a * real - cross, top * imag + across], axis=0).astype(BF16)


def side_by_side(values):
    return jnp.concatenate(values, axis=1)


def cols_kernel(
    source_ref, taps_ref, skip_ref, factor_ref, forward_ref, ahead_ref,
    partial_ref, image_ref, near, other, near_strip, other_strip,
    mixed_ref, spectrum_ref, sides,
):
    step = pl.program_id(0)
    height = near.shape[0]
    full = height + 2 * REACH
    chans = skip_ref.shape[0]

    @pl.when(step == 0)
    def _():
        sides[full] = jnp.zeros(sides.shape[1:], F32)
        for i in range(2 * REACH):
            base = source_ref[height, i // REACH] + i % REACH
            sides[base] = jnp.concatenate(
                [near_strip[i].astype(F32), other_strip[i].astype(F32)], axis=0
            )

        def place(r, _):
            for k in range(4):
                at = 4 * r + k
                sides[at + REACH] = jnp.concatenate(
                    [near[at].astype(F32), other[at].astype(F32)], axis=0
                )
            return 0

        lax.fori_loop(0, height // 4, place, 0)

    taps = [taps_ref[0, i][None, :] for i in range(KSIZE)]
    factor = paired(factor_ref)
    skip = skip_ref[...][None, :]

    def line(k):
        at = step * GROUP + k
        total = taps[0] * sides[source_ref[at, 0]]
        for i in range(1, KSIZE):
            total = total + taps[i] * sides[source_ref[at, i]]
        return jnp.concatenate([partial_ref[k], total.astype(BF16)], axis=0)

    for k in range(0, GROUP, PAIR):
        lines = side_by_side([line(k + n) for n in range(PAIR)])
        spectrum = dot(forward_ref[...], twice(lines))
        mixed = dot(ahead_ref[...], twice(filtered(spectrum, factor, False)))
        for n in range(PAIR):
            cut = slice(n * chans, (n + 1) * chans)
            spectrum_ref[k + n] = spectrum[:, cut].astype(BF16)
            mixed_ref[k + n] = mixed[:, cut] + skip * image_ref[k + n].astype(F32)


def cols_grad_kernel(
    own_ref, lags_ref, d_mixed_ref, spectrum_ref, image_ref, sums_ref, totals, skip_total
):
    step = pl.program_id(0)
    half, chans = totals.shape[1], totals.shape[2]

    @pl.when(step == 0)
    def _():
        totals[...] = jnp.zeros(totals.shape, F32)
        skip_total[...] = jnp.zeros(skip_total.shape, F32)

    for k in range(0, GROUP, PAIR):
        rows = [d_mixed_ref[k + n] for n in range(PAIR)]
        spectra = dot(own_ref[...], twice(side_by_side(rows)))
        found = []
        for n in range(PAIR):
            spectrum = spectra[:, n * chans : (n + 1) * chans]
            real, imag = spectrum[:half], spectrum[half:]
            other = spectrum_ref[k + n].astype(F32)
            other_real, other_imag = other[:half], other[half:]
            found.append((real * other_real, imag * other_imag, real * other_imag - imag * other_real))
            skip_total[...] += fold(rows[n].astype(F32) * image_ref[k + n].astype(F32))
        for m in range(3):
            totals[m] += sum(f[m] for f in found[1:]) + found[0][m]

    @pl.when(step == pl.num_programs(0) - 1)
    def _():
        both = jnp.concatenate([totals[0], totals[1], totals[2]], axis=0)
        sums_ref[...] = dot(lags_ref[...], both, lax.Precision.HIGHEST)
        sums_ref[KSIZE : KSIZE + 1] = jnp.sum(skip_total[...], axis=0, keepdims=True)


def transformed_back(factor, forward_ref, behind_ref, lines):
    chans = factor[0].shape[1] // PAIR
    beside = [jnp.concatenate([near.astype(F32), other.astype(F32)], axis=0).astype(BF16) for _, near, other in lines]
    wide = side_by_side([jnp.concatenate([line[0], side], axis=0) for line, side in zip(lines, beside)])
    spectrum = dot(forward_ref[...], twice(wide))
    some = [f[:, : spectrum.shape[1]] for f in factor]
    found = dot(behind_ref[...], twice(filtered(spectrum, some, True))).astype(BF16)
    return [found[:, n * chans : (n + 1) * chans] for n in range(len(lines))]


def paired(factor_ref):
    return [side_by_side([factor_ref[k]] * PAIR) for k in range(3)]


def cols_back_kernel(
    source_ref, factor_ref, forward_ref, behind_ref, d_mixed_ref, near, other, d_partial_ref, near_give, other_give
):
    step = pl.program_id(0)
    last = pl.num_programs(0) - 1
    factor = paired(factor_ref)
    for k in range(0, GROUP, PAIR):
        places = range(k, k + PAIR)
        found = transformed_back(
            factor, forward_ref, behind_ref, [(d_mixed_ref[i], near[i], other[i]) for i in places]
        )
        for i, value in zip(places, found):
            d_partial_ref[i] = value
    high = source_ref[GROUP * pl.num_programs(0), 2]
    for at, where, side in ((0, 0, 1), (last, GROUP - REACH, 0)):
        for to, place in ((near_give, side), (other_give, 1 - side)):

            @pl.when((step == at) & (high == place))
            def _():
                to[...] = d_partial_ref[where : where + REACH]


def rows_grad_kernel(source_ref, d_partial_ref, image, near, other, sums_ref, ext):
    height = d_partial_ref.shape[0]
    start_rows(ext, source_ref, image, near, other)

    def row(r, totals):
        totals = list(totals)
        for k in range(2):
            at = 2 * r + k
            d = d_partial_ref[at].astype(F32)
            for i in range(KSIZE):
                totals[i] = totals[i] + fold(d * ext[source_ref[at, i]])
        next_rows(ext, image, r)
        return tuple(totals)

    zero = jnp.zeros((8, LANES), F32)
    totals = lax.fori_loop(0, height // 2, row, (zero,) * KSIZE)
    for i in range(KSIZE):
        sums_ref[i : i + 1] = jnp.sum(totals[i], axis=0, keepdims=True)
    sums_ref[KSIZE : KSIZE + 1] = jnp.zeros((1, LANES), F32)


def rows_back_kernel(
    first, source_ref, taps_ref, skip_ref, d_partial_ref, beside, near, other, d_mixed_ref, grad_ref, *rest
):
    image_grad_ref, ext = rest[-2:]
    count = d_partial_ref.shape[0]
    height = 2 * count
    ext[height + 2 * REACH] = jnp.zeros(ext.shape[1:], F32)
    for i in range(REACH):
        ext[source_ref[height, 0] + i] = near[i].astype(F32)
        ext[source_ref[height, 1] + i] = other[i].astype(F32)
    beyond = count if first == 0 else count - EDGE
    for i in range(EDGE):
        ext[REACH + beyond + i] = beside[i].astype(F32)
    load_rows(ext, REACH + first, d_partial_ref)
    taps = [taps_ref[0, i][None, :] for i in range(KSIZE)]
    skip = skip_ref[...]

    def row(r, _):
        for k in range(4):
            at = 4 * r + k
            total = grad_ref[at].astype(F32) + skip * d_mixed_ref[at].astype(F32)
            for i in range(KSIZE):
                total = total + taps[i] * ext[source_ref[first + at, KSIZE - 1 - i]]
            image_grad_ref[at] = total.astype(BF16)
        return 0

    lax.fori_loop(0, count // 4, row, 0)


def feed_kernel(
    source_ref, mixed_ref, image_ref, grad_ref, w_in_ref, w_out_ref, b_in_ref, gain_ref, bias_ref, b_out_ref, scale_ref,
    output_ref, d_mixed_ref, col_near_ref, col_other_ref, keep_ref, give_ref,
    pieces_ref, b_sums_ref, sums_ref, act_ref, d_pre_ref, weights_ref,
):
    step = pl.program_id(0)
    last = pl.num_programs(0) - 1
    chans, hidden = w_in_ref.shape
    piece = 256
    pixels = d_mixed_ref.shape[0]
    lines = col_near_ref.shape[0] // EDGE
    width = pixels // lines
    height = lines * pl.num_programs(0)
    high, right = source_ref[height, 2], source_ref[height, 3]

    @pl.when(step == 0)
    def _():
        weights_ref[...] = jnp.zeros(weights_ref.shape, F32)
        b_sums_ref[...] = jnp.zeros(b_sums_ref.shape, F32)
        sums_ref[...] = jnp.zeros(sums_ref.shape, F32)

    gain, bias, b_out, scale = (ref[...][None, :] for ref in (gain_ref, bias_ref, b_out_ref, scale_ref))
    b_in = b_in_ref[...][None, :]
    mixed = mixed_ref[...]
    mean = jnp.mean(mixed, axis=-1, keepdims=True)
    centred = mixed - mean
    var = jnp.mean(centred * centred, axis=-1, keepdims=True)
    inverse = lax.rsqrt(var + 1e-06)
    xhat = centred * inverse
    normed = (xhat * gain + bias).astype(BF16)
    grad = grad_ref[...].astype(F32)
    d_branch = (scale * grad).astype(BF16)
    normed_t = jnp.concatenate([normed.T, jnp.ones((16, normed.shape[0]), BF16)], axis=0)
    d_branch_t = d_branch.T

    def inward(k):
        cut = slice(k, k + piece)
        pre = dot(normed, w_in_ref[:, cut]) + b_in[:, cut]
        return pre, dot(d_branch, w_out_ref[cut, :], dims=((1,), (1,)))

    ahead = inward(0)
    for k in range(0, hidden, piece):
        cut = slice(k, k + piece)
        pre, d_act = ahead
        if k + piece < hidden:
            ahead = inward(k + piece)
        half = 0.5 + 0.5 * lax.erf(pre * 0.7071067811865476)
        bell = jnp.exp(pre * pre * -0.5) * 0.3989422804014327
        act = (pre * half).astype(BF16)
        d_pre = (d_act * (half + pre * bell)).astype(BF16)
        act_ref[:, cut] = act
        d_pre_ref[:, cut] = d_pre
        found = dot(normed_t, d_pre)
        weights_ref[0:chans, cut] += found[:chans]
        b_sums_ref[:, cut] += found[chans : chans + 8]
        weights_ref[chans : 2 * chans, cut] += dot(d_branch_t, act)
    branch = dot(w_out_ref[...], act_ref[...], dims=((0,), (1,))).T + b_out
    output_ref[...] = (image_ref[...].astype(F32) + scale * branch).astype(BF16)
    d_normed = dot(w_in_ref[...], d_pre_ref[...], dims=((1,), (1,))).T
    g = d_normed * gain
    g_mean = jnp.mean(g, axis=-1, keepdims=True)
    g_xhat = jnp.mean(g * xhat, axis=-1, keepdims=True)
    d_mixed = (g - g_mean - xhat * g_xhat) * inverse
    d_mixed_ref[...] = d_mixed.astype(BF16)
    grid = d_mixed.reshape(lines, width, chans)
    left = grid[:, :EDGE].reshape(col_near_ref.shape)
    far = grid[:, width - EDGE :].reshape(col_near_ref.shape)
    col_near_ref[...] = jnp.where(right == 1, left, far).astype(BF16)
    col_other_ref[...] = jnp.where(right == 1, far, left).astype(BF16)
    sums_ref[0] += fold(d_normed * xhat)
    sums_ref[1] += fold(d_normed)
    sums_ref[2] += fold(d_branch.astype(F32))
    sums_ref[3] += fold(grad * branch)

    @pl.when(step == last)
    def _():
        for place in range(2):

            @pl.when(high == place)
            def _():
                keep_ref[...] = weights_ref[place * chans : (place + 1) * chans]
                give_ref[...] = weights_ref[(1 - place) * chans : (2 - place) * chans].astype(BF16)

        pieces_ref[0:4] = jnp.sum(sums_ref[...], axis=1)
        for k in range(hidden // chans):
            pieces_ref[4 + k : 5 + k] = b_sums_ref[0:1, k * chans : (k + 1) * chans]


def whole(shape):
    return pl.BlockSpec(shape, lambda *_: (0,) * len(shape))


def lane_block(*lead):
    return pl.BlockSpec((*lead, LANES), lambda c: (0,) * len(lead) + (c,))


def row_block(*rest):
    return pl.BlockSpec((GROUP, *rest), lambda r: (r,) + (0,) * len(rest))


SCALARS = pl.BlockSpec(memory_space=pltpu.SMEM)


def params(mib=60):
    return pltpu.CompilerParams(vmem_limit_bytes=mib * MIB)


def cost(us):
    return pl.CostEstimate(flops=int(us * 1e6), bytes_accessed=int(us * 1e3), transcendentals=0)


def mesh_steps():
    def bits(axis):
        return [(axis, 1 << k) for k in range(lax.axis_size(axis).bit_length() - 1)]

    (core, *high), low = bits("th"), bits("tw")
    mixed = [step for pair in zip(high, low) for step in pair]
    return [core] + mixed + high[len(low) :] + low[len(high) :]


def swap_two(block, first, second):
    if first[0] == second[0]:
        return swap(block, first[0], first[1] + second[1])
    bits = dict([first, second])
    high, low = lax.axis_size("th"), lax.axis_size("tw")
    pairs = [
        (i * low + j, (i ^ bits["th"]) * low + (j ^ bits["tw"])) for i in range(high) for j in range(low)
    ]
    return lax.ppermute(block, ("th", "tw"), pairs)


def place_in(steps):
    place = 0
    for n, (axis, bit) in enumerate(steps):
        place = place + lax.rem(lax.axis_index(axis) // bit, 2) * (1 << n)
    return place


def exchanges(steps):
    if len(steps) == 1:
        return [lambda v: swap(v, *steps[0])]
    return [lambda v: swap(v, *steps[0]), lambda v: swap(v, *steps[1]), lambda v: swap_two(v, *steps)]


def scatter(block, steps, beside):
    place = place_in(steps)
    size = block.shape[0] >> len(steps)
    parts = [lax.dynamic_slice_in_dim(block, (place ^ k) * size, size, 0) for k in range(1 << len(steps))]
    takes = [send(part) for send, part in zip(exchanges(steps), parts[1:])]
    done = beside(parts[1:])
    return sum([tie(take, *done) for take in takes], parts[0])


def gather(block, steps, beside):
    place = place_in(steps)
    takes = [send(block) for send in exchanges(steps)]
    done = beside([block])
    parts = [block] + [tie(take, *done) for take in takes]
    rows = []
    for q in range(len(parts)):
        found = parts[-1]
        for k in range(len(parts) - 1):
            found = jnp.where((place ^ q) == k, parts[k], found)
        rows.append(found)
    return jnp.concatenate(rows, axis=0)


def split_kernel(place_ref, keep_ref, take_ref, own_ref, *give_refs):
    size = own_ref.shape[0]
    for k, to in enumerate((own_ref, *give_refs)):
        rows = pl.ds(pl.multiple_of((place_ref[0] ^ k) * size, size), size)
        to[...] = (keep_ref[rows] + take_ref[rows].astype(F32)).astype(to.dtype)


def finish_kernel(side_ref, own_ref, other_ref, w_in_ref, w_out_ref):
    side = side_ref[0]

    @pl.when(side == 0)
    def _():
        w_in_ref[...] = own_ref[...].astype(F32)
        w_out_ref[...] = other_ref[...].T.astype(F32)

    @pl.when(side == 1)
    def _():
        w_in_ref[...] = other_ref[...].astype(F32)
        w_out_ref[...] = own_ref[...].T.astype(F32)


def per_device(
    image, image_heights, rate_log, freq, coef_re, coef_im, log_step, skip, ln_gain, ln_bias,
    w_in, b_in, w_out, b_out, layer_scale, out_grad,
):
    height, width, chans = image.shape
    hidden = w_in.shape[1]
    pixels = height * width
    full = height + 2 * REACH
    size = width + 2 * EDGE
    half = size // 2
    blocks = chans // LANES
    groups = height // GROUP
    straight, swapped, own, ahead, behind, lags, response = transforms(width)

    row_near, row_other = halo_rows(image)
    col_near, col_other, edges = halo_cols(image)

    rate_t, freq_t, cr_t, ci_t = (v.transpose(0, 2, 1) for v in (rate_log, freq, coef_re, coef_im))
    mode_shape = jax.ShapeDtypeStruct(rate_t.shape, F32)
    vmem = pl.BlockSpec(memory_space=pltpu.VMEM)
    taps, factor, forward, source, zr, zi = pl.pallas_call(
        functools.partial(taps_kernel, height),
        in_specs=[SCALARS] + [vmem] * 8,
        out_shape=[
            jax.ShapeDtypeStruct((2, KSIZE + 1, chans), F32),
            jax.ShapeDtypeStruct((3, half, chans), F32),
            jax.ShapeDtypeStruct((size, 2 * size), BF16),
            jax.ShapeDtypeStruct((height + 8, LANES), jnp.int32),
            mode_shape,
            mode_shape,
        ],
        cost_estimate=cost(5),
        name="taps",
    )(image_heights, rate_t, freq_t, cr_t, ci_t, tie(log_step, *edges), response, straight, swapped)

    near_strip, other_strip, strips = halo_cols(row_near, tie(row_other, taps))
    tile_shape = (height, width, chans)
    partial = pl.pallas_call(
        rows_kernel,
        grid=(blocks,),
        in_specs=[
            SCALARS, lane_block(2, KSIZE + 1), lane_block(height, width),
            lane_block(REACH, width), lane_block(REACH, width),
        ],
        out_specs=lane_block(height, width),
        out_shape=jax.ShapeDtypeStruct(tile_shape, BF16),
        scratch_shapes=[pltpu.VMEM((full + 1, width, LANES), F32)],
        compiler_params=params(),
        cost_estimate=cost(14),
        name="rows_forward",
    )(source, tie(taps, *strips), image, row_near, row_other)

    mixed, spectrum = pl.pallas_call(
        cols_kernel,
        grid=(groups,),
        in_specs=[
            SCALARS, whole((2, KSIZE + 1, chans)), whole((chans,)), whole((3, half, chans)),
            whole((size, 2 * size)), whole((width, 2 * size)),
            row_block(width, chans), row_block(width, chans),
            whole((height, EDGE, chans)), whole((height, EDGE, chans)),
            whole((2 * REACH, EDGE, chans)), whole((2 * REACH, EDGE, chans)),
        ],
        out_specs=[row_block(width, chans), row_block(size, chans)],
        out_shape=[
            jax.ShapeDtypeStruct(tile_shape, F32),
            jax.ShapeDtypeStruct((height, size, chans), BF16),
        ],
        scratch_shapes=[pltpu.VMEM((full + 1, 2 * EDGE, chans), F32)],
        compiler_params=params(),
        cost_estimate=cost(14),
        name="cols_forward",
    )(
        source, taps, skip, factor, forward, ahead, partial, image,
        col_near, col_other, near_strip, other_strip,
    )

    tile = 1536
    pixel_block = pl.BlockSpec((tile, chans), lambda i: (i, 0))
    col_block = pl.BlockSpec((tile // width * EDGE, chans), lambda i: (i, 0))
    output, d_mixed, col_near_give, col_other_give, keep, give, pieces = pl.pallas_call(
        feed_kernel,
        grid=(pixels // tile,),
        in_specs=[
            SCALARS, pixel_block, pixel_block, pixel_block,
            whole((chans, hidden)), whole((hidden, chans)), whole((hidden,)), *[whole((chans,))] * 4,
        ],
        out_specs=[
            pixel_block, pixel_block, col_block, col_block,
            whole((chans, hidden)), whole((chans, hidden)), whole((4 + hidden // chans, chans)),
        ],
        out_shape=[
            jax.ShapeDtypeStruct((pixels, chans), BF16),
            jax.ShapeDtypeStruct((pixels, chans), BF16),
            jax.ShapeDtypeStruct((height * EDGE, chans), BF16),
            jax.ShapeDtypeStruct((height * EDGE, chans), BF16),
            jax.ShapeDtypeStruct((chans, hidden), F32),
            jax.ShapeDtypeStruct((chans, hidden), BF16),
            jax.ShapeDtypeStruct((4 + hidden // chans, chans), F32),
        ],
        scratch_shapes=[
            pltpu.VMEM((8, hidden), F32), pltpu.VMEM((4, 8, chans), F32),
            pltpu.VMEM((tile, hidden), BF16), pltpu.VMEM((tile, hidden), BF16), pltpu.VMEM((2 * chans, hidden), F32),
        ],
        compiler_params=params(),
        cost_estimate=cost(70),
        name="feed_forward",
    )(
        source, mixed.reshape(pixels, chans), image.reshape(pixels, chans), out_grad.reshape(pixels, chans),
        w_in, w_out, b_in, ln_gain, ln_bias, b_out, layer_scale,
    )
    output = output.reshape(tile_shape)
    d_mixed = d_mixed.reshape(tile_shape)

    col_shape = (height, EDGE, chans)
    grad_col_near = swap(col_near_give, "tw", 1).reshape(col_shape)
    grad_col_other = swap_across(col_other_give, "tw").reshape(col_shape)

    core, *others = mesh_steps()
    phases = [others[k : k + 2] for k in range(0, len(others), 2)]
    take = swap(give, *core)
    col_sums = pl.pallas_call(
        cols_grad_kernel,
        grid=(groups,),
        in_specs=[
            whole((size, 2 * width)), whole((KSIZE + 1, 3 * half)),
            row_block(width, chans), row_block(size, chans), row_block(width, chans),
        ],
        out_specs=whole((KSIZE + 1, chans)),
        out_shape=jax.ShapeDtypeStruct((KSIZE + 1, chans), F32),
        scratch_shapes=[pltpu.VMEM((3, half, chans), F32), pltpu.VMEM((8, chans), F32)],
        compiler_params=params(),
        cost_estimate=cost(8),
        name="cols_grad",
    )(own, lags, d_mixed, spectrum, image)
    found = [col_sums]
    parts = 1 << len(phases[0])
    own_part, *gives = pl.pallas_call(
        split_kernel,
        in_specs=[SCALARS, vmem, vmem],
        out_shape=[
            jax.ShapeDtypeStruct((chans // parts, hidden), F32 if k == 0 else BF16) for k in range(parts)
        ],
        compiler_params=params(16),
        cost_estimate=cost(2),
        name="split",
    )(place_in(phases[0])[None], keep, tie(take, col_sums))

    edge = (REACH, width, chans)

    def cols_back(sent):
        found.extend(
            pl.pallas_call(
                cols_back_kernel,
                grid=(groups,),
                in_specs=[
                    SCALARS, whole((3, half, chans)), whole((size, 2 * size)), whole((width, 2 * size)),
                    row_block(width, chans), row_block(EDGE, chans), row_block(EDGE, chans),
                ],
                out_specs=[row_block(width, chans), whole(edge), whole(edge)],
                out_shape=[
                    jax.ShapeDtypeStruct(tile_shape, BF16),
                    jax.ShapeDtypeStruct(edge, BF16),
                    jax.ShapeDtypeStruct(edge, BF16),
                ],
                compiler_params=params(),
                cost_estimate=cost(12),
                name="cols_back",
            )(source, factor, forward, behind, tie(d_mixed, *sent), grad_col_near, grad_col_other)
        )
        return found[1:]

    takes = [send(part) for send, part in zip(exchanges(phases[0]), gives)]
    done = cols_back(gives)
    weights = sum([tie(part, *done).astype(F32) for part in takes], own_part)
    d_partial, near_give, other_give = found[1:]
    d_near = swap(near_give, "th", 1)
    d_other = swap_across(other_give, "th")

    def rows_grad(sent):
        found.append(
            pl.pallas_call(
                rows_grad_kernel,
                grid=(blocks,),
                in_specs=[
                    SCALARS, lane_block(height, width), lane_block(height, width),
                    lane_block(REACH, width), lane_block(REACH, width),
                ],
                out_specs=lane_block(KSIZE + 1),
                out_shape=jax.ShapeDtypeStruct((KSIZE + 1, chans), F32),
                scratch_shapes=[pltpu.VMEM((full + 1, width, LANES), F32)],
                compiler_params=params(),
                cost_estimate=cost(14),
                name="rows_grad",
            )(source, tie(d_partial, *sent), image, row_near, row_other)
        )
        return found[-1:]

    for n, later in enumerate(phases[1:]):
        weights = scatter(weights, later, rows_grad if n == 0 else lambda _: [])
    row_sums = found[-1]
    small = jnp.concatenate([tie(row_sums, weights, d_near, d_other), col_sums, pieces], axis=0)
    small = small + swap(small, *core)
    weights = weights.astype(BF16)
    for later in reversed(phases[1:]):
        weights = gather(weights, later, lambda _: [small])
    takes = [send(small) for send in exchanges(phases[0])]
    small = sum(takes, small)

    skip_row = tie(skip, give)[None, :]

    def rows_back(part, before, *waits):
        count = height // 2
        lanes = lambda rows, block=0: pl.BlockSpec((rows, width, LANES), lambda c: (block, 0, c))
        at = lanes(count, part)
        return pl.pallas_call(
            functools.partial(rows_back_kernel, part * count),
            grid=(blocks,),
            in_specs=[
                SCALARS, lane_block(2, KSIZE + 1), lane_block(1), at, lanes(EDGE, count // EDGE - part),
                lanes(REACH), lanes(REACH), at, at,
                *([] if before is None else [pl.BlockSpec(memory_space=pl.ANY)]),
            ],
            out_specs=at,
            out_shape=jax.ShapeDtypeStruct(tile_shape, BF16),
            scratch_shapes=[pltpu.VMEM((full + 1, width, LANES), F32)],
            compiler_params=params(),
            cost_estimate=cost(8),
            input_output_aliases={} if before is None else {9: 0},
            name="rows_back",
        )(
            source, taps, tie(skip_row, *waits), d_partial, d_partial, d_near, d_other, d_mixed, out_grad,
            *([] if before is None else [before]),
        )

    for n, later in enumerate(phases[1:]):
        takes = [send(small) for send in exchanges(later)]
        if n == 0:
            image_grad = rows_back(0, None, small)
        small = sum([tie(take, image_grad) for take in takes], small)

    def last_rows(sent):
        found.append(rows_back(1, image_grad, *sent))
        return found[-1:]

    weights = gather(tie(weights, small), phases[0], last_rows)
    image_grad = found[-1]
    cut = hidden // 4
    half_block = pl.BlockSpec((chans, cut), lambda k: (0, k))
    d_win, d_wout = pl.pallas_call(
        finish_kernel,
        grid=(4,),
        in_specs=[SCALARS, half_block, half_block],
        out_specs=[half_block, pl.BlockSpec((cut, chans), lambda k: (k, 0))],
        out_shape=[
            jax.ShapeDtypeStruct((chans, hidden), F32),
            jax.ShapeDtypeStruct((hidden, chans), F32),
        ],
        compiler_params=params(16),
        cost_estimate=cost(3),
        name="weight_grads",
    )(place_in([core])[None], weights, swap(weights, *core))
    vector = jax.ShapeDtypeStruct((chans,), F32)
    g_rate, g_freq, g_re, g_im, g_step, d_bin, d_skip, d_gain, d_bias, d_bout, d_scale = pl.pallas_call(
        taps_grad_kernel,
        out_shape=[mode_shape] * 4
        + [jax.ShapeDtypeStruct((2, chans), F32), jax.ShapeDtypeStruct((hidden,), F32)]
        + [vector] * 5,
        cost_estimate=cost(3),
        name="taps_grad",
    )(zr, zi, cr_t, ci_t, rate_t, freq_t, log_step, small)
    g_rate, g_freq, g_re, g_im = (v.transpose(0, 2, 1) for v in (g_rate, g_freq, g_re, g_im))
    return (
        output, image_grad, g_rate, g_freq, g_re, g_im, g_step, d_skip, d_gain, d_bias,
        d_win, d_bin, d_wout, d_bout, d_scale,
    )


def solution(mesh):
    tiled = P("th", "tw", None)
    return jax.shard_map(
        per_device,
        mesh=mesh,
        in_specs=(tiled,) + (P(),) * 14 + (tiled,),
        out_specs=(tiled, tiled) + (P(),) * 13,
        check_vma=False,
    )
```

time: 249 us -> 215 us (0.86)
  local copies, waits for them, and re-layouts: 16.5 us -> 4.79 us
  other arithmetic: 11.2 us -> 2.66 us
  waiting for transfers between devices: 14.3 us -> 6.89 us
  Pallas kernels: 158 us -> 152 us
    ppermute x22 -> x23, waiting for transfers between devices: 14.2 us -> 4.64 us  [swap(): return lax.ppermute(block, axis, [(i, i ^ bit) for i in range(count)])]
    dynamic_slice x4 -> x2, local copies, waits for them, and re-layouts: 5.45 us -> 1.35 us  [the longest x1 1.3 us: halo_rows(): lax.dynamic_slice_in_dim(block, (1 - place) * far, REACH, 0)]
    add x6 -> x4, other arithmetic: 4.13 us -> 0.81 us  [the longest x1 0.64 us: per_device(): small = sum([tie(take, image_grad) for take in takes], small)]
    slice x5 -> x0, local copies, waits for them, and re-layouts: 2.64 us -> none  [the longest x1 0.82 us: per_device(): b_sums[0].reshape(hidden // chans, chans)]
    ppermute x22 -> x23, starting transfers between devices: 36.3 us -> 38.8 us  [swap(): return lax.ppermute(block, axis, [(i, i ^ bit) for i in range(count)])]
  transfers between devices with their start and end apart: 30 -> 31, of which waited for: 6 -> 8; matrix products, arithmetic and copies ran while one was open for 7% -> 2% of each run, Pallas kernels for 31% -> 34%
where the time goes in v4:
time: 215 us
  Pallas kernels  152 us (71%)
  starting transfers between devices  46.9 us (22%)
  waiting for transfers between devices  6.89 us (3%)
  local copies, waits for them, and re-layouts  4.79 us (2%)
  other arithmetic  2.66 us (1%)
    pallas_call x1, Pallas kernels, per_device(): pl.pallas_call(feed_kernel, grid=(pixels // tile,), in_specs=[SCALARS, pi...  63.6 us
    ppermute x23, starting transfers between devices, swap(): return lax.ppermute(block, axis, [(i, i ^ bit) for i in range(count)])  38.8 us
    pallas_call x2, Pallas kernels, rows_back(): pl.pallas_call(functools.partial(rows_back_kernel, part * count), grid=(b...  18.5 us
    pallas_call x1, Pallas kernels, rows_grad(): pl.pallas_call(rows_grad_kernel, grid=(blocks,), in_specs=[SCALARS, lane_...  13.7 us
    pallas_call x1, Pallas kernels, per_device(): pl.pallas_call(cols_kernel, grid=(groups,), in_specs=[SCALARS, whole((2,...  13.5 us
    pallas_call x1, Pallas kernels, per_device(): pl.pallas_call(rows_kernel, grid=(blocks,), in_specs=[SCALARS, lane_block...  13.3 us
    pallas_call x1, Pallas kernels, cols_back(): pl.pallas_call(cols_back_kernel, grid=(groups,), in_specs=[SCALARS, whole...  11.2 us
    pallas_call x1, Pallas kernels, per_device(): pl.pallas_call(cols_grad_kernel, grid=(groups,), in_specs=[whole((size, 2...  8.77 us
  transfers between devices with their start and end apart: 31, of which 8 were waited for; matrix products, arithmetic and copies ran while one was open for 2% of the time, Pallas kernels for 34%

profile of v4, /device:TPU:0, one launch (start us, length us, event | category | flops | bytes accessed | tf_op | source)
XLA Modules:
  0.0 214.8 jit_solution(9448669575684807165)
XLA Ops:
  0.7 1.3 constant_dynamic-slice_fusion.8
  2.0 0.7 collective-permute-start.1
  2.7 4.3 %collective-permute-start = (bf16[7,96,384]{2,1,0:T(8,128)(2,1)S(1)}, bf16[7,96,384]{2,1,0:T(8,128)(2,1)S(1)}, u32[]{:S(2)}, u32[]{:S(2)}) collective-permute-start(bf16[7,96,384]{2,1,0:T(8,128)(2,1)S(1)} %get-tuple-element.137), channel_id=1, source_target_pairs={{0,8},{8,0},{16,24},{24,16},{1,9},{9,1},{17,25},{25,17},{2,10},{10... | collective-permute-start | bytes 1548296 | tf_op jit(solution)/shard_map/ppermute | solution.py:24
  7.0 1.9 constant_dynamic-slice_fusion.9
  9.0 1.5 collective-permute-start.2
  10.5 0.7 collective-permute-start.3
  11.2 3.3 %taps.1 = (f32[2,16,384]{2,1,0:T(8,128)}, f32[3,56,384]{2,1,0:T(8,128)}, bf16[112,224]{1,0:T(8,128)(2,1)}, s32[72,128]{1,0:T(8,128)}, f32[2,32,384]{2,1,0:T(8,128)}, /*index=5*/f32[2,32,384]{2,1,0:T(8,128)}) custom-call(s32[3]{0:T(128)} %heights_ref.1, f32[2,32,384]{2,1,0:T(8,128)} %bitcast.24, f32[2,32,384]{2,1,0:T(8,128)} %bitcast.26, ...), custom_call_target="tpu_custom_call" | custom-call | flops 5000000 | bytes 5000 | tf_op jit(solution)/shard_map/taps/pallas_call | solution.py:632
  14.6 0.7 collective-permute-start.5
  15.3 6.0 %collective-permute-start.4 = (bf16[14,8,384]{2,1,0:T(8,128)(2,1)S(1)}, bf16[14,8,384]{2,1,0:T(8,128)(2,1)S(1)}, u32[]{:S(2)}, u32[]{:S(2)}) collective-permute-start(bf16[14,8,384]{2,1,0:T(8,128)(2,1)S(1)} %pad_maximum_fusion.2), channel_id=1, source_target_pairs={{0,1},{1,0},{2,3},{3,2},{4,5},{5,4},{6,7},{7,6},{8,9},{9,8},{10,11... | collective-permute-start | bytes 258056 | tf_op jit(solution)/shard_map/ppermute | solution.py:24
  21.3 13.3 %rows_forward.1.partial_ref = bf16[64,96,384]{2,1,0:T(8,128)(2,1)} custom-call(s32[72,128]{1,0:T(8,128)} %get-tuple-element.77.source_ref, f32[2,16,384]{2,1,0:T(8,128)} %get-tuple-element.82.taps_ref, bf16[64,96,384]{2,1,0:T(8,128)(2,1)} %image.1, bf16[7,96,384]{2,1,0:T(8,128)(2,1)} %copy-done.2, bf16[7,96,384]{2,1,0:T(8,128)(2,1)} %copy-done.1), custom_call_target="tpu_custom_call" | custom-call | flops 14000000 | bytes 14000 | tf_op jit(solution)/shard_map/rows_forward/pallas_call | solution.py:649
  34.7 0.7 copy-done.5
  35.5 13.5 %cols_forward.1 = (f32[64,96,384]{2,1,0:T(8,128)}, bf16[64,112,384]{2,1,0:T(8,128)(2,1)}) custom-call(s32[72,128]{1,0:T(8,128)} %get-tuple-element.77.source_ref, f32[2,16,384]{2,1,0:T(8,128)} %get-tuple-element.82.taps_ref, f32[384]{0:T(512)} %skip_ref.1, f32[3,56,384]{2,1,0:T(8,128)} %get-tuple-element.79.factor_ref, ...), custom_call_target="tpu_custom_call" | custom-call | flops 14000000 | bytes 14000 | tf_op jit(solution)/shard_map/cols_forward/pallas_call | solution.py:664
  49.0 63.6 %feed_forward.1 = (bf16[6144,384]{1,0:T(8,128)(2,1)}, bf16[6144,384]{1,0:T(8,128)(2,1)}, bf16[512,384]{1,0:T(8,128)(2,1)}, bf16[512,384]{1,0:T(8,128)(2,1)}, f32...) custom-call(s32[72,128]{1,0:T(8,128)} %get-tuple-element.77.source_ref, f32[6144,384]{1,0:T(8,128)} %bitcast.23, ...), custom_call_target="tpu_custom_call" | custom-call | flops 70000000 | bytes 70000 | tf_op jit(solution)/shard_map/feed_forward/pallas_call | solution.py:691
  112.8 1.4 collective-permute-start.9
  114.2 8.8 %cols_grad.1 = f32[16,384]{1,0:T(8,128)} custom-call(bf16[112,192]{1,0:T(8,128)(2,1)} %constant.119.clone.own_ref, f32[16,168]{1,0:T(8,128)} %constant.120.clone.lags_ref, bf16[64,96,384]{2,1,0:T(8,128)(2,1)} %bitcast.18, bf16[64,112,384]{2,1,0:T(8,128)(2,1)} %get-tuple-element.89.spectrum_ref, bf16[64,96,384]{2,1,0:T(8,128)(2,1)} %image.1), custom_call_target="tpu_custom_call" | custom-call | flops 8000000 | bytes 8000 | tf_op jit(solution)/shard_map/cols_grad/pallas_call | solution.py:732
  123.0 1.1 split.1
  124.1 5.1 %collective-permute-start.10 = (bf16[96,1536]{1,0:T(8,128)(2,1)}, bf16[96,1536]{1,0:T(8,128)(2,1)S(1)}, u32[]{:S(2)}, u32[]{:S(2)}) collective-permute-start(bf16[96,1536]{1,0:T(8,128)(2,1)} %get-tuple-element.93), channel_id=1, source_target_pairs={{0,1},{1,0},{2,3},{3,2},{4,5},{5,4},{6,7},{7,6},{8,9},{9,8},{10,11... | collective-permute-start | bytes 884744 | tf_op jit(solution)/shard_map/ppermute | solution.py:24
  129.1 1.5 collective-permute-start.11
  130.6 0.5 collective-permute-done.8
  131.1 11.2 %cols_back.1 = (bf16[64,96,384]{2,1,0:T(8,128)(2,1)}, bf16[7,96,384]{2,1,0:T(8,128)(2,1)}, bf16[7,96,384]{2,1,0:T(8,128)(2,1)}) custom-call(s32[72,128]{1,0:T(8,128)} %get-tuple-element.77.source_ref, f32[3,56,384]{2,1,0:T(8,128)} %get-tuple-element.79.factor_ref, bf16[112,224]{1,0:T(8,128)(2,1)} %get-tuple-element.80.forward_ref, ...), custom_call_target="tpu_custom_call" | custom-call | flops 12000000 | bytes 12000 | tf_op jit(solution)/shard_map/cols_back/pallas_call | solution.py:763
  142.3 1.2 collective-permute-done.10
  143.4 0.5 collective-permute-done.11
  144.1 3.3 %collective-permute-start.12 = (f32[24,1536]{1,0:T(8,128)S(1)}, f32[24,1536]{1,0:T(8,128)S(1)}, u32[]{:S(2)}, u32[]{:S(2)}) collective-permute-start(f32[24,1536]{1,0:T(8,128)S(1)} %get-tuple-element.147), channel_id=1, source_target_pairs={{0,2},{1,3},{2,0},{3,1},{4,6},{5,7},{6,4},{7,5},{8,10},{9,11},{10,... | collective-permute-start | bytes 442376 | tf_op jit(solution)/shard_map/ppermute | solution.py:24
  147.3 2.4 %collective-permute-start.13 = (f32[24,1536]{1,0:T(8,128)S(1)}, f32[24,1536]{1,0:T(8,128)S(1)}, u32[]{:S(2)}, u32[]{:S(2)}) collective-permute-start(f32[24,1536]{1,0:T(8,128)S(1)} %get-tuple-element.145), channel_id=1, source_target_pairs={{0,4},{1,5},{2,6},{3,7},{4,0},{5,1},{6,2},{7,3},{8,12},{9,13},{10,... | collective-permute-start | bytes 442376 | tf_op jit(solution)/shard_map/ppermute | solution.py:24
  149.8 0.7 collective-permute-start.17
  150.5 13.7 %rows_grad.1 = f32[16,384]{1,0:T(8,128)} custom-call(s32[72,128]{1,0:T(8,128)} %get-tuple-element.77.source_ref, bf16[64,96,384]{2,1,0:T(8,128)(2,1)} %get-tuple-element.104.d_partial_ref.beside, bf16[64,96,384]{2,1,0:T(8,128)(2,1)} %image.1, bf16[7,96,384]{2,1,0:T(8,128)(2,1)} %copy-done.2, bf16[7,96,384]{2,1,0:T(8,128)(2,1)} %copy-done.1), custom_call_target="tpu_custom_call" | custom-call | flops 14000000 | bytes 14000 | tf_op jit(solution)/shard_map/rows_grad/pallas_call | solution.py:792
  164.4 0.8 pad_maximum_fusion.4
  165.2 1.7 collective-permute-start.18
  166.9 0.6 broadcast_in_dim.9.skip_ref
  167.5 3.7 %collective-permute-start.20 = (bf16[24,1536]{1,0:T(8,128)(2,1)S(1)}, bf16[24,1536]{1,0:T(8,128)(2,1)S(1)}, u32[]{:S(2)}, u32[]{:S(2)}) collective-permute-start(bf16[24,1536]{1,0:T(8,128)(2,1)S(1)} %add_add_fusion), channel_id=1, source_target_pairs={{0,6},{1,7},{2,4},{3,5},{4,2},{5,3},{6,0},{7,1},{8,14},{9,15},{10,... | collective-permute-start | bytes 221192 | tf_op jit(solution)/shard_map/ppermute | solution.py:24
  171.2 0.7 collective-permute-start.15
  171.9 0.7 fusion
  172.6 1.6 collective-permute-start.21
  174.2 1.5 collective-permute-start.22
  175.8 1.2 collective-permute-start.23
  177.2 1.9 collective-permute-done.22
  179.1 1.7 collective-permute-done.23
  181.1 2.9 %collective-permute-start.25 = (f32[40,384]{1,0:T(8,128)S(1)}, f32[40,384]{1,0:T(8,128)S(1)}, u32[]{:S(2)}, u32[]{:S(2)}) collective-permute-start(f32[40,384]{1,0:T(8,128)S(1)} %add_add_fusion.2), channel_id=1, source_target_pairs={{0,4},{1,5},{2,6},{3,7},{4,0},{5,1},{6,2},{7,3},{8,12},{9,13},{10,... | collective-permute-start | bytes 184328 | tf_op jit(solution)/shard_map/ppermute | solution.py:24
  184.0 1.4 collective-permute-start.26
  185.4 9.3 %rows_back.2.rest_0_ = bf16[64,96,384]{2,1,0:T(8,128)(2,1)} custom-call(s32[72,128]{1,0:T(8,128)} %get-tuple-element.77.source_ref, f32[2,16,384]{2,1,0:T(8,128)} %get-tuple-element.82.taps_ref, f32[1,384]{1,0:T(1,128)} %broadcast_in_dim.9.skip_ref, bf16[64,96,384]{2,1,0:T(8,128)(2,1)} %get-tuple-element.104.d_partial_ref.beside, ...), custom_call_target="tpu_custom_call" | custom-call | flops 8000000 | bytes 8000 | tf_op jit(solution)/shard_map/rows_back/pallas_call | solution.py:826
  194.7 0.6 add_add_fusion.1.g_ref
  195.4 1.2 collective-permute-start.29
  196.6 0.8 collective-permute-start.28
  197.4 1.5 collective-permute-start.27
  198.9 9.2 %rows_back.3 = bf16[64,96,384]{2,1,0:T(8,128)(2,1)} custom-call(s32[72,128]{1,0:T(8,128)} %get-tuple-element.77.source_ref, f32[2,16,384]{2,1,0:T(8,128)} %get-tuple-element.82.taps_ref, f32[1,384]{1,0:T(1,128)} %broadcast_in_dim.9.skip_ref, bf16[64,96,384]{2,1,0:T(8,128)(2,1)} %get-tuple-element.104.d_partial_ref.beside, ...), custom_call_target="tpu_custom_call", output_to_operand_aliasing={{}: (9, {})} | custom-call | flops 8000000 | bytes 8000 | tf_op jit(solution)/shard_map/rows_back/pallas_call | solution.py:826
  208.1 0.6 collective-permute-done.27
  209.0 2.5 %taps_grad.1 = (f32[2,32,384]{2,1,0:T(8,128)}, f32[2,32,384]{2,1,0:T(8,128)}, f32[2,32,384]{2,1,0:T(8,128)}, f32[2,32,384]{2,1,0:T(8,128)}, f32[2,384]{1,0:T(2,1...) custom-call(f32[2,32,384]{2,1,0:T(8,128)} %get-tuple-element.119.zr_, ...), custom_call_target="tpu_custom_call" | custom-call | flops 3000000 | bytes 3000 | tf_op jit(solution)/shard_map/taps_grad/pallas_call | solution.py:874
  211.9 2.9 %weight_grads.1 = (f32[384,1536]{1,0:T(8,128)}, f32[1536,384]{1,0:T(8,128)}) custom-call(s32[1]{0:T(128)} %bitcast.16.side_ref, bf16[384,1536]{1,0:T(8,128)(2,1)S(1)} %pad_maximum_fusion.own_ref, bf16[384,1536]{1,0:T(8,128)(2,1)S(1)} %collective-permute-done.30.other_ref), custom_call_target="tpu_custom_call" | custom-call | flops 3000000 | bytes 3000 | tf_op jit(solution)/shard_map/weight_grads/pallas_call | solution.py:860
  (68 shorter events, 1.9 us)
Async XLA Ops:
  2.0 12.5 %collective-permute-start.1 = (bf16[7,96,384]{2,1,0:T(8,128)(2,1)S(1)}, bf16[7,96,384]{2,1,0:T(8,128)(2,1)S(1)}, u32[]{:S(2)}, u32[]{:S(2)}) collective-permute-start(bf16[7,96,384]{2,1,0:T(8,128)(2,1)S(1)} %get-tuple-element.138), channel_id=1, source_target_pairs={{8,16},{16,8},{9,17},{17,9},{10,18},{18,10},{11,19},{19,11},{12,20... | collective-permute-start | bytes 1548296 | tf_op jit(solution)/shard_map/ppermute | solution.py:30
  2.7 11.9 %collective-permute-start = (bf16[7,96,384]{2,1,0:T(8,128)(2,1)S(1)}, bf16[7,96,384]{2,1,0:T(8,128)(2,1)S(1)}, u32[]{:S(2)}, u32[]{:S(2)}) collective-permute-start(bf16[7,96,384]{2,1,0:T(8,128)(2,1)S(1)} %get-tuple-element.137), channel_id=1, source_target_pairs={{0,8},{8,0},{16,24},{24,16},{1,9},{9,1},{17,25},{25,17},{2,10},{10... | collective-permute-start | bytes 1548296 | tf_op jit(solution)/shard_map/ppermute | solution.py:24
  9.0 25.6 %collective-permute-start.2 = (bf16[64,8,384]{2,1,0:T(8,128)(2,1)}, bf16[64,8,384]{2,1,0:T(8,128)(2,1)S(1)}, u32[]{:S(2)}, u32[]{:S(2)}) collective-permute-start(bf16[64,8,384]{2,1,0:T(8,128)(2,1)} %get-tuple-element.140), channel_id=1, source_target_pairs={{0,1},{1,0},{2,3},{3,2},{4,5},{5,4},{6,7},{7,6},{8,9},{9,8},{10,11... | collective-permute-start | bytes 1179656 | tf_op jit(solution)/shard_map/ppermute | solution.py:24
  10.5 24.1 %collective-permute-start.3 = (bf16[64,8,384]{2,1,0:T(8,128)(2,1)S(1)}, bf16[64,8,384]{2,1,0:T(8,128)(2,1)S(1)}, u32[]{:S(2)}, u32[]{:S(2)}) collective-permute-start(bf16[64,8,384]{2,1,0:T(8,128)(2,1)S(1)} %get-tuple-element.139), channel_id=1, source_target_pairs={{1,2},{3,4},{5,6},{2,1},{4,3},{6,5},{9,10},{11,12},{13,14},{10,9},... | collective-permute-start | bytes 1179656 | tf_op jit(solution)/shard_map/ppermute | solution.py:30
  14.5 6.8 %copy-start.1 = (bf16[7,96,384]{2,1,0:T(8,128)(2,1)}, bf16[7,96,384]{2,1,0:T(8,128)(2,1)S(1)}, u32[]{:S(2)}) copy-start(bf16[7,96,384]{2,1,0:T(8,128)(2,1)S(1)} %collective-permute-done.1.other) | copy-start | bytes 1548292
  14.6 6.7 %copy-start.2 = (bf16[7,96,384]{2,1,0:T(8,128)(2,1)}, bf16[7,96,384]{2,1,0:T(8,128)(2,1)S(1)}, u32[]{:S(2)}) copy-start(bf16[7,96,384]{2,1,0:T(8,128)(2,1)S(1)} %collective-permute-done.near) | copy-start | bytes 1548292
  14.6 20.0 %collective-permute-start.5 = (bf16[14,8,384]{2,1,0:T(8,128)(2,1)S(1)}, bf16[14,8,384]{2,1,0:T(8,128)(2,1)S(1)}, u32[]{:S(2)}, u32[]{:S(2)}) collective-permute-start(bf16[14,8,384]{2,1,0:T(8,128)(2,1)S(1)} %pad_maximum_fusion.3), channel_id=1, source_target_pairs={{1,2},{3,4},{5,6},{2,1},{4,3},{6,5},{9,10},{11,12},{13,14},{10,9},... | collective-permute-start | bytes 258056 | tf_op jit(solution)/shard_map/ppermute | solution.py:30
  15.3 19.3 %collective-permute-start.4 = (bf16[14,8,384]{2,1,0:T(8,128)(2,1)S(1)}, bf16[14,8,384]{2,1,0:T(8,128)(2,1)S(1)}, u32[]{:S(2)}, u32[]{:S(2)}) collective-permute-start(bf16[14,8,384]{2,1,0:T(8,128)(2,1)S(1)} %pad_maximum_fusion.2), channel_id=1, source_target_pairs={{0,1},{1,0},{2,3},{3,2},{4,5},{5,4},{6,7},{7,6},{8,9},{9,8},{10,11... | collective-permute-start | bytes 258056 | tf_op jit(solution)/shard_map/ppermute | solution.py:24
  34.6 0.7 copy-start.5
  34.6 0.9 copy-start.6
  34.6 0.9 copy-start.8
  34.7 0.9 copy-start.9
  112.6 10.4 %collective-permute-start.6 = (bf16[384,1536]{1,0:T(8,128)(2,1)}, bf16[384,1536]{1,0:T(8,128)(2,1)S(1)}, u32[]{:S(2)}, u32[]{:S(2)}) collective-permute-start(bf16[384,1536]{1,0:T(8,128)(2,1)} %get-tuple-element.85), channel_id=1, source_target_pairs={{0,8},{8,0},{16,24},{24,16},{1,9},{9,1},{17,25},{25,17},{2,10},{10... | collective-permute-start | bytes 3538952 | tf_op jit(solution)/shard_map/ppermute | solution.py:24
  112.7 18.3 %collective-permute-start.8 = (bf16[512,384]{1,0:T(8,128)(2,1)}, bf16[512,384]{1,0:T(8,128)(2,1)}, u32[]{:S(2)}, u32[]{:S(2)}) collective-permute-start(bf16[512,384]{1,0:T(8,128)(2,1)} %get-tuple-element.96), channel_id=1, source_target_pairs={{0,1},{1,0},{2,3},{3,2},{4,5},{5,4},{6,7},{7,6},{8,9},{9,8},{10,11... | collective-permute-start | bytes 1179656 | tf_op jit(solution)/shard_map/ppermute | solution.py:24
  112.8 18.2 %collective-permute-start.9 = (bf16[512,384]{1,0:T(8,128)(2,1)}, bf16[512,384]{1,0:T(8,128)(2,1)}, u32[]{:S(2)}, u32[]{:S(2)}) collective-permute-start(bf16[512,384]{1,0:T(8,128)(2,1)} %get-tuple-element.97), channel_id=1, source_target_pairs={{1,2},{3,4},{5,6},{2,1},{4,3},{6,5},{9,10},{11,12},{13,14},{10,9},... | collective-permute-start | bytes 1179656 | tf_op jit(solution)/shard_map/ppermute | solution.py:30
  114.2 8.8 %copy-start = (f32[384,1536]{1,0:T(8,128)S(1)}, f32[384,1536]{1,0:T(8,128)}, u32[]{:S(2)}) copy-start(f32[384,1536]{1,0:T(8,128)} %get-tuple-element.87.keep_ref) | copy-start | bytes 7077892
  124.1 18.2 %collective-permute-start.7 = (bf16[96,1536]{1,0:T(8,128)(2,1)}, bf16[96,1536]{1,0:T(8,128)(2,1)S(1)}, u32[]{:S(2)}, u32[]{:S(2)}) collective-permute-start(bf16[96,1536]{1,0:T(8,128)(2,1)} %get-tuple-element.92), channel_id=1, source_target_pairs={{0,16},{8,24},{16,0},{24,8},{1,17},{9,25},{17,1},{25,9},{2,18},{10... | collective-permute-start | bytes 884744 | tf_op jit(solution)/shard_map/ppermute | solution.py:24
  124.1 19.4 %collective-permute-start.10 = (bf16[96,1536]{1,0:T(8,128)(2,1)}, bf16[96,1536]{1,0:T(8,128)(2,1)S(1)}, u32[]{:S(2)}, u32[]{:S(2)}) collective-permute-start(bf16[96,1536]{1,0:T(8,128)(2,1)} %get-tuple-element.93), channel_id=1, source_target_pairs={{0,1},{1,0},{2,3},{3,2},{4,5},{5,4},{6,7},{7,6},{8,9},{9,8},{10,11... | collective-permute-start | bytes 884744 | tf_op jit(solution)/shard_map/ppermute | solution.py:24
  129.1 14.8 %collective-permute-start.11 = (bf16[96,1536]{1,0:T(8,128)(2,1)}, bf16[96,1536]{1,0:T(8,128)(2,1)S(1)}, u32[]{:S(2)}, u32[]{:S(2)}) collective-permute-start(bf16[96,1536]{1,0:T(8,128)(2,1)} %get-tuple-element.94), channel_id=1, source_target_pairs={{0,17},{1,16},{2,19},{3,18},{4,21},{5,20},{6,23},{7,22},{8,25},{9,... | collective-permute-start | bytes 884744 | tf_op jit(solution)/shard_map/ppermute | solution.py:552
  144.1 20.2 %collective-permute-start.12 = (f32[24,1536]{1,0:T(8,128)S(1)}, f32[24,1536]{1,0:T(8,128)S(1)}, u32[]{:S(2)}, u32[]{:S(2)}) collective-permute-start(f32[24,1536]{1,0:T(8,128)S(1)} %get-tuple-element.147), channel_id=1, source_target_pairs={{0,2},{1,3},{2,0},{3,1},{4,6},{5,7},{6,4},{7,5},{8,10},{9,11},{10,... | collective-permute-start | bytes 442376 | tf_op jit(solution)/shard_map/ppermute | solution.py:24
  147.3 16.9 %collective-permute-start.13 = (f32[24,1536]{1,0:T(8,128)S(1)}, f32[24,1536]{1,0:T(8,128)S(1)}, u32[]{:S(2)}, u32[]{:S(2)}) collective-permute-start(f32[24,1536]{1,0:T(8,128)S(1)} %get-tuple-element.145), channel_id=1, source_target_pairs={{0,4},{1,5},{2,6},{3,7},{4,0},{5,1},{6,2},{7,3},{8,12},{9,13},{10,... | collective-permute-start | bytes 442376 | tf_op jit(solution)/shard_map/ppermute | solution.py:24
  149.7 14.6 %collective-permute-start.14 = (f32[24,1536]{1,0:T(8,128)S(1)}, f32[24,1536]{1,0:T(8,128)S(1)}, u32[]{:S(2)}, u32[]{:S(2)}) collective-permute-start(f32[24,1536]{1,0:T(8,128)S(1)} %get-tuple-element.146), channel_id=1, source_target_pairs={{0,6},{1,7},{2,4},{3,5},{4,2},{5,3},{6,0},{7,1},{8,14},{9,15},{10,... | collective-permute-start | bytes 442376 | tf_op jit(solution)/shard_map/ppermute | solution.py:24
  149.8 14.5 %collective-permute-start.16 = (bf16[7,96,384]{2,1,0:T(8,128)(2,1)}, bf16[7,96,384]{2,1,0:T(8,128)(2,1)S(1)}, u32[]{:S(2)}, u32[]{:S(2)}) collective-permute-start(bf16[7,96,384]{2,1,0:T(8,128)(2,1)} %get-tuple-element.99), channel_id=1, source_target_pairs={{0,8},{8,0},{16,24},{24,16},{1,9},{9,1},{17,25},{25,17},{2,10},{10... | collective-permute-start | bytes 1548296 | tf_op jit(solution)/shard_map/ppermute | solution.py:24
  149.8 14.5 %collective-permute-start.17 = (bf16[7,96,384]{2,1,0:T(8,128)(2,1)}, bf16[7,96,384]{2,1,0:T(8,128)(2,1)S(1)}, u32[]{:S(2)}, u32[]{:S(2)}) collective-permute-start(bf16[7,96,384]{2,1,0:T(8,128)(2,1)} %get-tuple-element.100), channel_id=1, source_target_pairs={{8,16},{16,8},{9,17},{17,9},{10,18},{18,10},{11,19},{19,11},{12,20... | collective-permute-start | bytes 1548296 | tf_op jit(solution)/shard_map/ppermute | solution.py:30
  150.5 13.9 %copy-start.7 = (f32[16,384]{1,0:T(8,128)S(1)}, f32[16,384]{1,0:T(8,128)}, u32[]{:S(2)}) copy-start(f32[16,384]{1,0:T(8,128)} %cols_grad.1) | copy-start | bytes 73732
  150.5 13.9 %copy-start.10 = (f32[8,384]{1,0:T(8,128)S(1)}, f32[8,384]{1,0:T(8,128)}, u32[]{:S(2)}) copy-start(f32[8,384]{1,0:T(8,128)} %get-tuple-element.109) | copy-start | bytes 36868
  150.5 16.4 %copy-start.11 = (f32[384]{0:T(512)S(1)}, f32[384]{0:T(512)}, u32[]{:S(2)}) copy-start(f32[384]{0:T(512)} %skip_ref.1) | copy-start | bytes 4612
  164.3 21.0 %copy-start.3 = (bf16[7,96,384]{2,1,0:T(8,128)(2,1)}, bf16[7,96,384]{2,1,0:T(8,128)(2,1)S(1)}, u32[]{:S(2)}) copy-start(bf16[7,96,384]{2,1,0:T(8,128)(2,1)S(1)} %collective-permute-done.16.near) | copy-start | bytes 1548292
  164.4 21.0 %copy-start.4 = (bf16[7,96,384]{2,1,0:T(8,128)(2,1)}, bf16[7,96,384]{2,1,0:T(8,128)(2,1)S(1)}, u32[]{:S(2)}) copy-start(bf16[7,96,384]{2,1,0:T(8,128)(2,1)S(1)} %collective-permute-done.17.other) | copy-start | bytes 1548292
  165.2 6.7 %collective-permute-start.18 = (f32[40,384]{1,0:T(8,128)S(1)}, f32[40,384]{1,0:T(8,128)S(1)}, u32[]{:S(2)}, u32[]{:S(2)}) collective-permute-start(f32[40,384]{1,0:T(8,128)S(1)} %pad_maximum_fusion.4), channel_id=1, source_target_pairs={{0,8},{8,0},{16,24},{24,16},{1,9},{9,1},{17,25},{25,17},{2,10},{10... | collective-permute-start | bytes 184328 | tf_op jit(solution)/shard_map/ppermute | solution.py:24
  167.5 8.3 %collective-permute-start.20 = (bf16[24,1536]{1,0:T(8,128)(2,1)S(1)}, bf16[24,1536]{1,0:T(8,128)(2,1)S(1)}, u32[]{:S(2)}, u32[]{:S(2)}) collective-permute-start(bf16[24,1536]{1,0:T(8,128)(2,1)S(1)} %add_add_fusion), channel_id=1, source_target_pairs={{0,6},{1,7},{2,4},{3,5},{4,2},{5,3},{6,0},{7,1},{8,14},{9,15},{10,... | collective-permute-start | bytes 221192 | tf_op jit(solution)/shard_map/ppermute | solution.py:24
  171.2 5.8 %collective-permute-start.19 = (bf16[24,1536]{1,0:T(8,128)(2,1)S(1)}, bf16[24,1536]{1,0:T(8,128)(2,1)S(1)}, u32[]{:S(2)}, u32[]{:S(2)}) collective-permute-start(bf16[24,1536]{1,0:T(8,128)(2,1)S(1)} %add_add_fusion), channel_id=1, source_target_pairs={{0,2},{1,3},{2,0},{3,1},{4,6},{5,7},{6,4},{7,5},{8,10},{9,11},{10,... | collective-permute-start | bytes 221192 | tf_op jit(solution)/shard_map/ppermute | solution.py:24
  171.2 6.0 %collective-permute-start.15 = (bf16[24,1536]{1,0:T(8,128)(2,1)S(1)}, bf16[24,1536]{1,0:T(8,128)(2,1)S(1)}, u32[]{:S(2)}, u32[]{:S(2)}) collective-permute-start(bf16[24,1536]{1,0:T(8,128)(2,1)S(1)} %add_add_fusion), channel_id=1, source_target_pairs={{0,4},{1,5},{2,6},{3,7},{4,0},{5,1},{6,2},{7,3},{8,12},{9,13},{10,... | collective-permute-start | bytes 221192 | tf_op jit(solution)/shard_map/ppermute | solution.py:24
  172.6 4.6 %collective-permute-start.21 = (f32[40,384]{1,0:T(8,128)S(1)}, f32[40,384]{1,0:T(8,128)S(1)}, u32[]{:S(2)}, u32[]{:S(2)}) collective-permute-start(f32[40,384]{1,0:T(8,128)S(1)} %fusion), channel_id=1, source_target_pairs={{0,16},{8,24},{16,0},{24,8},{1,17},{9,25},{17,1},{25,9},{2,18},{10... | collective-permute-start | bytes 184328 | tf_op jit(solution)/shard_map/ppermute | solution.py:24
  174.2 4.9 %collective-permute-start.22 = (f32[40,384]{1,0:T(8,128)S(1)}, f32[40,384]{1,0:T(8,128)S(1)}, u32[]{:S(2)}, u32[]{:S(2)}) collective-permute-start(f32[40,384]{1,0:T(8,128)S(1)} %fusion), channel_id=1, source_target_pairs={{0,1},{1,0},{2,3},{3,2},{4,5},{5,4},{6,7},{7,6},{8,9},{9,8},{10,11... | collective-permute-start | bytes 184328 | tf_op jit(solution)/shard_map/ppermute | solution.py:24
  175.8 5.1 %collective-permute-start.23 = (f32[40,384]{1,0:T(8,128)S(1)}, f32[40,384]{1,0:T(8,128)S(1)}, u32[]{:S(2)}, u32[]{:S(2)}) collective-permute-start(f32[40,384]{1,0:T(8,128)S(1)} %fusion), channel_id=1, source_target_pairs={{0,17},{1,16},{2,19},{3,18},{4,21},{5,20},{6,23},{7,22},{8,25},{9,... | collective-permute-start | bytes 184328 | tf_op jit(solution)/shard_map/ppermute | solution.py:552
  180.9 13.8 %collective-permute-start.24 = (f32[40,384]{1,0:T(8,128)S(1)}, f32[40,384]{1,0:T(8,128)S(1)}, u32[]{:S(2)}, u32[]{:S(2)}) collective-permute-start(f32[40,384]{1,0:T(8,128)S(1)} %add_add_fusion.2), channel_id=1, source_target_pairs={{0,2},{1,3},{2,0},{3,1},{4,6},{5,7},{6,4},{7,5},{8,10},{9,11},{10,... | collective-permute-start | bytes 184328 | tf_op jit(solution)/shard_map/ppermute | solution.py:24
  181.1 13.6 %collective-permute-start.25 = (f32[40,384]{1,0:T(8,128)S(1)}, f32[40,384]{1,0:T(8,128)S(1)}, u32[]{:S(2)}, u32[]{:S(2)}) collective-permute-start(f32[40,384]{1,0:T(8,128)S(1)} %add_add_fusion.2), channel_id=1, source_target_pairs={{0,4},{1,5},{2,6},{3,7},{4,0},{5,1},{6,2},{7,3},{8,12},{9,13},{10,... | collective-permute-start | bytes 184328 | tf_op jit(solution)/shard_map/ppermute | solution.py:24
  184.0 10.8 %collective-permute-start.26 = (f32[40,384]{1,0:T(8,128)S(1)}, f32[40,384]{1,0:T(8,128)S(1)}, u32[]{:S(2)}, u32[]{:S(2)}) collective-permute-start(f32[40,384]{1,0:T(8,128)S(1)} %add_add_fusion.2), channel_id=1, source_target_pairs={{0,6},{1,7},{2,4},{3,5},{4,2},{5,3},{6,0},{7,1},{8,14},{9,15},{10,... | collective-permute-start | bytes 184328 | tf_op jit(solution)/shard_map/ppermute | solution.py:24
  195.4 12.7 %collective-permute-start.29 = (bf16[96,1536]{1,0:T(8,128)(2,1)S(1)}, bf16[96,1536]{1,0:T(8,128)(2,1)S(1)}, u32[]{:S(2)}, u32[]{:S(2)}) collective-permute-start(bf16[96,1536]{1,0:T(8,128)(2,1)S(1)} %pad_maximum_fusion.1), channel_id=1, source_target_pairs={{0,17},{1,16},{2,19},{3,18},{4,21},{5,20},{6,23},{7,22},{8,25},{9,... | collective-permute-start | bytes 884744 | tf_op jit(solution)/shard_map/ppermute | solution.py:552
  196.6 11.5 %collective-permute-start.28 = (bf16[96,1536]{1,0:T(8,128)(2,1)S(1)}, bf16[96,1536]{1,0:T(8,128)(2,1)S(1)}, u32[]{:S(2)}, u32[]{:S(2)}) collective-permute-start(bf16[96,1536]{1,0:T(8,128)(2,1)S(1)} %pad_maximum_fusion.1), channel_id=1, source_target_pairs={{0,16},{8,24},{16,0},{24,8},{1,17},{9,25},{17,1},{25,9},{2,18},{10... | collective-permute-start | bytes 884744 | tf_op jit(solution)/shard_map/ppermute | solution.py:24
  197.4 11.4 %collective-permute-start.27 = (bf16[96,1536]{1,0:T(8,128)(2,1)S(1)}, bf16[96,1536]{1,0:T(8,128)(2,1)S(1)}, u32[]{:S(2)}, u32[]{:S(2)}) collective-permute-start(bf16[96,1536]{1,0:T(8,128)(2,1)S(1)} %pad_maximum_fusion.1), channel_id=1, source_target_pairs={{0,1},{1,0},{2,3},{3,2},{4,5},{5,4},{6,7},{7,6},{8,9},{9,8},{10,11... | collective-permute-start | bytes 884744 | tf_op jit(solution)/shard_map/ppermute | solution.py:24
  208.9 2.9 %collective-permute-start.30 = (bf16[384,1536]{1,0:T(8,128)(2,1)S(1)}, bf16[384,1536]{1,0:T(8,128)(2,1)S(1)}, u32[]{:S(2)}, u32[]{:S(2)}) collective-permute-start(bf16[384,1536]{1,0:T(8,128)(2,1)S(1)} %pad_maximum_fusion.own_ref), channel_id=1, source_target_pairs={{0,8},{8,0},{16,24},{24,16},{1,9},{9,1},{17,25},{25,17},{2,10},{10... | collective-permute-start | bytes 3538952 | tf_op jit(solution)/shard_map/ppermute | solution.py:24

commit v5 on v4

--- a/solution.py
+++ b/solution.py
@@ -109,7 +109,7 @@
 
 
 def taps_kernel(
-    height, heights_ref, rate_ref, freq_ref, cr_ref, ci_ref, log_step_ref, response_ref, straight_ref, swapped_ref,
+    height, heights_ref, rate_ref, freq_ref, cr_ref, ci_ref, log_step_ref, skip_ref, response_ref, straight_ref, swapped_ref,
     taps_ref, factor_ref, forward_ref, source_ref, zr_ref, zi_ref,
 ):
     half = factor_ref.shape[1]
@@ -124,7 +124,8 @@
         for m in range(KSIZE):
             taps_ref[d, m] = 2.0 * jnp.sum(cr * ur - ci * ui, axis=0)
             ur, ui = ur * zr - ui * zi, ur * zi + ui * zr
-        taps_ref[d, KSIZE] = jnp.zeros_like(taps_ref[d, KSIZE])
+    taps_ref[0, KSIZE] = skip_ref[...]
+    taps_ref[1, KSIZE] = jnp.zeros_like(skip_ref[...])
     factor = dot(response_ref[...], taps_ref[1], lax.Precision.HIGHEST)
     for k in range(3):
         factor_ref[k] = factor[k * half : (k + 1) * half]
@@ -393,7 +394,7 @@
 
 
 def rows_back_kernel(
-    first, source_ref, taps_ref, skip_ref, d_partial_ref, beside, near, other, d_mixed_ref, grad_ref, *rest
+    first, source_ref, taps_ref, d_partial_ref, beside, near, other, d_mixed_ref, grad_ref, *rest
 ):
     image_grad_ref, ext = rest[-2:]
     count = d_partial_ref.shape[0]
@@ -407,7 +408,7 @@
         ext[REACH + beyond + i] = beside[i].astype(F32)
     load_rows(ext, REACH + first, d_partial_ref)
     taps = [taps_ref[0, i][None, :] for i in range(KSIZE)]
-    skip = skip_ref[...]
+    skip = taps_ref[0, KSIZE][None, :]
 
     def row(r, _):
         for k in range(4):
@@ -631,7 +632,7 @@
     vmem = pl.BlockSpec(memory_space=pltpu.VMEM)
     taps, factor, forward, source, zr, zi = pl.pallas_call(
         functools.partial(taps_kernel, height),
-        in_specs=[SCALARS] + [vmem] * 8,
+        in_specs=[SCALARS] + [vmem] * 9,
         out_shape=[
             jax.ShapeDtypeStruct((2, KSIZE + 1, chans), F32),
             jax.ShapeDtypeStruct((3, half, chans), F32),
@@ -642,7 +643,7 @@
         ],
         cost_estimate=cost(5),
         name="taps",
-    )(image_heights, rate_t, freq_t, cr_t, ci_t, tie(log_step, *edges), response, straight, swapped)
+    )(image_heights, rate_t, freq_t, cr_t, ci_t, tie(log_step, *edges), skip, response, straight, swapped)
 
     near_strip, other_strip, strips = halo_cols(row_near, tie(row_other, taps))
     tile_shape = (height, width, chans)
@@ -817,8 +818,6 @@
     takes = [send(small) for send in exchanges(phases[0])]
     small = sum(takes, small)
 
-    skip_row = tie(skip, give)[None, :]
-
     def rows_back(part, before, *waits):
         count = height // 2
         lanes = lambda rows, block=0: pl.BlockSpec((rows, width, LANES), lambda c: (block, 0, c))
@@ -827,7 +826,7 @@
             functools.partial(rows_back_kernel, part * count),
             grid=(blocks,),
             in_specs=[
-                SCALARS, lane_block(2, KSIZE + 1), lane_block(1), at, lanes(EDGE, count // EDGE - part),
+                SCALARS, lane_block(2, KSIZE + 1), at, lanes(EDGE, count // EDGE - part),
                 lanes(REACH), lanes(REACH), at, at,
                 *([] if before is None else [pl.BlockSpec(memory_space=pl.ANY)]),
             ],
@@ -836,10 +835,10 @@
             scratch_shapes=[pltpu.VMEM((full + 1, width, LANES), F32)],
             compiler_params=params(),
             cost_estimate=cost(8),
-            input_output_aliases={} if before is None else {9: 0},
+            input_output_aliases={} if before is None else {8: 0},
             name="rows_back",
         )(
-            source, taps, tie(skip_row, *waits), d_partial, d_partial, d_near, d_other, d_mixed, out_grad,
+            source, tie(taps, *waits), d_partial, d_partial, d_near, d_other, d_mixed, out_grad,
             *([] if before is None else [before]),
         )
 

time: 215 us -> 214 us (level)
  transfers between devices with their start and end apart: 31 -> 31, of which waited for: 8 -> 8; matrix products, arithmetic and copies ran while one was open for 2% -> 1% of each run, Pallas kernels for 34% -> 34%
where the time goes in v5:
time: 214 us
  Pallas kernels  152 us (71%)
  starting transfers between devices  46.9 us (22%)
  waiting for transfers between devices  7.14 us (3%)
  local copies, waits for them, and re-layouts  4.22 us (2%)
  other arithmetic  2.67 us (1%)
    pallas_call x1, Pallas kernels, per_device(): pl.pallas_call(feed_kernel, grid=(pixels // tile,), in_specs=[SCALARS, pi...  63.6 us
    ppermute x23, starting transfers between devices, swap(): return lax.ppermute(block, axis, [(i, i ^ bit) for i in range(count)])  38.8 us
    pallas_call x2, Pallas kernels, rows_back(): pl.pallas_call(functools.partial(rows_back_kernel, part * count), grid=(b...  18 us
    pallas_call x1, Pallas kernels, rows_grad(): pl.pallas_call(rows_grad_kernel, grid=(blocks,), in_specs=[SCALARS, lane_...  13.7 us
    pallas_call x1, Pallas kernels, per_device(): pl.pallas_call(cols_kernel, grid=(groups,), in_specs=[SCALARS, whole((2,...  13.5 us
    pallas_call x1, Pallas kernels, per_device(): pl.pallas_call(rows_kernel, grid=(blocks,), in_specs=[SCALARS, lane_block...  13.3 us
    pallas_call x1, Pallas kernels, cols_back(): pl.pallas_call(cols_back_kernel, grid=(groups,), in_specs=[SCALARS, whole...  11.2 us
    pallas_call x1, Pallas kernels, per_device(): pl.pallas_call(cols_grad_kernel, grid=(groups,), in_specs=[whole((size, 2...  8.78 us
  transfers between devices with their start and end apart: 31, of which 8 were waited for; matrix products, arithmetic and copies ran while one was open for 1% of the time, Pallas kernels for 34%

profile of v5, /device:TPU:0, one launch (start us, length us, event | category | flops | bytes accessed | tf_op | source)
XLA Modules:
  0.0 213.9 jit_solution(4470868093061260865)
XLA Ops:
  0.7 1.3 constant_dynamic-slice_fusion.8
  2.0 0.7 collective-permute-start.1
  2.7 4.3 %collective-permute-start = (bf16[7,96,384]{2,1,0:T(8,128)(2,1)S(1)}, bf16[7,96,384]{2,1,0:T(8,128)(2,1)S(1)}, u32[]{:S(2)}, u32[]{:S(2)}) collective-permute-start(bf16[7,96,384]{2,1,0:T(8,128)(2,1)S(1)} %get-tuple-element.135), channel_id=1, source_target_pairs={{0,8},{8,0},{16,24},{24,16},{1,9},{9,1},{17,25},{25,17},{2,10},{10... | collective-permute-start | bytes 1548296 | tf_op jit(solution)/shard_map/ppermute | solution.py:24
  7.0 1.9 constant_dynamic-slice_fusion.9
  9.0 1.5 collective-permute-start.2
  10.5 0.7 collective-permute-start.3
  11.2 3.4 %taps.1 = (f32[2,16,384]{2,1,0:T(8,128)}, f32[3,56,384]{2,1,0:T(8,128)}, bf16[112,224]{1,0:T(8,128)(2,1)}, s32[72,128]{1,0:T(8,128)}, f32[2,32,384]{2,1,0:T(8,128)}, /*index=5*/f32[2,32,384]{2,1,0:T(8,128)}) custom-call(s32[3]{0:T(128)} %heights_ref.1, f32[2,32,384]{2,1,0:T(8,128)} %bitcast.24, f32[2,32,384]{2,1,0:T(8,128)} %bitcast.26, ...), custom_call_target="tpu_custom_call" | custom-call | flops 5000000 | bytes 5000 | tf_op jit(solution)/shard_map/taps/pallas_call | solution.py:633
  14.7 0.7 collective-permute-start.5
  15.4 6.0 %collective-permute-start.4 = (bf16[14,8,384]{2,1,0:T(8,128)(2,1)S(1)}, bf16[14,8,384]{2,1,0:T(8,128)(2,1)S(1)}, u32[]{:S(2)}, u32[]{:S(2)}) collective-permute-start(bf16[14,8,384]{2,1,0:T(8,128)(2,1)S(1)} %pad_maximum_fusion.2), channel_id=1, source_target_pairs={{0,1},{1,0},{2,3},{3,2},{4,5},{5,4},{6,7},{7,6},{8,9},{9,8},{10,11... | collective-permute-start | bytes 258056 | tf_op jit(solution)/shard_map/ppermute | solution.py:24
  21.3 13.3 %rows_forward.1.partial_ref = bf16[64,96,384]{2,1,0:T(8,128)(2,1)} custom-call(s32[72,128]{1,0:T(8,128)} %get-tuple-element.76.source_ref, f32[2,16,384]{2,1,0:T(8,128)} %get-tuple-element.116.taps_ref, bf16[64,96,384]{2,1,0:T(8,128)(2,1)} %image.1, bf16[7,96,384]{2,1,0:T(8,128)(2,1)} %copy-done.2, bf16[7,96,384]{2,1,0:T(8,128)(2,1)} %copy-done.1), custom_call_target="tpu_custom_call" | custom-call | flops 14000000 | bytes 14000 | tf_op jit(solution)/shard_map/rows_forward/pallas_call | solution.py:650
  34.7 0.7 copy-done.5
  35.6 13.5 %cols_forward.1 = (f32[64,96,384]{2,1,0:T(8,128)}, bf16[64,112,384]{2,1,0:T(8,128)(2,1)}) custom-call(s32[72,128]{1,0:T(8,128)} %get-tuple-element.76.source_ref, f32[2,16,384]{2,1,0:T(8,128)} %get-tuple-element.116.taps_ref, f32[384]{0:T(512)} %skip_ref.3, f32[3,56,384]{2,1,0:T(8,128)} %get-tuple-element.78.factor_ref, ...), custom_call_target="tpu_custom_call" | custom-call | flops 14000000 | bytes 14000 | tf_op jit(solution)/shard_map/cols_forward/pallas_call | solution.py:665
  49.1 63.6 %feed_forward.1 = (bf16[6144,384]{1,0:T(8,128)(2,1)}, bf16[6144,384]{1,0:T(8,128)(2,1)}, bf16[512,384]{1,0:T(8,128)(2,1)}, bf16[512,384]{1,0:T(8,128)(2,1)}, f32...) custom-call(s32[72,128]{1,0:T(8,128)} %get-tuple-element.76.source_ref, f32[6144,384]{1,0:T(8,128)} %bitcast.23, ...), custom_call_target="tpu_custom_call" | custom-call | flops 70000000 | bytes 70000 | tf_op jit(solution)/shard_map/feed_forward/pallas_call | solution.py:692
  112.9 1.4 collective-permute-start.9
  114.3 8.8 %cols_grad.1 = f32[16,384]{1,0:T(8,128)} custom-call(bf16[112,192]{1,0:T(8,128)(2,1)} %constant.119.clone.own_ref, f32[16,168]{1,0:T(8,128)} %constant.120.clone.lags_ref, bf16[64,96,384]{2,1,0:T(8,128)(2,1)} %bitcast.18, bf16[64,112,384]{2,1,0:T(8,128)(2,1)} %get-tuple-element.87.spectrum_ref, bf16[64,96,384]{2,1,0:T(8,128)(2,1)} %image.1), custom_call_target="tpu_custom_call" | custom-call | flops 8000000 | bytes 8000 | tf_op jit(solution)/shard_map/cols_grad/pallas_call | solution.py:733
  123.0 1.1 split.1
  124.1 5.1 %collective-permute-start.10 = (bf16[96,1536]{1,0:T(8,128)(2,1)}, bf16[96,1536]{1,0:T(8,128)(2,1)S(1)}, u32[]{:S(2)}, u32[]{:S(2)}) collective-permute-start(bf16[96,1536]{1,0:T(8,128)(2,1)} %get-tuple-element.91), channel_id=1, source_target_pairs={{0,1},{1,0},{2,3},{3,2},{4,5},{5,4},{6,7},{7,6},{8,9},{9,8},{10,11... | collective-permute-start | bytes 884744 | tf_op jit(solution)/shard_map/ppermute | solution.py:24
  129.2 1.5 collective-permute-start.11
  130.6 0.5 collective-permute-done.8
  131.1 11.2 %cols_back.1 = (bf16[64,96,384]{2,1,0:T(8,128)(2,1)}, bf16[7,96,384]{2,1,0:T(8,128)(2,1)}, bf16[7,96,384]{2,1,0:T(8,128)(2,1)}) custom-call(s32[72,128]{1,0:T(8,128)} %get-tuple-element.76.source_ref, f32[3,56,384]{2,1,0:T(8,128)} %get-tuple-element.78.factor_ref, bf16[112,224]{1,0:T(8,128)(2,1)} %get-tuple-element.79.forward_ref, ...), custom_call_target="tpu_custom_call" | custom-call | flops 12000000 | bytes 12000 | tf_op jit(solution)/shard_map/cols_back/pallas_call | solution.py:764
  142.3 1.1 collective-permute-done.10
  143.4 0.5 collective-permute-done.11
  144.1 3.3 %collective-permute-start.12 = (f32[24,1536]{1,0:T(8,128)S(1)}, f32[24,1536]{1,0:T(8,128)S(1)}, u32[]{:S(2)}, u32[]{:S(2)}) collective-permute-start(f32[24,1536]{1,0:T(8,128)S(1)} %get-tuple-element.145), channel_id=1, source_target_pairs={{0,2},{1,3},{2,0},{3,1},{4,6},{5,7},{6,4},{7,5},{8,10},{9,11},{10,... | collective-permute-start | bytes 442376 | tf_op jit(solution)/shard_map/ppermute | solution.py:24
  147.4 2.3 %collective-permute-start.13 = (f32[24,1536]{1,0:T(8,128)S(1)}, f32[24,1536]{1,0:T(8,128)S(1)}, u32[]{:S(2)}, u32[]{:S(2)}) collective-permute-start(f32[24,1536]{1,0:T(8,128)S(1)} %get-tuple-element.143), channel_id=1, source_target_pairs={{0,4},{1,5},{2,6},{3,7},{4,0},{5,1},{6,2},{7,3},{8,12},{9,13},{10,... | collective-permute-start | bytes 442376 | tf_op jit(solution)/shard_map/ppermute | solution.py:24
  149.8 0.7 collective-permute-start.17
  150.6 13.7 %rows_grad.1 = f32[16,384]{1,0:T(8,128)} custom-call(s32[72,128]{1,0:T(8,128)} %get-tuple-element.76.source_ref, bf16[64,96,384]{2,1,0:T(8,128)(2,1)} %get-tuple-element.102.d_partial_ref.beside, bf16[64,96,384]{2,1,0:T(8,128)(2,1)} %image.1, bf16[7,96,384]{2,1,0:T(8,128)(2,1)} %copy-done.2, bf16[7,96,384]{2,1,0:T(8,128)(2,1)} %copy-done.1), custom_call_target="tpu_custom_call" | custom-call | flops 14000000 | bytes 14000 | tf_op jit(solution)/shard_map/rows_grad/pallas_call | solution.py:793
  164.4 0.8 pad_maximum_fusion.4
  165.2 1.7 collective-permute-start.18
  166.9 3.7 %collective-permute-start.20 = (bf16[24,1536]{1,0:T(8,128)(2,1)S(1)}, bf16[24,1536]{1,0:T(8,128)(2,1)S(1)}, u32[]{:S(2)}, u32[]{:S(2)}) collective-permute-start(bf16[24,1536]{1,0:T(8,128)(2,1)S(1)} %add_add_fusion), channel_id=1, source_target_pairs={{0,6},{1,7},{2,4},{3,5},{4,2},{5,3},{6,0},{7,1},{8,14},{9,15},{10,... | collective-permute-start | bytes 221192 | tf_op jit(solution)/shard_map/ppermute | solution.py:24
  170.6 0.7 collective-permute-start.15
  171.3 0.7 fusion
  172.0 1.6 collective-permute-start.21
  173.7 1.5 collective-permute-start.22
  175.2 1.2 collective-permute-start.23
  176.6 1.9 collective-permute-done.22
  178.6 1.7 collective-permute-done.23
  180.5 2.9 %collective-permute-start.25 = (f32[40,384]{1,0:T(8,128)S(1)}, f32[40,384]{1,0:T(8,128)S(1)}, u32[]{:S(2)}, u32[]{:S(2)}) collective-permute-start(f32[40,384]{1,0:T(8,128)S(1)} %add_add_fusion.2), channel_id=1, source_target_pairs={{0,4},{1,5},{2,6},{3,7},{4,0},{5,1},{6,2},{7,3},{8,12},{9,13},{10,... | collective-permute-start | bytes 184328 | tf_op jit(solution)/shard_map/ppermute | solution.py:24
  183.4 1.4 collective-permute-start.26
  184.8 9.0 %rows_back.2.rest_0_ = bf16[64,96,384]{2,1,0:T(8,128)(2,1)} custom-call(s32[72,128]{1,0:T(8,128)} %get-tuple-element.76.source_ref, f32[2,16,384]{2,1,0:T(8,128)} %get-tuple-element.116.taps_ref, bf16[64,96,384]{2,1,0:T(8,128)(2,1)} %get-tuple-element.102.d_partial_ref.beside, bf16[64,96,384]{2,1,0:T(8,128)(2,1)} %get-tuple-element.102.d_partial_ref.beside, ...), custom_call_target="tpu_custom_call" | custom-call | flops 8000000 | bytes 8000 | tf_op jit(solution)/shard_map/rows_back/pallas_call | solution.py:825
  193.8 0.7 add_add_fusion.1.g_ref
  194.5 1.2 collective-permute-start.29
  195.7 0.8 collective-permute-start.28
  196.5 1.5 collective-permute-start.27
  198.0 9.0 %rows_back.3 = bf16[64,96,384]{2,1,0:T(8,128)(2,1)} custom-call(s32[72,128]{1,0:T(8,128)} %get-tuple-element.76.source_ref, f32[2,16,384]{2,1,0:T(8,128)} %get-tuple-element.116.taps_ref, bf16[64,96,384]{2,1,0:T(8,128)(2,1)} %get-tuple-element.102.d_partial_ref.beside, ...), custom_call_target="tpu_custom_call", output_to_operand_aliasing={{}: (8, {})} | custom-call | flops 8000000 | bytes 8000 | tf_op jit(solution)/shard_map/rows_back/pallas_call | solution.py:825
  207.0 0.9 collective-permute-done.27
  208.2 2.5 %taps_grad.1 = (f32[2,32,384]{2,1,0:T(8,128)}, f32[2,32,384]{2,1,0:T(8,128)}, f32[2,32,384]{2,1,0:T(8,128)}, f32[2,32,384]{2,1,0:T(8,128)}, f32[2,384]{1,0:T(2,1...) custom-call(f32[2,32,384]{2,1,0:T(8,128)} %get-tuple-element.117.zr_, ...), custom_call_target="tpu_custom_call" | custom-call | flops 3000000 | bytes 3000 | tf_op jit(solution)/shard_map/taps_grad/pallas_call | solution.py:873
  210.7 0.3 collective-permute-done.30.other_ref
  211.0 2.9 %weight_grads.1 = (f32[384,1536]{1,0:T(8,128)}, f32[1536,384]{1,0:T(8,128)}) custom-call(s32[1]{0:T(128)} %bitcast.16.side_ref, bf16[384,1536]{1,0:T(8,128)(2,1)S(1)} %pad_maximum_fusion.own_ref, bf16[384,1536]{1,0:T(8,128)(2,1)S(1)} %collective-permute-done.30.other_ref), custom_call_target="tpu_custom_call" | custom-call | flops 3000000 | bytes 3000 | tf_op jit(solution)/shard_map/weight_grads/pallas_call | solution.py:859
  (65 shorter events, 1.6 us)
Async XLA Ops:
  2.0 12.6 %collective-permute-start.1 = (bf16[7,96,384]{2,1,0:T(8,128)(2,1)S(1)}, bf16[7,96,384]{2,1,0:T(8,128)(2,1)S(1)}, u32[]{:S(2)}, u32[]{:S(2)}) collective-permute-start(bf16[7,96,384]{2,1,0:T(8,128)(2,1)S(1)} %get-tuple-element.136), channel_id=1, source_target_pairs={{8,16},{16,8},{9,17},{17,9},{10,18},{18,10},{11,19},{19,11},{12,20... | collective-permute-start | bytes 1548296 | tf_op jit(solution)/shard_map/ppermute | solution.py:30
  2.7 11.9 %collective-permute-start = (bf16[7,96,384]{2,1,0:T(8,128)(2,1)S(1)}, bf16[7,96,384]{2,1,0:T(8,128)(2,1)S(1)}, u32[]{:S(2)}, u32[]{:S(2)}) collective-permute-start(bf16[7,96,384]{2,1,0:T(8,128)(2,1)S(1)} %get-tuple-element.135), channel_id=1, source_target_pairs={{0,8},{8,0},{16,24},{24,16},{1,9},{9,1},{17,25},{25,17},{2,10},{10... | collective-permute-start | bytes 1548296 | tf_op jit(solution)/shard_map/ppermute | solution.py:24
  9.0 25.7 %collective-permute-start.2 = (bf16[64,8,384]{2,1,0:T(8,128)(2,1)}, bf16[64,8,384]{2,1,0:T(8,128)(2,1)S(1)}, u32[]{:S(2)}, u32[]{:S(2)}) collective-permute-start(bf16[64,8,384]{2,1,0:T(8,128)(2,1)} %get-tuple-element.138), channel_id=1, source_target_pairs={{0,1},{1,0},{2,3},{3,2},{4,5},{5,4},{6,7},{7,6},{8,9},{9,8},{10,11... | collective-permute-start | bytes 1179656 | tf_op jit(solution)/shard_map/ppermute | solution.py:24
  10.5 24.2 %collective-permute-start.3 = (bf16[64,8,384]{2,1,0:T(8,128)(2,1)S(1)}, bf16[64,8,384]{2,1,0:T(8,128)(2,1)S(1)}, u32[]{:S(2)}, u32[]{:S(2)}) collective-permute-start(bf16[64,8,384]{2,1,0:T(8,128)(2,1)S(1)} %get-tuple-element.137), channel_id=1, source_target_pairs={{1,2},{3,4},{5,6},{2,1},{4,3},{6,5},{9,10},{11,12},{13,14},{10,9},... | collective-permute-start | bytes 1179656 | tf_op jit(solution)/shard_map/ppermute | solution.py:30
  14.6 6.8 %copy-start.1 = (bf16[7,96,384]{2,1,0:T(8,128)(2,1)}, bf16[7,96,384]{2,1,0:T(8,128)(2,1)S(1)}, u32[]{:S(2)}) copy-start(bf16[7,96,384]{2,1,0:T(8,128)(2,1)S(1)} %collective-permute-done.1.other) | copy-start | bytes 1548292
  14.6 6.7 %copy-start.2 = (bf16[7,96,384]{2,1,0:T(8,128)(2,1)}, bf16[7,96,384]{2,1,0:T(8,128)(2,1)S(1)}, u32[]{:S(2)}) copy-start(bf16[7,96,384]{2,1,0:T(8,128)(2,1)S(1)} %collective-permute-done.near) | copy-start | bytes 1548292
  14.7 20.0 %collective-permute-start.5 = (bf16[14,8,384]{2,1,0:T(8,128)(2,1)S(1)}, bf16[14,8,384]{2,1,0:T(8,128)(2,1)S(1)}, u32[]{:S(2)}, u32[]{:S(2)}) collective-permute-start(bf16[14,8,384]{2,1,0:T(8,128)(2,1)S(1)} %pad_maximum_fusion.3), channel_id=1, source_target_pairs={{1,2},{3,4},{5,6},{2,1},{4,3},{6,5},{9,10},{11,12},{13,14},{10,9},... | collective-permute-start | bytes 258056 | tf_op jit(solution)/shard_map/ppermute | solution.py:30
  15.4 19.3 %collective-permute-start.4 = (bf16[14,8,384]{2,1,0:T(8,128)(2,1)S(1)}, bf16[14,8,384]{2,1,0:T(8,128)(2,1)S(1)}, u32[]{:S(2)}, u32[]{:S(2)}) collective-permute-start(bf16[14,8,384]{2,1,0:T(8,128)(2,1)S(1)} %pad_maximum_fusion.2), channel_id=1, source_target_pairs={{0,1},{1,0},{2,3},{3,2},{4,5},{5,4},{6,7},{7,6},{8,9},{9,8},{10,11... | collective-permute-start | bytes 258056 | tf_op jit(solution)/shard_map/ppermute | solution.py:24
  34.6 0.7 copy-start.5
  34.7 0.9 copy-start.6
  34.7 0.9 copy-start.8
  34.7 0.9 copy-start.9
  112.7 10.4 %collective-permute-start.6 = (bf16[384,1536]{1,0:T(8,128)(2,1)}, bf16[384,1536]{1,0:T(8,128)(2,1)S(1)}, u32[]{:S(2)}, u32[]{:S(2)}) collective-permute-start(bf16[384,1536]{1,0:T(8,128)(2,1)} %get-tuple-element.85), channel_id=1, source_target_pairs={{0,8},{8,0},{16,24},{24,16},{1,9},{9,1},{17,25},{25,17},{2,10},{10... | collective-permute-start | bytes 3538952 | tf_op jit(solution)/shard_map/ppermute | solution.py:24
  112.7 18.4 %collective-permute-start.8 = (bf16[512,384]{1,0:T(8,128)(2,1)}, bf16[512,384]{1,0:T(8,128)(2,1)}, u32[]{:S(2)}, u32[]{:S(2)}) collective-permute-start(bf16[512,384]{1,0:T(8,128)(2,1)} %get-tuple-element.94), channel_id=1, source_target_pairs={{0,1},{1,0},{2,3},{3,2},{4,5},{5,4},{6,7},{7,6},{8,9},{9,8},{10,11... | collective-permute-start | bytes 1179656 | tf_op jit(solution)/shard_map/ppermute | solution.py:24
  112.9 18.2 %collective-permute-start.9 = (bf16[512,384]{1,0:T(8,128)(2,1)}, bf16[512,384]{1,0:T(8,128)(2,1)}, u32[]{:S(2)}, u32[]{:S(2)}) collective-permute-start(bf16[512,384]{1,0:T(8,128)(2,1)} %get-tuple-element.95), channel_id=1, source_target_pairs={{1,2},{3,4},{5,6},{2,1},{4,3},{6,5},{9,10},{11,12},{13,14},{10,9},... | collective-permute-start | bytes 1179656 | tf_op jit(solution)/shard_map/ppermute | solution.py:30
  114.3 8.8 %copy-start = (f32[384,1536]{1,0:T(8,128)S(1)}, f32[384,1536]{1,0:T(8,128)}, u32[]{:S(2)}) copy-start(f32[384,1536]{1,0:T(8,128)} %get-tuple-element.84.keep_ref) | copy-start | bytes 7077892
  124.1 18.2 %collective-permute-start.7 = (bf16[96,1536]{1,0:T(8,128)(2,1)}, bf16[96,1536]{1,0:T(8,128)(2,1)S(1)}, u32[]{:S(2)}, u32[]{:S(2)}) collective-permute-start(bf16[96,1536]{1,0:T(8,128)(2,1)} %get-tuple-element.90), channel_id=1, source_target_pairs={{0,16},{8,24},{16,0},{24,8},{1,17},{9,25},{17,1},{25,9},{2,18},{10... | collective-permute-start | bytes 884744 | tf_op jit(solution)/shard_map/ppermute | solution.py:24
  124.1 19.3 %collective-permute-start.10 = (bf16[96,1536]{1,0:T(8,128)(2,1)}, bf16[96,1536]{1,0:T(8,128)(2,1)S(1)}, u32[]{:S(2)}, u32[]{:S(2)}) collective-permute-start(bf16[96,1536]{1,0:T(8,128)(2,1)} %get-tuple-element.91), channel_id=1, source_target_pairs={{0,1},{1,0},{2,3},{3,2},{4,5},{5,4},{6,7},{7,6},{8,9},{9,8},{10,11... | collective-permute-start | bytes 884744 | tf_op jit(solution)/shard_map/ppermute | solution.py:24
  129.2 14.8 %collective-permute-start.11 = (bf16[96,1536]{1,0:T(8,128)(2,1)}, bf16[96,1536]{1,0:T(8,128)(2,1)S(1)}, u32[]{:S(2)}, u32[]{:S(2)}) collective-permute-start(bf16[96,1536]{1,0:T(8,128)(2,1)} %get-tuple-element.92), channel_id=1, source_target_pairs={{0,17},{1,16},{2,19},{3,18},{4,21},{5,20},{6,23},{7,22},{8,25},{9,... | collective-permute-start | bytes 884744 | tf_op jit(solution)/shard_map/ppermute | solution.py:553
  144.1 20.1 %collective-permute-start.12 = (f32[24,1536]{1,0:T(8,128)S(1)}, f32[24,1536]{1,0:T(8,128)S(1)}, u32[]{:S(2)}, u32[]{:S(2)}) collective-permute-start(f32[24,1536]{1,0:T(8,128)S(1)} %get-tuple-element.145), channel_id=1, source_target_pairs={{0,2},{1,3},{2,0},{3,1},{4,6},{5,7},{6,4},{7,5},{8,10},{9,11},{10,... | collective-permute-start | bytes 442376 | tf_op jit(solution)/shard_map/ppermute | solution.py:24
  147.4 16.9 %collective-permute-start.13 = (f32[24,1536]{1,0:T(8,128)S(1)}, f32[24,1536]{1,0:T(8,128)S(1)}, u32[]{:S(2)}, u32[]{:S(2)}) collective-permute-start(f32[24,1536]{1,0:T(8,128)S(1)} %get-tuple-element.143), channel_id=1, source_target_pairs={{0,4},{1,5},{2,6},{3,7},{4,0},{5,1},{6,2},{7,3},{8,12},{9,13},{10,... | collective-permute-start | bytes 442376 | tf_op jit(solution)/shard_map/ppermute | solution.py:24
  149.7 14.5 %collective-permute-start.14 = (f32[24,1536]{1,0:T(8,128)S(1)}, f32[24,1536]{1,0:T(8,128)S(1)}, u32[]{:S(2)}, u32[]{:S(2)}) collective-permute-start(f32[24,1536]{1,0:T(8,128)S(1)} %get-tuple-element.144), channel_id=1, source_target_pairs={{0,6},{1,7},{2,4},{3,5},{4,2},{5,3},{6,0},{7,1},{8,14},{9,15},{10,... | collective-permute-start | bytes 442376 | tf_op jit(solution)/shard_map/ppermute | solution.py:24
  149.8 14.5 %collective-permute-start.16 = (bf16[7,96,384]{2,1,0:T(8,128)(2,1)}, bf16[7,96,384]{2,1,0:T(8,128)(2,1)S(1)}, u32[]{:S(2)}, u32[]{:S(2)}) collective-permute-start(bf16[7,96,384]{2,1,0:T(8,128)(2,1)} %get-tuple-element.97), channel_id=1, source_target_pairs={{0,8},{8,0},{16,24},{24,16},{1,9},{9,1},{17,25},{25,17},{2,10},{10... | collective-permute-start | bytes 1548296 | tf_op jit(solution)/shard_map/ppermute | solution.py:24
  149.8 14.5 %collective-permute-start.17 = (bf16[7,96,384]{2,1,0:T(8,128)(2,1)}, bf16[7,96,384]{2,1,0:T(8,128)(2,1)S(1)}, u32[]{:S(2)}, u32[]{:S(2)}) collective-permute-start(bf16[7,96,384]{2,1,0:T(8,128)(2,1)} %get-tuple-element.98), channel_id=1, source_target_pairs={{8,16},{16,8},{9,17},{17,9},{10,18},{18,10},{11,19},{19,11},{12,20... | collective-permute-start | bytes 1548296 | tf_op jit(solution)/shard_map/ppermute | solution.py:30
  150.5 13.8 %copy-start.7 = (f32[16,384]{1,0:T(8,128)S(1)}, f32[16,384]{1,0:T(8,128)}, u32[]{:S(2)}) copy-start(f32[16,384]{1,0:T(8,128)} %cols_grad.1) | copy-start | bytes 73732
  150.6 13.8 %copy-start.10 = (f32[8,384]{1,0:T(8,128)S(1)}, f32[8,384]{1,0:T(8,128)}, u32[]{:S(2)}) copy-start(f32[8,384]{1,0:T(8,128)} %get-tuple-element.107) | copy-start | bytes 36868
  164.3 20.5 %copy-start.3 = (bf16[7,96,384]{2,1,0:T(8,128)(2,1)}, bf16[7,96,384]{2,1,0:T(8,128)(2,1)S(1)}, u32[]{:S(2)}) copy-start(bf16[7,96,384]{2,1,0:T(8,128)(2,1)S(1)} %collective-permute-done.16.near) | copy-start | bytes 1548292
  164.3 20.5 %copy-start.4 = (bf16[7,96,384]{2,1,0:T(8,128)(2,1)}, bf16[7,96,384]{2,1,0:T(8,128)(2,1)S(1)}, u32[]{:S(2)}) copy-start(bf16[7,96,384]{2,1,0:T(8,128)(2,1)S(1)} %collective-permute-done.17.other) | copy-start | bytes 1548292
  165.2 6.1 %collective-permute-start.18 = (f32[40,384]{1,0:T(8,128)S(1)}, f32[40,384]{1,0:T(8,128)S(1)}, u32[]{:S(2)}, u32[]{:S(2)}) collective-permute-start(f32[40,384]{1,0:T(8,128)S(1)} %pad_maximum_fusion.4), channel_id=1, source_target_pairs={{0,8},{8,0},{16,24},{24,16},{1,9},{9,1},{17,25},{25,17},{2,10},{10... | collective-permute-start | bytes 184328 | tf_op jit(solution)/shard_map/ppermute | solution.py:24
  166.9 8.3 %collective-permute-start.20 = (bf16[24,1536]{1,0:T(8,128)(2,1)S(1)}, bf16[24,1536]{1,0:T(8,128)(2,1)S(1)}, u32[]{:S(2)}, u32[]{:S(2)}) collective-permute-start(bf16[24,1536]{1,0:T(8,128)(2,1)S(1)} %add_add_fusion), channel_id=1, source_target_pairs={{0,6},{1,7},{2,4},{3,5},{4,2},{5,3},{6,0},{7,1},{8,14},{9,15},{10,... | collective-permute-start | bytes 221192 | tf_op jit(solution)/shard_map/ppermute | solution.py:24
  170.6 5.8 %collective-permute-start.19 = (bf16[24,1536]{1,0:T(8,128)(2,1)S(1)}, bf16[24,1536]{1,0:T(8,128)(2,1)S(1)}, u32[]{:S(2)}, u32[]{:S(2)}) collective-permute-start(bf16[24,1536]{1,0:T(8,128)(2,1)S(1)} %add_add_fusion), channel_id=1, source_target_pairs={{0,2},{1,3},{2,0},{3,1},{4,6},{5,7},{6,4},{7,5},{8,10},{9,11},{10,... | collective-permute-start | bytes 221192 | tf_op jit(solution)/shard_map/ppermute | solution.py:24
  170.6 6.0 %collective-permute-start.15 = (bf16[24,1536]{1,0:T(8,128)(2,1)S(1)}, bf16[24,1536]{1,0:T(8,128)(2,1)S(1)}, u32[]{:S(2)}, u32[]{:S(2)}) collective-permute-start(bf16[24,1536]{1,0:T(8,128)(2,1)S(1)} %add_add_fusion), channel_id=1, source_target_pairs={{0,4},{1,5},{2,6},{3,7},{4,0},{5,1},{6,2},{7,3},{8,12},{9,13},{10,... | collective-permute-start | bytes 221192 | tf_op jit(solution)/shard_map/ppermute | solution.py:24
  172.0 4.6 %collective-permute-start.21 = (f32[40,384]{1,0:T(8,128)S(1)}, f32[40,384]{1,0:T(8,128)S(1)}, u32[]{:S(2)}, u32[]{:S(2)}) collective-permute-start(f32[40,384]{1,0:T(8,128)S(1)} %fusion), channel_id=1, source_target_pairs={{0,16},{8,24},{16,0},{24,8},{1,17},{9,25},{17,1},{25,9},{2,18},{10... | collective-permute-start | bytes 184328 | tf_op jit(solution)/shard_map/ppermute | solution.py:24
  173.7 4.9 %collective-permute-start.22 = (f32[40,384]{1,0:T(8,128)S(1)}, f32[40,384]{1,0:T(8,128)S(1)}, u32[]{:S(2)}, u32[]{:S(2)}) collective-permute-start(f32[40,384]{1,0:T(8,128)S(1)} %fusion), channel_id=1, source_target_pairs={{0,1},{1,0},{2,3},{3,2},{4,5},{5,4},{6,7},{7,6},{8,9},{9,8},{10,11... | collective-permute-start | bytes 184328 | tf_op jit(solution)/shard_map/ppermute | solution.py:24
  175.2 5.1 %collective-permute-start.23 = (f32[40,384]{1,0:T(8,128)S(1)}, f32[40,384]{1,0:T(8,128)S(1)}, u32[]{:S(2)}, u32[]{:S(2)}) collective-permute-start(f32[40,384]{1,0:T(8,128)S(1)} %fusion), channel_id=1, source_target_pairs={{0,17},{1,16},{2,19},{3,18},{4,21},{5,20},{6,23},{7,22},{8,25},{9,... | collective-permute-start | bytes 184328 | tf_op jit(solution)/shard_map/ppermute | solution.py:553
  180.3 13.5 %collective-permute-start.24 = (f32[40,384]{1,0:T(8,128)S(1)}, f32[40,384]{1,0:T(8,128)S(1)}, u32[]{:S(2)}, u32[]{:S(2)}) collective-permute-start(f32[40,384]{1,0:T(8,128)S(1)} %add_add_fusion.2), channel_id=1, source_target_pairs={{0,2},{1,3},{2,0},{3,1},{4,6},{5,7},{6,4},{7,5},{8,10},{9,11},{10,... | collective-permute-start | bytes 184328 | tf_op jit(solution)/shard_map/ppermute | solution.py:24
  180.5 13.3 %collective-permute-start.25 = (f32[40,384]{1,0:T(8,128)S(1)}, f32[40,384]{1,0:T(8,128)S(1)}, u32[]{:S(2)}, u32[]{:S(2)}) collective-permute-start(f32[40,384]{1,0:T(8,128)S(1)} %add_add_fusion.2), channel_id=1, source_target_pairs={{0,4},{1,5},{2,6},{3,7},{4,0},{5,1},{6,2},{7,3},{8,12},{9,13},{10,... | collective-permute-start | bytes 184328 | tf_op jit(solution)/shard_map/ppermute | solution.py:24
  183.4 10.5 %collective-permute-start.26 = (f32[40,384]{1,0:T(8,128)S(1)}, f32[40,384]{1,0:T(8,128)S(1)}, u32[]{:S(2)}, u32[]{:S(2)}) collective-permute-start(f32[40,384]{1,0:T(8,128)S(1)} %add_add_fusion.2), channel_id=1, source_target_pairs={{0,6},{1,7},{2,4},{3,5},{4,2},{5,3},{6,0},{7,1},{8,14},{9,15},{10,... | collective-permute-start | bytes 184328 | tf_op jit(solution)/shard_map/ppermute | solution.py:24
  194.5 12.5 %collective-permute-start.29 = (bf16[96,1536]{1,0:T(8,128)(2,1)S(1)}, bf16[96,1536]{1,0:T(8,128)(2,1)S(1)}, u32[]{:S(2)}, u32[]{:S(2)}) collective-permute-start(bf16[96,1536]{1,0:T(8,128)(2,1)S(1)} %pad_maximum_fusion.1), channel_id=1, source_target_pairs={{0,17},{1,16},{2,19},{3,18},{4,21},{5,20},{6,23},{7,22},{8,25},{9,... | collective-permute-start | bytes 884744 | tf_op jit(solution)/shard_map/ppermute | solution.py:553
  195.7 11.3 %collective-permute-start.28 = (bf16[96,1536]{1,0:T(8,128)(2,1)S(1)}, bf16[96,1536]{1,0:T(8,128)(2,1)S(1)}, u32[]{:S(2)}, u32[]{:S(2)}) collective-permute-start(bf16[96,1536]{1,0:T(8,128)(2,1)S(1)} %pad_maximum_fusion.1), channel_id=1, source_target_pairs={{0,16},{8,24},{16,0},{24,8},{1,17},{9,25},{17,1},{25,9},{2,18},{10... | collective-permute-start | bytes 884744 | tf_op jit(solution)/shard_map/ppermute | solution.py:24
  196.5 11.4 %collective-permute-start.27 = (bf16[96,1536]{1,0:T(8,128)(2,1)S(1)}, bf16[96,1536]{1,0:T(8,128)(2,1)S(1)}, u32[]{:S(2)}, u32[]{:S(2)}) collective-permute-start(bf16[96,1536]{1,0:T(8,128)(2,1)S(1)} %pad_maximum_fusion.1), channel_id=1, source_target_pairs={{0,1},{1,0},{2,3},{3,2},{4,5},{5,4},{6,7},{7,6},{8,9},{9,8},{10,11... | collective-permute-start | bytes 884744 | tf_op jit(solution)/shard_map/ppermute | solution.py:24
  208.1 2.9 %collective-permute-start.30 = (bf16[384,1536]{1,0:T(8,128)(2,1)S(1)}, bf16[384,1536]{1,0:T(8,128)(2,1)S(1)}, u32[]{:S(2)}, u32[]{:S(2)}) collective-permute-start(bf16[384,1536]{1,0:T(8,128)(2,1)S(1)} %pad_maximum_fusion.own_ref), channel_id=1, source_target_pairs={{0,8},{8,0},{16,24},{24,16},{1,9},{9,1},{17,25},{25,17},{2,10},{10... | collective-permute-start | bytes 3538952 | tf_op jit(solution)/shard_map/ppermute | solution.py:24
